TPU v7x, 32 devices: a whole 2x2x4 slice. The times are simulated.
32 devices in a mesh: dp: 2 (over x), ctx: 4 (over y, core), tp: 4 (over z).
Axes of the slice: x: 2, y: 2, z: 4, core: 2. Of those that a mesh axis runs over, the one named last changes fastest.
Arguments:
- tokens: bfloat16 [4, 2048, 1280], P('dp', ('ctx', 'tp')), may hold values from -6 to 6
- prefix: int32 [4], P('dp'), may hold values from 204 to 1024
- w_query: bfloat16 [2, 1280, 1280], P(None, ('dp', 'ctx'), 'tp'), may hold values from -0.15625 to 0.15625
- key_weight: bfloat16 [2, 1280, 320], P(None, ('dp', 'ctx')), may hold values from -0.15625 to 0.15625
- value_weight: bfloat16 [2, 1280, 320], P(None, ('dp', 'ctx')), may hold values from -0.15625 to 0.15625
- w_out: bfloat16 [2, 1280, 1280], P(None, ('dp', 'ctx'), 'tp'), may hold values from -3 to 3
- w_gate: bfloat16 [2, 1280, 3584], P(None, ('dp', 'ctx'), 'tp'), may hold values from -0.15625 to 0.15625
- w_up: bfloat16 [2, 1280, 3584], P(None, ('dp', 'ctx'), 'tp'), may hold values from -0.15625 to 0.15625
- w_down: bfloat16 [2, 1280, 3584], P(None, ('dp', 'ctx'), 'tp'), may hold values from -0.09375 to 0.09375
- gain_attn: bfloat16 [2, 1280], P(None, ('dp', 'ctx')), may hold values from 0.099609375 to 1.8984375
- gain_ffn: bfloat16 [2, 1280], P(None, ('dp', 'ctx')), may hold values from 0.099609375 to 1.8984375
- cotangent: bfloat16 [4, 2048, 1280], P('dp', ('ctx', 'tp')), may hold values from -6 to 6
Outputs:
- output: bfloat16 [4, 2048, 1280], P('dp', ('ctx', 'tp'))
- grad_tokens: float32 [4, 2048, 1280], P('dp', ('ctx', 'tp'))
- grad_w_query: float32 [2, 1280, 1280], P(None, ('dp', 'ctx'), 'tp')
- grad_w_key: float32 [2, 1280, 320], P(None, ('dp', 'ctx'))
- grad_w_value: float32 [2, 1280, 320], P(None, ('dp', 'ctx'))
- grad_w_out: float32 [2, 1280, 1280], P(None, ('dp', 'ctx'), 'tp')
- grad_w_gate: float32 [2, 1280, 3584], P(None, ('dp', 'ctx'), 'tp')
- grad_w_up: float32 [2, 1280, 3584], P(None, ('dp', 'ctx'), 'tp')
- grad_w_down: float32 [2, 1280, 3584], P(None, ('dp', 'ctx'), 'tp')
- grad_gain_attn: float32 [2, 1280], P(None, ('dp', 'ctx'))
- grad_gain_ffn: float32 [2, 1280], P(None, ('dp', 'ctx'))
All inputs are finite; a program needn't handle non-finite values.
Results may differ from a plain program's by a relative error of at most 0.035.
Values may be sent and summed in bfloat16 or wider, within the bound.
A program may use at most 384 MiB of HBM per device.

v0:
```python
import math

import jax
import jax.numpy as jnp
from jax import lax
from jax.sharding import PartitionSpec as P

QUERY_HEADS = 20
KEY_VALUE_HEADS = 5
HEAD_SIZE = 64


epsilon = 1e-05
masked_score = -1e30


def rms_parts(values):
    factor = lax.rsqrt(jnp.mean(values * values, axis=-1, keepdims=True) + epsilon)
    return (values * factor, factor)


def rope_tables(positions):
    half_size = HEAD_SIZE // 2
    frequency = jnp.exp(-math.log(10000.0) * jnp.arange(half_size).astype(jnp.float32) / half_size)
    angles = positions.astype(jnp.float32)[:, None] * frequency[None, :]
    return (jnp.cos(angles)[:, None, :], jnp.sin(angles)[:, None, :])


def rotate(values, cosine, sine):
    half_size = values.shape[-1] // 2
    first_half = values[..., :half_size]
    second_half = values[..., half_size:]
    return jnp.concatenate(
        [first_half * cosine - second_half * sine, second_half * cosine + first_half * sine],
        axis=-1,
    )


def rotate_back(gradient, cosine, sine):
    half_size = gradient.shape[-1] // 2
    first_half = gradient[..., :half_size]
    second_half = gradient[..., half_size:]
    return jnp.concatenate(
        [first_half * cosine + second_half * sine, second_half * cosine - first_half * sine],
        axis=-1,
    )


def contract_rows(left_side, right_side):
    return lax.dot_general(
        left_side, right_side, (((0,), (0,)), ((), ())), preferred_element_type=jnp.float32
    )


def contract_cols(left_side, right_side):
    return lax.dot_general(
        left_side, right_side, (((1,), (1,)), ((), ())), preferred_element_type=jnp.float32
    )


def spread_rows(values):
    return lax.all_gather(values, "tp", axis=1, tiled=True)


def collect_rows(values):
    return lax.psum_scatter(
        values.astype(jnp.bfloat16), "tp", scatter_dimension=1, tiled=True
    ).astype(jnp.float32)


def spread_grads(values):
    return lax.all_gather(values, "tp", axis=1, tiled=True)


def collect_grads(values):
    return lax.psum_scatter(
        values.astype(jnp.bfloat16), "tp", scatter_dimension=1, tiled=True
    ).astype(jnp.float32)


def scatter_grads(members):
    return (
        lax.psum_scatter(
            members[0].astype(jnp.bfloat16), ("dp", "ctx"), scatter_dimension=0, tiled=True
        ).astype(jnp.float32),
        lax.psum_scatter(
            members[1].astype(jnp.bfloat16), ("dp", "ctx"), scatter_dimension=0, tiled=True
        ).astype(jnp.float32),
        lax.psum_scatter(
            members[2].astype(jnp.bfloat16), ("dp", "ctx"), scatter_dimension=0, tiled=True
        ).astype(jnp.float32),
        lax.psum_scatter(
            members[3].astype(jnp.bfloat16), ("dp", "ctx"), scatter_dimension=0, tiled=True
        ).astype(jnp.float32),
        lax.psum_scatter(
            members[4].astype(jnp.bfloat16), ("dp", "ctx"), scatter_dimension=0, tiled=True
        ).astype(jnp.float32),
        lax.psum_scatter(
            members[5].astype(jnp.bfloat16), ("dp", "ctx"), scatter_dimension=0, tiled=True
        ).astype(jnp.float32),
        lax.psum_scatter(
            members[6].astype(jnp.bfloat16), ("dp", "ctx"), scatter_dimension=0, tiled=True
        ).astype(jnp.float32),
        lax.psum_scatter(
            members[7].astype(jnp.bfloat16), ("dp", "ctx"), scatter_dimension=0, tiled=True
        ).astype(jnp.float32),
        lax.psum_scatter(
            members[8].astype(jnp.bfloat16), ("dp", "ctx"), scatter_dimension=0, tiled=True
        ).astype(jnp.float32),
    )


def keep_same(current):
    return current


def over_blocks(carry_state, key_rows, value_rows, step_block):
    key_count = key_rows.shape[1]
    block_width = 512

    def one_block(block_index, current):
        offset = block_index * block_width
        key_block = lax.dynamic_slice_in_dim(key_rows, offset, block_width, 1)
        value_block = lax.dynamic_slice_in_dim(value_rows, offset, block_width, 1)
        return step_block(current, key_block, value_block, offset)

    return lax.fori_loop(0, key_count // block_width, one_block, carry_state)


def reduce_layer(
    grad_wq, grad_wk, grad_wv, grad_wo, grad_wg, grad_wu, grad_wd, grad_attn_gain, grad_ffn_gain
):
    grad_wk, grad_wv, grad_attn_gain, grad_ffn_gain = (
        lax.psum(grad_wk.astype(jnp.bfloat16), "tp").astype(jnp.float32),
        lax.psum(grad_wv.astype(jnp.bfloat16), "tp").astype(jnp.float32),
        lax.psum(grad_attn_gain.astype(jnp.bfloat16), "tp").astype(jnp.float32),
        lax.psum(grad_ffn_gain.astype(jnp.bfloat16), "tp").astype(jnp.float32),
    )
    return scatter_grads(
        (
            grad_wq,
            grad_wk,
            grad_wv,
            grad_wo,
            grad_wg,
            grad_wu,
            grad_wd,
            grad_attn_gain,
            grad_ffn_gain,
        )
    )


def per_device(
    tokens,
    prefix,
    w_query,
    key_weight,
    value_weight,
    w_out,
    w_gate,
    w_up,
    w_down,
    gain_attn,
    gain_ffn,
    cotangent,
):
    layer_count = w_query.shape[0]
    seq_count = tokens.shape[0]
    hidden_width = tokens.shape[2]
    block_rows = tokens.shape[1] * lax.axis_size("tp")
    flat_rows = seq_count * block_rows
    heads_here = w_query.shape[2] // HEAD_SIZE
    group_width = QUERY_HEADS // KEY_VALUE_HEADS
    tp_rank = lax.axis_index("tp")
    low_head = tp_rank * heads_here // group_width
    pick_index = (tp_rank * heads_here + jnp.arange(heads_here)) // group_width - low_head
    head_pick = (pick_index[:, None] == jnp.arange(2)[None, :]).astype(jnp.float32)
    query_pos = lax.axis_index("ctx") * block_rows + jnp.arange(block_rows)
    cosine, sine = rope_tables(query_pos)
    score_scale = 1.0 / math.sqrt(HEAD_SIZE)
    last_query = query_pos[-1]
    longest = jnp.max(prefix)

    def needed(key_start):
        return (key_start <= last_query) | (key_start < longest)

    def block_scores(query_heads, key_heads, key_start):
        key_pos = key_start + jnp.arange(key_heads.shape[1])
        visible = (key_pos[None, None, :] <= query_pos[None, :, None]) | (
            key_pos[None, None, :] < prefix[:, None, None]
        )
        scores = (
            jnp.einsum(
                "shqd,skhd->shqk", query_heads, key_heads, preferred_element_type=jnp.float32
            )
            * score_scale
        )
        return (jnp.where(visible[:, None], scores, masked_score), visible[:, None])

    stream = tokens.astype(jnp.float32)
    saved = []
    for layer_index in range(layer_count):
        gathered = (
            lax.all_gather(w_query[layer_index], ("dp", "ctx"), axis=0, tiled=True),
            lax.all_gather(key_weight[layer_index], ("dp", "ctx"), axis=0, tiled=True),
            lax.all_gather(value_weight[layer_index], ("dp", "ctx"), axis=0, tiled=True),
            lax.all_gather(w_out[layer_index], ("dp", "ctx"), axis=0, tiled=True),
            lax.all_gather(w_gate[layer_index], ("dp", "ctx"), axis=0, tiled=True),
            lax.all_gather(w_up[layer_index], ("dp", "ctx"), axis=0, tiled=True),
            lax.all_gather(w_down[layer_index], ("dp", "ctx"), axis=0, tiled=True),
            lax.all_gather(gain_attn[layer_index], ("dp", "ctx"), axis=0, tiled=True),
            lax.all_gather(gain_ffn[layer_index], ("dp", "ctx"), axis=0, tiled=True),
        )
        wq_full, wk_full, wv_full, wo_full, wg_full, wu_full, wd_full, attn_gain, ffn_gain = (
            gathered
        )
        wk_here = lax.dynamic_slice_in_dim(wk_full, low_head * HEAD_SIZE, 2 * HEAD_SIZE, 1)
        wv_here = lax.dynamic_slice_in_dim(wv_full, low_head * HEAD_SIZE, 2 * HEAD_SIZE, 1)
        unit_one, factor_one = rms_parts(stream)
        normed = spread_rows(
            (unit_one * attn_gain.astype(jnp.float32)).astype(jnp.bfloat16)
        ).reshape(flat_rows, hidden_width)
        query_lin = jnp.dot(normed, wq_full, preferred_element_type=jnp.float32).reshape(
            seq_count, block_rows, heads_here, HEAD_SIZE
        )
        query_heads = jnp.transpose(
            rotate(query_lin, cosine, sine).astype(jnp.bfloat16), (0, 2, 1, 3)
        )
        key_lin = jnp.dot(normed, wk_here, preferred_element_type=jnp.float32).reshape(
            seq_count, block_rows, 2, HEAD_SIZE
        )
        key_rows = rotate(key_lin, cosine, sine).astype(jnp.bfloat16)
        value_rows = (
            jnp.dot(normed, wv_here, preferred_element_type=jnp.float32)
            .reshape(seq_count, block_rows, 2, HEAD_SIZE)
            .astype(jnp.bfloat16)
        )

        def attention_step_block(carry_state, key_block, value_block, key_start):

            def attention_compute(current):
                running_max, running_sum, running_out = current
                key_heads = jnp.take(key_block, pick_index, axis=2)
                value_heads = jnp.take(value_block, pick_index, axis=2)
                scores, visible = block_scores(query_heads, key_heads, key_start)
                new_max = jnp.maximum(running_max, jnp.max(scores, axis=-1))
                weights = jnp.where(visible, jnp.exp(scores - new_max[..., None]), 0.0)
                decay = jnp.exp(running_max - new_max)
                update = jnp.einsum(
                    "shqk,skhd->shqd",
                    weights.astype(jnp.bfloat16),
                    value_heads,
                    preferred_element_type=jnp.float32,
                )
                return (
                    new_max,
                    running_sum * decay + jnp.sum(weights, axis=-1),
                    running_out * decay[..., None] + update,
                )

            return lax.cond(needed(key_start), attention_compute, keep_same, carry_state)

        attention_start_state = (
            jnp.full((seq_count, heads_here, block_rows), masked_score, jnp.float32),
            jnp.zeros((seq_count, heads_here, block_rows), jnp.float32),
            jnp.zeros((seq_count, heads_here, block_rows, HEAD_SIZE), jnp.float32),
        )
        running_max, running_sum, running_out = over_blocks(
            attention_start_state,
            lax.all_gather(key_rows, "ctx", axis=1, tiled=True),
            lax.all_gather(value_rows, "ctx", axis=1, tiled=True),
            attention_step_block,
        )
        attended = running_out / running_sum[..., None]
        log_sums = running_max + jnp.log(running_sum)
        attended_rows = (
            jnp.transpose(attended, (0, 2, 1, 3))
            .reshape(flat_rows, heads_here * HEAD_SIZE)
            .astype(jnp.bfloat16)
        )
        attn_part = contract_cols(attended_rows, wo_full).reshape(
            seq_count, block_rows, hidden_width
        )
        middle = stream + collect_rows(attn_part)
        unit_two, factor_two = rms_parts(middle)
        normed_ffn = spread_rows(
            (unit_two * ffn_gain.astype(jnp.float32)).astype(jnp.bfloat16)
        ).reshape(flat_rows, hidden_width)
        gate_lin = jnp.dot(normed_ffn, wg_full, preferred_element_type=jnp.float32)
        up_lin = jnp.dot(normed_ffn, wu_full, preferred_element_type=jnp.float32)
        hidden = (gate_lin / (1.0 + jnp.exp(-gate_lin)) * up_lin).astype(jnp.bfloat16)
        ffn_part = contract_cols(hidden, wd_full).reshape(seq_count, block_rows, hidden_width)
        saved.append(
            (
                gathered,
                wk_here,
                wv_here,
                unit_one,
                factor_one,
                normed,
                query_heads,
                key_rows,
                value_rows,
                attended,
                log_sums,
                attended_rows,
                unit_two,
                factor_two,
                normed_ffn,
                gate_lin,
                up_lin,
                hidden,
            )
        )
        stream = middle + collect_rows(ffn_part)
    grad_stream = cotangent.astype(jnp.float32)
    layer_grads = [None] * layer_count
    for layer_index in reversed(range(layer_count)):
        (
            gathered,
            wk_here,
            wv_here,
            unit_one,
            factor_one,
            normed,
            query_heads,
            key_rows,
            value_rows,
            attended,
            log_sums,
            attended_rows,
            unit_two,
            factor_two,
            normed_ffn,
            gate_lin,
            up_lin,
            hidden,
        ) = saved[layer_index]
        wq_full, wk_full, wv_full, wo_full, wg_full, wu_full, wd_full, attn_gain, ffn_gain = (
            gathered
        )
        grad_rows = spread_grads(grad_stream.astype(jnp.bfloat16)).reshape(flat_rows, hidden_width)
        grad_hidden = jnp.dot(grad_rows, wd_full, preferred_element_type=jnp.float32)
        grad_wd = contract_rows(grad_rows, hidden)
        sigmoid_gate = 1.0 / (1.0 + jnp.exp(-gate_lin))
        grad_gate = (
            grad_hidden * up_lin * sigmoid_gate * (1.0 + gate_lin * (1.0 - sigmoid_gate))
        ).astype(jnp.bfloat16)
        grad_up = (grad_hidden * gate_lin * sigmoid_gate).astype(jnp.bfloat16)
        grad_normed_ffn = contract_cols(grad_gate, wg_full) + contract_cols(grad_up, wu_full)
        grad_wg = contract_rows(normed_ffn, grad_gate)
        grad_wu = contract_rows(normed_ffn, grad_up)
        grad_local = collect_grads(grad_normed_ffn.reshape(seq_count, block_rows, hidden_width))
        grad_ffn_gain = jnp.sum(grad_local * unit_two, axis=(0, 1))
        grad_unit = grad_local * ffn_gain.astype(jnp.float32)
        grad_stream = grad_stream + factor_two * (
            grad_unit - unit_two * jnp.mean(grad_unit * unit_two, axis=-1, keepdims=True)
        )
        grad_rows = spread_grads(grad_stream.astype(jnp.bfloat16)).reshape(flat_rows, hidden_width)
        grad_attended = jnp.dot(grad_rows, wo_full, preferred_element_type=jnp.float32)
        grad_wo = contract_rows(grad_rows, attended_rows)
        grad_out = jnp.transpose(
            grad_attended.astype(jnp.bfloat16).reshape(
                seq_count, block_rows, heads_here, HEAD_SIZE
            ),
            (0, 2, 1, 3),
        )
        row_delta = jnp.sum(grad_out.astype(jnp.float32) * attended, axis=-1)

        def step_block(carry_state, key_block, value_block, key_start):

            def step_compute(current):
                grad_query, grad_key_all, grad_value_all = current
                key_heads = jnp.take(key_block, pick_index, axis=2)
                value_heads = jnp.take(value_block, pick_index, axis=2)
                scores, visible = block_scores(query_heads, key_heads, key_start)
                probs = jnp.where(visible, jnp.exp(scores - log_sums[..., None]), 0.0)
                grad_probs = jnp.einsum(
                    "shqd,skhd->shqk", grad_out, value_heads, preferred_element_type=jnp.float32
                )
                grad_scores = (probs * (grad_probs - row_delta[..., None])).astype(jnp.bfloat16)
                grad_query = (
                    grad_query
                    + jnp.einsum(
                        "shqk,skhd->shqd",
                        grad_scores,
                        key_heads,
                        preferred_element_type=jnp.float32,
                    )
                    * score_scale
                )
                key_terms = (
                    jnp.einsum(
                        "shqk,shqd->skhd",
                        grad_scores,
                        query_heads,
                        preferred_element_type=jnp.float32,
                    )
                    * score_scale
                )
                value_terms = jnp.einsum(
                    "shqk,shqd->skhd",
                    probs.astype(jnp.bfloat16),
                    grad_out,
                    preferred_element_type=jnp.float32,
                )
                key_terms = jnp.einsum(
                    "skhd,hg->skgd", key_terms, head_pick, precision=lax.Precision.HIGHEST
                )
                value_terms = jnp.einsum(
                    "skhd,hg->skgd", value_terms, head_pick, precision=lax.Precision.HIGHEST
                )
                block_width = key_block.shape[1]
                old_keys = lax.dynamic_slice_in_dim(grad_key_all, key_start, block_width, 1)
                old_values = lax.dynamic_slice_in_dim(grad_value_all, key_start, block_width, 1)
                grad_key_all = lax.dynamic_update_slice_in_dim(
                    grad_key_all, old_keys + key_terms, key_start, 1
                )
                grad_value_all = lax.dynamic_update_slice_in_dim(
                    grad_value_all, old_values + value_terms, key_start, 1
                )
                return (grad_query, grad_key_all, grad_value_all)

            return lax.cond(needed(key_start), step_compute, keep_same, carry_state)

        full_length = block_rows * lax.axis_size("ctx")
        start_state = (
            jnp.zeros((seq_count, heads_here, block_rows, HEAD_SIZE), jnp.float32),
            jnp.zeros((seq_count, full_length, 2, HEAD_SIZE), jnp.float32),
            jnp.zeros((seq_count, full_length, 2, HEAD_SIZE), jnp.float32),
        )
        grad_query, grad_key_all, grad_value_all = over_blocks(
            start_state,
            lax.all_gather(key_rows, "ctx", axis=1, tiled=True),
            lax.all_gather(value_rows, "ctx", axis=1, tiled=True),
            step_block,
        )
        grad_key_rows, grad_value_rows = (
            lax.psum_scatter(
                grad_key_all.astype(jnp.bfloat16), "ctx", scatter_dimension=1, tiled=True
            ).astype(jnp.float32),
            lax.psum_scatter(
                grad_value_all.astype(jnp.bfloat16), "ctx", scatter_dimension=1, tiled=True
            ).astype(jnp.float32),
        )
        grad_query_rows = (
            rotate_back(jnp.transpose(grad_query, (0, 2, 1, 3)), cosine, sine)
            .astype(jnp.bfloat16)
            .reshape(flat_rows, heads_here * HEAD_SIZE)
        )
        grad_key_flat = (
            rotate_back(grad_key_rows, cosine, sine)
            .astype(jnp.bfloat16)
            .reshape(flat_rows, 2 * HEAD_SIZE)
        )
        grad_value_flat = grad_value_rows.astype(jnp.bfloat16).reshape(flat_rows, 2 * HEAD_SIZE)
        grad_normed = (
            contract_cols(grad_query_rows, wq_full)
            + contract_cols(grad_key_flat, wk_here)
            + contract_cols(grad_value_flat, wv_here)
        )
        grad_wq = contract_rows(normed, grad_query_rows)
        unused_heads = jnp.zeros((hidden_width, KEY_VALUE_HEADS * HEAD_SIZE), jnp.float32)
        grad_wk = lax.dynamic_update_slice_in_dim(
            unused_heads, contract_rows(normed, grad_key_flat), low_head * HEAD_SIZE, 1
        )
        grad_wv = lax.dynamic_update_slice_in_dim(
            unused_heads, contract_rows(normed, grad_value_flat), low_head * HEAD_SIZE, 1
        )
        grad_local = collect_grads(grad_normed.reshape(seq_count, block_rows, hidden_width))
        grad_attn_gain = jnp.sum(grad_local * unit_one, axis=(0, 1))
        grad_unit = grad_local * attn_gain.astype(jnp.float32)
        grad_stream = grad_stream + factor_one * (
            grad_unit - unit_one * jnp.mean(grad_unit * unit_one, axis=-1, keepdims=True)
        )
        layer_grads[layer_index] = reduce_layer(
            grad_wq,
            grad_wk,
            grad_wv,
            grad_wo,
            grad_wg,
            grad_wu,
            grad_wd,
            grad_attn_gain,
            grad_ffn_gain,
        )
    stacked = [
        jnp.stack(
            [layer_grads[layer_index][member_index] for layer_index in range(layer_count)], axis=0
        )
        for member_index in range(9)
    ]
    return (
        stream.astype(jnp.bfloat16),
        grad_stream,
        stacked[0],
        stacked[1],
        stacked[2],
        stacked[3],
        stacked[4],
        stacked[5],
        stacked[6],
        stacked[7],
        stacked[8],
    )


def solution(mesh):
    in_specs = (
        P("dp", ("ctx", "tp"), None),
        P("dp"),
        P(None, ("dp", "ctx"), "tp"),
        P(None, ("dp", "ctx"), None),
        P(None, ("dp", "ctx"), None),
        P(None, ("dp", "ctx"), "tp"),
        P(None, ("dp", "ctx"), "tp"),
        P(None, ("dp", "ctx"), "tp"),
        P(None, ("dp", "ctx"), "tp"),
        P(None, ("dp", "ctx")),
        P(None, ("dp", "ctx")),
        P("dp", ("ctx", "tp"), None),
    )
    out_specs = (
        P("dp", ("ctx", "tp"), None),
        P("dp", ("ctx", "tp"), None),
        P(None, ("dp", "ctx"), "tp"),
        P(None, ("dp", "ctx"), None),
        P(None, ("dp", "ctx"), None),
        P(None, ("dp", "ctx"), "tp"),
        P(None, ("dp", "ctx"), "tp"),
        P(None, ("dp", "ctx"), "tp"),
        P(None, ("dp", "ctx"), "tp"),
        P(None, ("dp", "ctx")),
        P(None, ("dp", "ctx")),
    )
    return jax.shard_map(
        per_device, mesh=mesh, in_specs=in_specs, out_specs=out_specs, check_vma=False
    )
```

profile of v0, /device:TPU:0, one launch (start us, length us, event | category | flops | bytes accessed | tf_op | source)
XLA Modules:
  0.0 2727.3 jit_solution(1345411886569768870)
XLA Ops:
  183.6 74.4 %reduce-scatter.31.cloned.1.call-done = bf16[2,128,1280]{2,1,0:T(8,128)(2,1)} async-done(((bf16[2,512,1280]{2,1,0:T(8,128)(2,1)}), bf16[2,128,1280]{2,1,0:T(8,128)(2,1)}) %reduce-scatter.31.cloned.1.call-update) | async-done | bytes 655376 | tf_op jit(solution)/shard_map/reduce_scatter | solution.py:66
  263.9 52.3 %all-gather.43.cloned.1.call-done = bf16[2,512,1280]{2,1,0:T(8,128)(2,1)} async-done(((bf16[2,128,1280]{2,1,0:T(8,128)(2,1)}), bf16[2,512,1280]{2,1,0:T(8,128)(2,1)}) %all-gather.43.cloned.1.call-update) | async-done | bytes 2621456 | tf_op jit(solution)/shard_map/all_gather | solution.py:62
  382.9 52.2 %reduce-scatter.33.cloned.1.call-done = bf16[2,128,1280]{2,1,0:T(8,128)(2,1)} async-done(((bf16[2,512,1280]{2,1,0:T(8,128)(2,1)}), bf16[2,128,1280]{2,1,0:T(8,128)(2,1)}) %reduce-scatter.33.cloned.1.call-update) | async-done | bytes 655376 | tf_op jit(solution)/shard_map/reduce_scatter | solution.py:66
  572.7 75.4 %reduce-scatter.35.cloned.1.call-done = bf16[2,128,1280]{2,1,0:T(8,128)(2,1)} async-done(((bf16[2,512,1280]{2,1,0:T(8,128)(2,1)}), bf16[2,128,1280]{2,1,0:T(8,128)(2,1)}) %reduce-scatter.35.cloned.1.call-update) | async-done | bytes 655376 | tf_op jit(solution)/shard_map/reduce_scatter | solution.py:66
  678.7 56.7 %all-gather.51.cloned.1.call-done = bf16[2,512,1280]{2,1,0:T(8,128)(2,1)} async-done(((bf16[2,128,1280]{2,1,0:T(8,128)(2,1)}), bf16[2,512,1280]{2,1,0:T(8,128)(2,1)}) %all-gather.51.cloned.1.call-update) | async-done | bytes 2621456 | tf_op jit(solution)/shard_map/all_gather | solution.py:62
  772.3 49.1 %all-gather.53.cloned.1.call-done = bf16[2,512,1280]{2,1,0:T(8,128)(2,1)} async-done(((bf16[2,128,1280]{2,1,0:T(8,128)(2,1)}), bf16[2,512,1280]{2,1,0:T(8,128)(2,1)}) %all-gather.53.cloned.1.call-update) | async-done | bytes 2621456 | tf_op jit(solution)/shard_map/all_gather | solution.py:72
  868.3 52.2 %reduce-scatter.39.cloned.1.call-done = bf16[2,128,1280]{2,1,0:T(8,128)(2,1)} async-done(((bf16[2,512,1280]{2,1,0:T(8,128)(2,1)}), bf16[2,128,1280]{2,1,0:T(8,128)(2,1)}) %reduce-scatter.39.cloned.1.call-update) | async-done | bytes 655376 | tf_op jit(solution)/shard_map/reduce_scatter | solution.py:76
  925.4 54.5 %all-gather.55.cloned.1.call-done = bf16[2,512,1280]{2,1,0:T(8,128)(2,1)} async-done(((bf16[2,128,1280]{2,1,0:T(8,128)(2,1)}), bf16[2,512,1280]{2,1,0:T(8,128)(2,1)}) %all-gather.55.cloned.1.call-update) | async-done | bytes 2621456 | tf_op jit(solution)/shard_map/all_gather | solution.py:72
  992.0 58.2 %while.74 = (s32[]{:T(128)}, f32[2,5,512,64]{2,3,1,0:T(8,128)}, f32[2,2048,2,64]{1,2,3,0:T(2,128)}, f32[2,2048,2,64]{1,2,3,0:T(2,128)}, s32[]{:T(128)}, /*index=...) while((s32[]{:T(128)}, f32[2,5,512,64]{2,3,1,0:T(8,128)}, ...), condition=%wide.region_27.29_spmd.clone, body=%wide.region_24.28_spmd.clone.sunk | while | flops 1727597696 | bytes 72827896 | solution.py:127
  1055.0 102.8 %copy.165 = bf16[2,2048,2,64]{2,3,0,1:T(8,128)(2,1)} copy(bf16[2,2048,2,64]{1,2,3,0:T(2,128)(2,1)S(1)} %convert_element_type.479) | data formatting | bytes 2097152
  1157.8 97.2 %reshape.727 = bf16[2048,256]{1,0:T(8,128)(2,1)} reshape(bf16[2048,2,64,2]{3,2,1,0:T(8,128)(2,1)} %bitcast.110) | data formatting | bytes 2097152
  1268.6 61.8 %reduce-scatter.79.cloned.1.call-done = bf16[512,256]{1,0:T(8,128)(2,1)} async-done(((bf16[2048,256]{1,0:T(8,128)(2,1)}), bf16[512,256]{1,0:T(8,128)(2,1)}) %reduce-scatter.79.cloned.1.call-update) | async-done | bytes 262160
  1394.6 52.2 %reduce-scatter.43.cloned.1.call-done = bf16[2,128,1280]{2,1,0:T(8,128)(2,1)} async-done(((bf16[2,512,1280]{2,1,0:T(8,128)(2,1)}), bf16[2,128,1280]{2,1,0:T(8,128)(2,1)}) %reduce-scatter.43.cloned.1.call-update) | async-done | bytes 655376 | tf_op jit(solution)/shard_map/reduce_scatter | solution.py:76
  1450.8 54.6 %all-gather.57.cloned.1.call-done = bf16[2,512,1280]{2,1,0:T(8,128)(2,1)} async-done(((bf16[2,128,1280]{2,1,0:T(8,128)(2,1)}), bf16[2,512,1280]{2,1,0:T(8,128)(2,1)}) %all-gather.57.cloned.1.call-update) | async-done | bytes 2621456 | tf_op jit(solution)/shard_map/all_gather | solution.py:72
  1574.4 51.7 %reduce-scatter.37.cloned.1.call-done = bf16[2,128,1280]{2,1,0:T(8,128)(2,1)} async-done(((bf16[2,512,1280]{2,1,0:T(8,128)(2,1)}), bf16[2,128,1280]{2,1,0:T(8,128)(2,1)}) %reduce-scatter.37.cloned.1.call-update) | async-done | bytes 655376 | tf_op jit(solution)/shard_map/reduce_scatter | solution.py:66
  1630.9 54.3 %all-gather.59.cloned.1.call-done = bf16[2,512,1280]{2,1,0:T(8,128)(2,1)} async-done(((bf16[2,128,1280]{2,1,0:T(8,128)(2,1)}), bf16[2,512,1280]{2,1,0:T(8,128)(2,1)}) %all-gather.59.cloned.1.call-update) | async-done | bytes 2621456 | tf_op jit(solution)/shard_map/all_gather | solution.py:72
  1697.3 58.2 %while.75 = (s32[]{:T(128)}, f32[2,5,512,64]{2,3,1,0:T(8,128)}, f32[2,2048,2,64]{1,2,3,0:T(2,128)}, f32[2,2048,2,64]{1,2,3,0:T(2,128)}, s32[]{:T(128)}, /*index=...) while((s32[]{:T(128)}, f32[2,5,512,64]{2,3,1,0:T(8,128)}, ...), condition=%wide.region_38.40_spmd.clone, body=%wide.region_35.39_spmd.clone.sunk | while | flops 1727597696 | bytes 72827896 | solution.py:127
  1760.4 102.8 %copy.167 = bf16[2,2048,2,64]{2,3,0,1:T(8,128)(2,1)} copy(bf16[2,2048,2,64]{1,2,3,0:T(2,128)(2,1)S(1)} %convert_element_type.498) | data formatting | bytes 2097152
  1863.2 97.3 %reshape.729 = bf16[2048,256]{1,0:T(8,128)(2,1)} reshape(bf16[2048,2,64,2]{3,2,1,0:T(8,128)(2,1)} %bitcast.113) | data formatting | bytes 2097152
  1981.6 54.4 %reduce-scatter.81.cloned.1.call-done = bf16[512,256]{1,0:T(8,128)(2,1)} async-done(((bf16[2048,256]{1,0:T(8,128)(2,1)}), bf16[512,256]{1,0:T(8,128)(2,1)}) %reduce-scatter.81.cloned.1.call-update) | async-done | bytes 262160
  2239.8 45.9 %reduce-scatter.67.cloned.1.call-done = bf16[160,896]{1,0:T(8,128)(2,1)} async-done(((bf16[1280,896]{1,0:T(8,128)(2,1)}), bf16[160,896]{1,0:T(8,128)(2,1)}) %reduce-scatter.67.cloned.1.call-update) | async-done | bytes 286736 | tf_op jit(solution)/shard_map/reduce_scatter | solution.py:101
  2331.1 45.9 %reduce-scatter.63.cloned.1.call-done = bf16[160,896]{1,0:T(8,128)(2,1)} async-done(((bf16[1280,896]{1,0:T(8,128)(2,1)}), bf16[160,896]{1,0:T(8,128)(2,1)}) %reduce-scatter.63.cloned.1.call-update) | async-done | bytes 286736 | tf_op jit(solution)/shard_map/reduce_scatter | solution.py:98
  2422.4 45.8 %reduce-scatter.59.cloned.1.call-done = bf16[160,896]{1,0:T(8,128)(2,1)} async-done(((bf16[1280,896]{1,0:T(8,128)(2,1)}), bf16[160,896]{1,0:T(8,128)(2,1)}) %reduce-scatter.59.cloned.1.call-update) | async-done | bytes 286736 | tf_op jit(solution)/shard_map/reduce_scatter | solution.py:95
  2630.7 49.1 %reduce-scatter.49.cloned.1.call-done = bf16[2,128,1280]{2,1,0:T(8,128)(2,1)} async-done(((bf16[2,512,1280]{2,1,0:T(8,128)(2,1)}), bf16[2,128,1280]{2,1,0:T(8,128)(2,1)}) %reduce-scatter.49.cloned.1.call-update) | async-done | bytes 655376 | tf_op jit(solution)/shard_map/reduce_scatter | solution.py:76
  (749 shorter events, 1517.7 us)
Async XLA Ops:
  263.6 171.5 %reduce-scatter.33.cloned.1.call-start = ((), (), s32[]{:S(2)}) async-start(), calls=%async_computation.31 | async-start | bytes 3276800 | tf_op jit(solution)/shard_map/reduce_scatter | solution.py:66
  651.3 170.0 %all-gather.53.cloned.1.call-start = ((), (), s32[]{:S(2)}) async-start(), calls=%async_computation.38 | async-start | bytes 3276800 | tf_op jit(solution)/shard_map/all_gather | solution.py:72
  652.0 199.0 %all-gather.71.cloned.1.call-start = ((), (), s32[]{:S(2)}) async-start(), calls=%async_computation.63 | async-start | bytes 2580480 | tf_op jit(solution)/shard_map/all_gather | solution.py:211
  652.6 268.0 %reduce-scatter.39.cloned.1.call-start = ((), (), s32[]{:S(2)}) async-start(), calls=%async_computation.39 | async-start | bytes 3276800 | tf_op jit(solution)/shard_map/reduce_scatter | solution.py:76
  925.3 336.9 %reduce-scatter.41.cloned.1.call-start = ((), (), s32[]{:S(2)}) async-start(), calls=%async_computation.41 | async-start | bytes 1310720 | tf_op jit(solution)/shard_map/reduce_scatter | solution.py:440
  1054.0 276.4 %reduce-scatter.79.cloned.1.call-start = ((), (), s32[]{:S(2)}) async-start(), calls=%async_computation.68 | async-start | bytes 1310720
  1255.0 191.8 %reduce-scatter.43.cloned.1.call-start = ((), (), s32[]{:S(2)}) async-start(), calls=%async_computation.42 | async-start | bytes 3276800 | tf_op jit(solution)/shard_map/reduce_scatter | solution.py:76
  1630.8 342.6 %reduce-scatter.47.cloned.1.call-start = ((), (), s32[]{:S(2)}) async-start(), calls=%async_computation.46 | async-start | bytes 1310720 | tf_op jit(solution)/shard_map/reduce_scatter | solution.py:440
  1759.4 276.6 %reduce-scatter.81.cloned.1.call-start = ((), (), s32[]{:S(2)}) async-start(), calls=%async_computation.69 | async-start | bytes 1310720
  1960.5 209.7 %reduce-scatter.73.cloned.1.call-start = ((), (), s32[]{:S(2)}) async-start(), calls=%async_computation.65 | async-start | bytes 1105920 | tf_op jit(solution)/shard_map/reduce_scatter | solution.py:86
  1967.0 203.3 %reduce-scatter.77.cloned.1.call-start = ((), (), s32[]{:S(2)}) async-start(), calls=%async_computation.67 | async-start | bytes 1105920 | tf_op jit(solution)/shard_map/reduce_scatter | solution.py:89
  1973.4 196.9 %reduce-scatter.71.cloned.1.call-start = ((), (), s32[]{:S(2)}) async-start(), calls=%async_computation.64 | async-start | bytes 1105920 | tf_op jit(solution)/shard_map/reduce_scatter | solution.py:86
  1981.5 212.6 %reduce-scatter.75.cloned.1.call-start = ((), (), s32[]{:S(2)}) async-start(), calls=%async_computation.66 | async-start | bytes 1105920 | tf_op jit(solution)/shard_map/reduce_scatter | solution.py:89
  2106.5 179.2 %reduce-scatter.67.cloned.1.call-start = ((), (), s32[]{:S(2)}) async-start(), calls=%async_computation.56 | async-start | bytes 2580480 | tf_op jit(solution)/shard_map/reduce_scatter | solution.py:101
  2113.1 218.0 %reduce-scatter.65.cloned.1.call-start = ((), (), s32[]{:S(2)}) async-start(), calls=%async_computation.55 | async-start | bytes 2580480 | tf_op jit(solution)/shard_map/reduce_scatter | solution.py:98
  2119.9 257.1 %reduce-scatter.63.cloned.1.call-start = ((), (), s32[]{:S(2)}) async-start(), calls=%async_computation.54 | async-start | bytes 2580480 | tf_op jit(solution)/shard_map/reduce_scatter | solution.py:98
  2127.0 295.5 %reduce-scatter.61.cloned.1.call-start = ((), (), s32[]{:S(2)}) async-start(), calls=%async_computation.53 | async-start | bytes 2580480 | tf_op jit(solution)/shard_map/reduce_scatter | solution.py:95
  2133.8 334.5 %reduce-scatter.59.cloned.1.call-start = ((), (), s32[]{:S(2)}) async-start(), calls=%async_computation.52 | async-start | bytes 2580480 | tf_op jit(solution)/shard_map/reduce_scatter | solution.py:95
  2140.5 366.7 %reduce-scatter.57.cloned.1.call-start = ((), (), s32[]{:S(2)}) async-start(), calls=%async_computation.51 | async-start | bytes 1105920 | tf_op jit(solution)/shard_map/reduce_scatter | solution.py:92
  2146.2 400.3 %reduce-scatter.55.cloned.1.call-start = ((), (), s32[]{:S(2)}) async-start(), calls=%async_computation.50 | async-start | bytes 1105920 | tf_op jit(solution)/shard_map/reduce_scatter | solution.py:92
  2151.4 434.5 %reduce-scatter.53.cloned.1.call-start = ((), (), s32[]{:S(2)}) async-start(), calls=%async_computation.49 | async-start | bytes 1105920 | tf_op jit(solution)/shard_map/reduce_scatter | solution.py:83
  2155.8 469.5 %reduce-scatter.51.cloned.1.call-start = ((), (), s32[]{:S(2)}) async-start(), calls=%async_computation.48 | async-start | bytes 1105920 | tf_op jit(solution)/shard_map/reduce_scatter | solution.py:83
  2160.7 466.4 %all-reduce.14.cloned.1.call-start = ((), (), s32[]{:S(2)}) async-start(), calls=%async_computation.70 | async-start | bytes 983040 | tf_op jit(solution)/shard_map/psum | solution.py:134
  2194.2 485.5 %reduce-scatter.49.cloned.1.call-start = ((), (), s32[]{:S(2)}) async-start(), calls=%async_computation.47 | async-start | bytes 3276800 | tf_op jit(solution)/shard_map/reduce_scatter | solution.py:76
  (117 other events, 7741.6 us)
Sparse Core Ops, SparseCore 0:
  42.4 54.7 all-gather.36
  181.8 76.2 reduce-scatter.30
  383.0 52.0 reduce-scatter.32
  868.4 52.0 reduce-scatter.38
  925.4 54.4 all-gather.54
  1054.1 75.2 reduce-scatter.40
  1255.1 75.2 reduce-scatter.78
  1394.7 52.0 reduce-scatter.42
  1450.9 54.4 all-gather.56
  1521.2 50.9 reduce-scatter.44
  1574.3 51.7 reduce-scatter.36
  1759.5 75.2 reduce-scatter.46
  1960.6 75.2 reduce-scatter.80
  2039.6 35.7 reduce-scatter.72
  2079.0 35.7 reduce-scatter.76
  2158.4 35.7 reduce-scatter.74
  2197.5 42.2 reduce-scatter.68
  2243.5 42.1 reduce-scatter.66
  2288.9 42.1 reduce-scatter.64
  2334.8 42.1 reduce-scatter.62
  2380.2 42.1 reduce-scatter.60
  2426.0 42.1 reduce-scatter.58
  2589.5 35.7 reduce-scatter.50
  2627.6 52.0 reduce-scatter.48
  (8 shorter events, 215.7 us)
Sparse Core Ops, SparseCore 1:
  184.6 52.6 all-gather.60
  261.8 54.3 all-gather.42
  318.5 27.3 all-gather.62
  348.4 28.5 all-gather.64
  438.8 54.3 all-gather.44
  572.2 76.0 reduce-scatter.34
  650.5 28.1 all-gather.68
  680.7 54.6 all-gather.50
  737.7 27.3 all-gather.66
  766.7 54.6 all-gather.52
  823.6 27.3 all-gather.70
  1630.9 54.3 all-gather.58
  2194.3 38.5 all-reduce.13
where the time goes:
time: 2740 us; the launch traced here: 2730 us
  waiting for transfers between devices  1520 us (55%)
  local copies, waits for them, and re-layouts  608 us (22%)
  matrix products  309 us (11%)
  blocking collectives  162 us (6%)
  other arithmetic  83.9 us (3%)
    unnamed x211, local copies, waits for them, and re-layouts  486 us
    reduce_scatter x4, waiting for transfers between devices, collect_rows(): lax.psum_scatter(values.astype(jnp.bfloat16), 'tp', scatter_dimension=1,...  254 us
    all_gather x4, waiting for transfers between devices, spread_grads(): return lax.all_gather(values, 'tp', axis=1, tiled=True)  212 us
    reduce_scatter x4, waiting for transfers between devices, collect_grads(): lax.psum_scatter(values.astype(jnp.bfloat16), 'tp', scatter_dimension=1,...  198 us
    all_gather x4, waiting for transfers between devices, spread_rows(): return lax.all_gather(values, 'tp', axis=1, tiled=True)  172 us
    unnamed x47, waiting for transfers between devices  119 us
    reduce_scatter x2, waiting for transfers between devices, scatter_grads(): lax.psum_scatter(members[5].astype(jnp.bfloat16), ('dp', 'ctx'), scatter_...  89.2 us
    reduce_scatter x2, waiting for transfers between devices, scatter_grads(): lax.psum_scatter(members[4].astype(jnp.bfloat16), ('dp', 'ctx'), scatter_...  89.1 us
  transfers between devices with their start and end apart: 45, of which 35 were waited for; matrix products, arithmetic and copies ran while one was open for 24% of the time, Pallas kernels for 0%

commit v1 on v0

v1 whole, which is shorter than its diff:
```python
import functools
import math

import jax
import jax.numpy as jnp
from jax import lax
from jax.experimental import pallas as pl
from jax.experimental.pallas import tpu as pltpu
from jax.sharding import PartitionSpec as P

QUERY_HEADS = 20
KEY_VALUE_HEADS = 5
D = 64
GROUP = QUERY_HEADS // KEY_VALUE_HEADS
EPS = 1e-05
MASKED = -1e30
BF = jnp.bfloat16
F32 = jnp.float32
SLOTS = 4
LANES = 128


def nt(a, b):
    return lax.dot_general(a, b, (((1,), (1,)), ((), ())), preferred_element_type=F32)


def nn(a, b):
    return lax.dot_general(a, b, (((1,), (0,)), ((), ())), preferred_element_type=F32)


def tn(a, b):
    return lax.dot_general(a, b, (((0,), (0,)), ((), ())), preferred_element_type=F32)


def half_turn(x):
    lane = lax.broadcasted_iota(jnp.int32, x.shape, 1)
    return jnp.where((lane & 32) == 0, pltpu.roll(x, LANES - 32, 1), pltpu.roll(x, 32, 1))


def call(kernel, ins, outs, smem=0, scratch=(), flops=0, exps=0, vmem=56):
    total = sum(math.prod(a.shape) * a.dtype.itemsize for a in ins) + sum(
        math.prod(s) * jnp.dtype(d).itemsize for s, d in outs
    )
    return pl.pallas_call(
        kernel,
        out_shape=[jax.ShapeDtypeStruct(s, d) for s, d in outs],
        in_specs=[pl.BlockSpec(memory_space=pltpu.SMEM)] * smem
        + [pl.BlockSpec(memory_space=pltpu.VMEM)] * (len(ins) - smem),
        out_specs=[pl.BlockSpec(memory_space=pltpu.VMEM)] * len(outs),
        scratch_shapes=list(scratch),
        compiler_params=pltpu.CompilerParams(vmem_limit_bytes=vmem * 2**20),
        cost_estimate=pl.CostEstimate(
            flops=int(flops), bytes_accessed=int(total), transcendentals=int(exps)
        ),
    )(*ins)


def flip(x, axis, m):
    return lax.ppermute(x, axis, [(i, i ^ m) for i in range(4)])


def ctx_gather(x):
    far = flip(x, "ctx", 2)
    return [x, flip(x, "ctx", 1), far, flip(far, "ctx", 1)]


def ctx_reduce(parts):
    far = (parts[2].astype(F32) + flip(parts[3], "ctx", 1).astype(F32)).astype(BF)
    near = flip(parts[1], "ctx", 1)
    return parts[0].astype(F32) + near.astype(F32) + flip(far, "ctx", 2).astype(F32)


def inner(t):
    return (t == 1) | (t == 2)


def tp_gather(x):
    t = lax.axis_index("tp")
    two = flip(x, "tp", 2)
    mid = lax.ppermute(x, "tp", [(1, 2), (2, 1)])
    end = lax.ppermute(two, "tp", [(1, 0), (2, 3)])
    return [x, flip(x, "tp", 1), two, jnp.where(inner(t), mid, end)]


def tp_reduce(parts):
    one = flip(parts[1], "tp", 1)
    handed = lax.ppermute(parts[3], "tp", [(0, 1), (3, 2)])
    mid = lax.ppermute(parts[3], "tp", [(1, 2), (2, 1)])
    two = flip((parts[2].astype(F32) + handed.astype(F32)).astype(BF), "tp", 2)
    return (
        parts[0].astype(F32) + one.astype(F32) + two.astype(F32) + mid.astype(F32)
    )


def ctx_exchange(stacked, own_first):
    c = lax.axis_index("ctx")
    got = []
    for m in range(4):
        piece = lax.dynamic_index_in_dim(stacked, c ^ m, 0, keepdims=False)
        got.append(piece if m == 0 else flip(piece, "ctx", m))
    return by_ctx(jnp.stack(got))


def by_ctx(stacked):
    c = lax.axis_index("ctx")
    return jnp.stack(
        [lax.dynamic_index_in_dim(stacked, c ^ i, 0, keepdims=False) for i in range(4)]
    )


def head_side(c, heads, h):
    return (c * heads + h) // GROUP - (c * heads) // GROUP


def qkv_kernel(heads, s_ref, x0, x1, x2, x3, w_ref, cos_ref, sin_ref, rows_o, q_o, kv_o):
    del s_ref
    block = x0.shape[0]
    for m, x in enumerate((x0, x1, x2, x3)):
        rows_o[m] = x[...]
    rows = rows_o[...].reshape(4 * block, x0.shape[1])
    cos, sin = cos_ref[...], sin_ref[...]
    at = 0
    total = (heads + 2) * LANES
    while at < total:
        width = min(3 * LANES, total - at)
        lin = nt(rows, w_ref[at : at + width])
        for j in range(width // LANES):
            slot = at // LANES + j
            v = lin[:, j * LANES : (j + 1) * LANES]
            if slot <= heads:
                v = v * cos + half_turn(v) * sin
            if slot < heads:
                v = (v * 0.125).astype(BF)
                for m in range(4):
                    q_o[m, slot] = v[m * block : (m + 1) * block]
            else:
                v = v.astype(BF)
                lo = (slot - heads) * LANES
                for m in range(4):
                    kv_o[m, :, lo : lo + LANES] = v[m * block : (m + 1) * block]
        at += width


def side_mask(c, heads, block):
    head = lax.broadcasted_iota(jnp.int32, (heads * block, LANES), 0) // block
    lane = lax.broadcasted_iota(jnp.int32, (heads * block, LANES), 1)
    return (lane // D) == ((c * heads + head) // GROUP - (c * heads) // GROUP)


def key_positions(t, block, first, count):
    row = lax.broadcasted_iota(jnp.int32, (count, 1), 0)
    return first + ((row // block) ^ t) * block + row % block


def attn_kernel(
    heads, s_ref, q_ref, k0, k1, k2, k3, w_ref, att_o, lse_o, p0, p1, p2, p3, k_s, vt_s, m_s, l_s, a_s
):
    c, t, prefix = s_ref[0], s_ref[1], s_ref[2]
    block = q_ref.shape[2]
    keys = 4 * block
    wide = heads * block
    for ck in range(4):
        m = c ^ ck
        v = jnp.concatenate([r[m, :, LANES:] for r in (k0, k1, k2, k3)], axis=0)
        vt_s[ck] = jnp.transpose(v.astype(F32)).astype(BF)
        for i, r in enumerate((k0, k1, k2, k3)):
            k_s[ck, i * block : (i + 1) * block] = r[m, :, :LANES]
    mask = side_mask(c, heads, block)
    q_at = lax.broadcasted_iota(jnp.int32, (1, wide), 1) % block + t * block

    for cq in range(4):
        m = c ^ cq
        q = q_ref[m].reshape(wide, LANES)
        m_s[...] = jnp.full_like(m_s, MASKED)
        l_s[...] = jnp.zeros_like(l_s)
        a_s[...] = jnp.zeros_like(a_s)

        def step(ck, q=q, cq=cq):
            s = nt(k_s[ck], q)
            if ck >= cq:
                at = key_positions(t, block, ck * keys, keys)
                seen = (at <= q_at + cq * keys) | (at < prefix)
                s = jnp.where(seen, s, MASKED)
            old = m_s[...]
            top = jnp.maximum(old, jnp.max(s, axis=0, keepdims=True))
            p = jnp.exp(s - top)
            decay = jnp.exp(old - top)
            l_s[...] = l_s[...] * decay + jnp.sum(p, axis=0, keepdims=True)
            a_s[...] = a_s[...] * decay + nn(vt_s[ck], p.astype(BF))
            m_s[...] = top

        for ck in range(4):
            if ck <= cq:
                step(ck)
            else:
                pl.when(ck * keys < prefix)(functools.partial(step, ck))
        o = jnp.transpose(a_s[...] / l_s[...])
        o = jnp.where(mask, o, 0.0).astype(BF)
        for h in range(heads):
            att_o[m, :, h * LANES : (h + 1) * LANES] = o[h * block : (h + 1) * block]
        lse_o[cq] = m_s[...] + jnp.log(l_s[...])
    full = att_o[...].reshape(4 * block, heads * LANES)
    w_at = (heads + 2) * LANES
    part = nn(full, w_ref[w_at : w_at + heads * LANES]).astype(BF)
    for m, r in enumerate((p0, p1, p2, p3)):
        r[...] = part[m * block : (m + 1) * block]


def attn_back_kernel(
    heads, s_ref, y0, y1, y2, y3, w_ref, q_ref, k0, k1, k2, k3, att_ref, lse_ref, cos_ref, sin_ref,
    rows_o, dq_o, g0, g1, g2, g3, do_s, de_s, dqt_s, dk_s, dv_s
):
    c, t, prefix = s_ref[0], s_ref[1], s_ref[2]
    block = q_ref.shape[2]
    keys = 4 * block
    wide = heads * block
    for m, y in enumerate((y0, y1, y2, y3)):
        rows_o[m] = y[...]
    w_at = (heads + 2) * LANES
    do = nt(rows_o[...].reshape(keys, y0.shape[1]), w_ref[w_at : w_at + heads * LANES]).astype(BF)
    for m in range(4):
        for h in range(heads):
            do_s[m, h * block : (h + 1) * block] = do[m * block : (m + 1) * block, h * LANES : (h + 1) * LANES]
    mask = side_mask(c, heads, block)
    for cq in range(4):
        m = c ^ cq
        a = att_ref[m]
        a = jnp.concatenate([a[:, h * LANES : (h + 1) * LANES] for h in range(heads)], axis=0)
        prod = a.astype(F32) * do_s[m].astype(F32)
        de_s[cq] = jnp.sum(jnp.transpose(prod), axis=0, keepdims=True)
    dqt_s[...] = jnp.zeros_like(dqt_s)
    q_at = lax.broadcasted_iota(jnp.int32, (1, wide), 1) % block + t * block
    for ck in range(4):
        mk = c ^ ck
        k = jnp.concatenate([r[mk, :, :LANES] for r in (k0, k1, k2, k3)], axis=0)
        v = jnp.concatenate([r[mk, :, LANES:] for r in (k0, k1, k2, k3)], axis=0)
        kt = jnp.transpose(k.astype(F32)).astype(BF)
        dk_s[...] = jnp.zeros_like(dk_s)
        dv_s[...] = jnp.zeros_like(dv_s)

        def step(cq, k=k, v=v, kt=kt, ck=ck):
            m = c ^ cq
            q = q_ref[m].reshape(wide, LANES)
            d_out = do_s[m]
            p = jnp.exp(nt(k, q) - lse_ref[cq])
            if ck >= cq:
                at = key_positions(t, block, ck * keys, keys)
                seen = (at <= q_at + cq * keys) | (at < prefix)
                p = jnp.where(seen, p, 0.0)
            ds = (p * (nt(v, d_out) - de_s[cq])).astype(BF)
            dk_s[...] += nn(ds, q)
            dv_s[...] += nn(p.astype(BF), d_out)
            dqt_s[cq] += nn(kt, ds)

        for cq in range(4):
            if cq >= ck:
                step(cq)
            else:
                pl.when(ck * keys < prefix)(functools.partial(step, cq))
        for i, r in enumerate((g0, g1, g2, g3)):
            r[mk, :, :LANES] = dk_s[i * block : (i + 1) * block].astype(BF)
            r[mk, :, LANES:] = dv_s[i * block : (i + 1) * block].astype(BF)
    for cq in range(4):
        m = c ^ cq
        dq = jnp.transpose(dqt_s[cq]) * 0.125
        turned = half_turn(dq)
        cos, sin = cos_ref[m], sin_ref[m]
        for h in range(heads):
            own = slice(h * block, (h + 1) * block)
            back = dq[own] * cos - turned[own] * sin
            dq_o[m, :, h * LANES : (h + 1) * LANES] = jnp.where(mask[own], back, 0.0).astype(BF)


def proj_back_kernel(heads, g0, g1, g2, g3, dq_ref, w_ref, cos_ref, sin_ref, d_o, p0, p1, p2, p3):
    block = dq_ref.shape[1]
    low = heads * LANES
    for m in range(4):
        d_o[m, :, :low] = dq_ref[m]
        total = (
            g0[m].astype(F32) + g1[m].astype(F32) + g2[m].astype(F32) + g3[m].astype(F32)
        )
        dk = total[:, :LANES]
        dk = dk * cos_ref[m] - half_turn(dk) * sin_ref[m]
        d_o[m, :, low : low + LANES] = dk.astype(BF)
        d_o[m, :, low + LANES :] = total[:, LANES:].astype(BF)
    full = d_o[...].reshape(4 * block, low + 2 * LANES)
    part = nn(full, w_ref[: low + 2 * LANES]).astype(BF)
    for m, r in enumerate((p0, p1, p2, p3)):
        r[...] = part[m * block : (m + 1) * block]


def chunks(width, step=256):
    return [(at, min(step, width - at)) for at in range(0, width, step)]


def ffn_kernel(x0, x1, x2, x3, w_ref, rows_o, gate_o, up_o, p0, p1, p2, p3, acc):
    block = x0.shape[0]
    for m, x in enumerate((x0, x1, x2, x3)):
        rows_o[m] = x[...]
    rows = rows_o[...].reshape(4 * block, x0.shape[1])
    for at, width in chunks(w_ref.shape[1]):
        g = nt(rows, w_ref[0, at : at + width])
        u = nt(rows, w_ref[1, at : at + width])
        gate_o[:, at : at + width] = g.astype(BF)
        up_o[:, at : at + width] = u.astype(BF)
        hidden = (g / (1.0 + jnp.exp(-g)) * u).astype(BF)
        term = nn(hidden, w_ref[2, at : at + width])
        if at == 0:
            acc[...] = term
        else:
            acc[...] += term
    for m, r in enumerate((p0, p1, p2, p3)):
        r[...] = acc[m * block : (m + 1) * block].astype(BF)


def ffn_back_kernel(
    y0, y1, y2, y3, w_ref, gate_ref, up_ref, rows_o, dg_o, du_o, h_o, p0, p1, p2, p3, acc
):
    block = y0.shape[0]
    for m, y in enumerate((y0, y1, y2, y3)):
        rows_o[m] = y[...]
    rows = rows_o[...].reshape(4 * block, y0.shape[1])
    for at, width in chunks(w_ref.shape[1]):
        own = slice(at, at + width)
        dh = nt(rows, w_ref[2, own])
        g = gate_ref[:, own].astype(F32)
        u = up_ref[:, own].astype(F32)
        s = 1.0 / (1.0 + jnp.exp(-g))
        dg = (dh * u * s * (1.0 + g * (1.0 - s))).astype(BF)
        du = (dh * g * s).astype(BF)
        dg_o[:, own] = dg
        du_o[:, own] = du
        h_o[:, own] = (g * s * u).astype(BF)
        term = nn(dg, w_ref[0, own]) + nn(du, w_ref[1, own])
        if at == 0:
            acc[...] = term
        else:
            acc[...] += term
    for m, r in enumerate((p0, p1, p2, p3)):
        r[...] = acc[m * block : (m + 1) * block].astype(BF)


def weight_grad_kernel(parts, count, *refs):
    lefts, rights, outs = refs[:count], refs[count : 2 * count], refs[2 * count :]
    cols = rights[0].shape[-1] // parts
    rows = lefts[0].shape[0]
    for x in range(parts):
        for at, width in chunks(lefts[0].shape[1]):
            total = None
            for left, right in zip(lefts, rights):
                r = right[:, :, x * cols : (x + 1) * cols].reshape(rows, cols)
                term = tn(left[:, at : at + width], r)
                total = term if total is None else total + term
            outs[x][at : at + width] = total.astype(BF)


def pad_kernel(heads, s_ref, w_ref, o_ref):
    c = s_ref[0]
    o_ref[...] = jnp.zeros_like(o_ref)
    for h in range(heads):
        side = head_side(c, heads, h) * D
        o_ref[pl.ds(pl.multiple_of(h * LANES + side, D), D)] = w_ref[h * D : (h + 1) * D]
        o_ref[pl.ds(pl.multiple_of((heads + 2 + h) * LANES + side, D), D)] = w_ref[
            heads * D + 2 * LANES + h * D : heads * D + 2 * LANES + (h + 1) * D
        ]
    o_ref[heads * LANES : (heads + 2) * LANES] = w_ref[heads * D : heads * D + 2 * LANES]


def unpad_kernel(heads, s_ref, a_ref, b_ref, o_ref):
    c = s_ref[0]
    for h in range(heads):
        at = pl.multiple_of(h * LANES + head_side(c, heads, h) * D, D)
        o_ref[h * D : (h + 1) * D] = a_ref[pl.ds(at, D)]
        lo = heads * D + 2 * LANES + h * D
        o_ref[lo : lo + D] = b_ref[pl.ds(at, D)]
    o_ref[heads * D : heads * D + 2 * LANES] = a_ref[heads * LANES : (heads + 2) * LANES]


def rms(v):
    r = lax.rsqrt(jnp.mean(v * v, axis=-1, keepdims=True) + EPS)
    return v * r, r


def per_device(
    tokens, prefix, w_query, key_weight, value_weight, w_out, w_gate, w_up, w_down, gain_attn, gain_ffn,
    cotangent,
):
    layers = w_query.shape[0]
    seqs, block, width = tokens.shape
    dps = lax.axis_size("dp")
    x, c, t = (lax.axis_index(a) for a in ("dp", "ctx", "tp"))
    heads = w_query.shape[2] // D
    share = w_query.shape[1]
    part = 4 * share
    units = w_gate.shape[2]
    quarter = units // 4
    low = (c * heads) // GROUP
    keys = 4 * block
    long = 4 * keys

    half = D // 2
    freq = jnp.exp(-math.log(10000.0) * jnp.arange(half).astype(F32) / half)
    at = ((c ^ jnp.arange(4)) * keys + t * block)[:, None] + jnp.arange(block)[None, :]
    angle = at.astype(F32).reshape(keys, 1) * freq[None, :]
    cos = jnp.tile(jnp.cos(angle), (1, 4))
    sin = jnp.sin(angle)
    sin = jnp.concatenate([-sin, sin, -sin, sin], axis=1)
    cos4, sin4 = cos.reshape(4, block, LANES), sin.reshape(4, block, LANES)
    scalars = [
        jnp.stack([c, t, prefix[s]]).astype(jnp.int32) for s in range(seqs)
    ]

    gains = jnp.stack([gain_attn, gain_ffn])
    gains = lax.all_gather(gains, ("dp", "ctx"), axis=2, tiled=True).astype(F32)

    def spread_dp(own):
        if dps == 2:
            other = lax.ppermute(own, "dp", [(0, 1), (1, 0)])
            return jnp.concatenate(
                [jnp.where(x == 0, own, other), jnp.where(x == 0, other, own)], axis=-1
            )
        return lax.all_gather(own, "dp", axis=own.ndim - 1, tiled=True)

    def attn_weights(l):
        qo = jnp.concatenate([w_query[l], w_out[l]], axis=1)
        slots = jnp.stack(tp_gather(qo))
        to_ctx = jnp.stack(
            [lax.dynamic_index_in_dim(slots, t ^ i, 0, keepdims=False) for i in range(4)]
        )
        got = ctx_exchange(to_ctx, True).reshape(part, 2 * heads * D).T
        kv = jnp.concatenate([key_weight[l], value_weight[l]], axis=1)
        kv = by_ctx(jnp.stack([kv] + [flip(kv, "ctx", m) for m in (1, 2, 3)]))
        kv = kv.reshape(part, 2 * KEY_VALUE_HEADS * D).T
        k = lax.dynamic_slice_in_dim(kv, low * D, 2 * D, 0)
        v = lax.dynamic_slice_in_dim(kv, (KEY_VALUE_HEADS + low) * D, 2 * D, 0)
        own = jnp.concatenate([got[: heads * D], k, v, got[heads * D :]], axis=0)
        full = spread_dp(own)
        return call(
            functools.partial(pad_kernel, heads),
            [scalars[0], full],
            [((2 * (heads + 1) * LANES, width), BF)],
            smem=1,
        )[0]

    def ffn_weights(l):
        raw = jnp.concatenate([w_gate[l], w_up[l], w_down[l]], axis=0).T
        got = ctx_exchange(raw.reshape(4, quarter, 3 * share), True)
        own = jnp.transpose(got.reshape(4, quarter, 3, share), (2, 1, 0, 3)).reshape(
            3, quarter, part
        )
        slots = [spread_dp(s) for s in tp_gather(own)]
        return jnp.concatenate(slots, axis=1)

    watt = [None] * layers
    wffn = [None] * layers
    for l in range(layers):
        watt[l] = attn_weights(l)
        wffn[l] = ffn_weights(l)

    stream = [tokens[s].astype(F32) for s in range(seqs)]
    kept = {}
    for l in range(layers):
        for s in range(seqs):
            u, _ = rms(stream[s])
            pieces = ctx_gather((u * gains[0, l]).astype(BF))
            rows, q, kv = call(
                functools.partial(qkv_kernel, heads),
                [scalars[s], *pieces, watt[l], cos, sin],
                [((4, block, width), BF), ((4, heads, block, LANES), BF), ((4, block, 2 * LANES), BF)],
                smem=1,
                flops=2 * keys * width * (heads + 2) * LANES,
            )
            kvs = tp_gather(kv)
            att, lse, *parts = call(
                functools.partial(attn_kernel, heads),
                [scalars[s], q, *kvs, watt[l]],
                [((4, block, heads * LANES), BF), ((4, 1, heads * block), F32)] + [((block, width), BF)] * 4,
                smem=1,
                scratch=[
                    pltpu.VMEM((4, keys, LANES), BF),
                    pltpu.VMEM((4, LANES, keys), BF),
                    pltpu.VMEM((1, heads * block), F32),
                    pltpu.VMEM((1, heads * block), F32),
                    pltpu.VMEM((LANES, heads * block), F32),
                ],
                flops=2 * 2 * keys * long * heads * 256 * 0.7 + 2 * keys * heads * LANES * width,
                exps=keys * long * heads,
            )
            middle = stream[s] + ctx_reduce(parts)
            u, _ = rms(middle)
            pieces = ctx_gather((u * gains[1, l]).astype(BF))
            frows, gate, up, *parts = call(
                ffn_kernel,
                [*pieces, wffn[l]],
                [((4, block, width), BF)] + [((keys, units), BF)] * 2 + [((block, width), BF)] * 4,
                scratch=[pltpu.VMEM((keys, width), F32)],
                flops=2 * keys * width * units * 3,
            )
            kept[l, s] = (stream[s], rows, q, kvs, att, lse, middle, frows, gate, up)
            stream[s] = middle + ctx_reduce(parts)

    def norm_back(grad, local, v, gain):
        u, r = rms(v)
        e = local * gain
        grad = grad + r * (e - u * jnp.mean(e * u, axis=-1, keepdims=True))
        return grad, jnp.sum(local * u, axis=0)

    def weight_grad(lefts, rights):
        n = len(lefts)
        u_count = lefts[0].shape[-1]
        return call(
            functools.partial(weight_grad_kernel, dps if dps == 2 else 1, n),
            [a.reshape(keys, u_count) for a in lefts] + list(rights),
            [((u_count, width // dps), BF)] * 2 if dps == 2 else [((u_count, width), BF)],
            flops=2 * n * keys * u_count * width,
        )

    def collect_dp(halves):
        if dps == 2:
            mine = jnp.where(x == 0, halves[0], halves[1])
            other = jnp.where(x == 0, halves[1], halves[0])
            got = lax.ppermute(other, "dp", [(0, 1), (1, 0)])
            return mine.astype(F32) + got.astype(F32)
        return lax.psum_scatter(
            halves[0], "dp", scatter_dimension=halves[0].ndim - 1, tiled=True
        ).astype(F32)

    grads = {}

    def ffn_grads(l, lefts_rights):
        sums = [collect_dp(weight_grad(a, b)).reshape(4, quarter, part) for a, b in lefts_rights]
        slots = [jnp.stack([s[i] for s in sums]).astype(BF) for i in range(4)]
        own = tp_reduce(slots).reshape(3 * quarter, part).astype(BF)
        got = ctx_exchange(own.T.reshape(4, share, 3 * quarter), False).astype(F32)
        got = jnp.transpose(got.reshape(4, share, 3, quarter), (2, 1, 0, 3)).reshape(3, share, units)
        grads[l, "g"], grads[l, "u"], grads[l, "d"] = got[0], got[1], got[2]

    def attn_grads(l, dqkv, rows, att, drows):
        a = weight_grad(dqkv, rows)
        b = weight_grad(att, drows)
        halves = [
            call(
                functools.partial(unpad_kernel, heads),
                [scalars[0], i, j],
                [((2 * heads * D + 2 * LANES, i.shape[1]), BF)],
                smem=1,
            )[0]
            for i, j in zip(a, b)
        ]
        own = collect_dp(halves).astype(BF).T.reshape(4, share, 2 * heads * D + 2 * LANES)
        got = ctx_exchange(own, False)
        lo, hi = heads * D, heads * D + 2 * LANES
        qo = jnp.concatenate([got[:, :, :lo], got[:, :, hi:]], axis=-1)
        qo = [lax.dynamic_index_in_dim(qo, t ^ i, 0, keepdims=False) for i in range(4)]
        qo = tp_reduce(qo)
        grads[l, "q"], grads[l, "o"] = qo[:, :lo], qo[:, lo:]
        kv = got[:, :, lo:hi].astype(F32)
        both = []
        for first in (0, LANES):
            total = jnp.zeros((share, KEY_VALUE_HEADS * D), F32)
            for i in range(4):
                h = i * heads // GROUP
                term = kv[i, :, first : first + LANES]
                total = total + jnp.pad(term, ((0, 0), (h * D, (KEY_VALUE_HEADS - 2 - h) * D)))
            both.append(total)
        both = jnp.concatenate(both, axis=1)
        sent = both.astype(BF)
        for m in (1, 2, 3):
            both = both + flip(sent, "tp", m).astype(F32)
        grads[l, "k"], grads[l, "v"] = (
            both[:, : KEY_VALUE_HEADS * D],
            both[:, KEY_VALUE_HEADS * D :],
        )

    grad = [cotangent[s].astype(F32) for s in range(seqs)]
    gain_sums = {}
    for l in reversed(range(layers)):
        hidden, dgate, dup, dy = [], [], [], []
        gain_sums[1, l] = 0.0
        gain_sums[0, l] = 0.0
        for s in range(seqs):
            _, _, _, _, _, _, middle, frows, gate, up = kept[l, s]
            drows, dg, du, hid, *parts = call(
                ffn_back_kernel,
                [*ctx_gather(grad[s].astype(BF)), wffn[l], gate, up],
                [((4, block, width), BF)] + [((keys, units), BF)] * 3 + [((block, width), BF)] * 4,
                scratch=[pltpu.VMEM((keys, width), F32)],
                flops=2 * keys * width * units * 3,
            )
            hidden.append(hid), dgate.append(dg), dup.append(du), dy.append(drows)
            grad[s], extra = norm_back(grad[s], ctx_reduce(parts), middle, gains[1, l])
            gain_sums[1, l] += extra
        ffn_grads(
            l,
            [
                (dgate, [kept[l, s][7] for s in range(seqs)]),
                (dup, [kept[l, s][7] for s in range(seqs)]),
                (hidden, dy),
            ],
        )
        dqkvs, dys = [], []
        for s in range(seqs):
            start, rows, q, kvs, att, lse, *_ = kept[l, s]
            drows, dq, *dkv = call(
                functools.partial(attn_back_kernel, heads),
                [scalars[s], *ctx_gather(grad[s].astype(BF)), watt[l], q, *kvs, att, lse, cos4, sin4],
                [((4, block, width), BF), ((4, block, heads * LANES), BF)] + [((4, block, 2 * LANES), BF)] * 4,
                smem=1,
                scratch=[
                    pltpu.VMEM((4, heads * block, LANES), BF),
                    pltpu.VMEM((4, 1, heads * block), F32),
                    pltpu.VMEM((4, LANES, heads * block), F32),
                    pltpu.VMEM((keys, LANES), F32),
                    pltpu.VMEM((keys, LANES), F32),
                ],
                flops=2 * 5 * keys * long * heads * 256 * 0.7 + 2 * keys * heads * LANES * width,
                exps=keys * long * heads,
            )
            one = flip(dkv[1], "tp", 1)
            handed = lax.ppermute(dkv[3], "tp", [(0, 1), (3, 2)])
            mid = lax.ppermute(dkv[3], "tp", [(1, 2), (2, 1)])
            two = flip((dkv[2].astype(F32) + handed.astype(F32)).astype(BF), "tp", 2)
            dqkv, *parts = call(
                functools.partial(proj_back_kernel, heads),
                [dkv[0], one, two, mid, dq, watt[l], cos4, sin4],
                [((4, block, (heads + 2) * LANES), BF)] + [((block, width), BF)] * 4,
                flops=2 * keys * (heads + 2) * LANES * width,
            )
            dqkvs.append(dqkv), dys.append(drows)
            grad[s], extra = norm_back(grad[s], ctx_reduce(parts), start, gains[0, l])
            gain_sums[0, l] += extra
        attn_grads(
            l,
            dqkvs,
            [kept[l, s][1] for s in range(seqs)],
            [kept[l, s][4] for s in range(seqs)],
            dys,
        )

    sums = jnp.stack([gain_sums[k, l] for k in range(2) for l in range(layers)])
    sums = lax.psum(sums, ("dp", "ctx", "tp"))
    sums = lax.dynamic_slice_in_dim(sums, (x * 4 + c) * share, share, 1).reshape(2, layers, share)

    def stacked(name):
        return jnp.stack([grads[l, name] for l in range(layers)])

    return (
        jnp.stack(stream).astype(BF),
        jnp.stack(grad),
        stacked("q"),
        stacked("k"),
        stacked("v"),
        stacked("o"),
        stacked("g"),
        stacked("u"),
        stacked("d"),
        sums[0],
        sums[1],
    )


def solution(mesh):
    rows = P("dp", ("ctx", "tp"), None)
    sharded = P(None, ("dp", "ctx"), "tp")
    heads = P(None, ("dp", "ctx"), None)
    gains = P(None, ("dp", "ctx"))
    in_specs = (rows, P("dp"), sharded, heads, heads, sharded, sharded, sharded, sharded, gains, gains, rows)
    out_specs = (rows, rows, sharded, heads, heads, sharded, sharded, sharded, sharded, gains, gains)
    return jax.shard_map(
        per_device, mesh=mesh, in_specs=in_specs, out_specs=out_specs, check_vma=False
    )
```

time: 2740 us -> 1340 us (0.49)
  waiting for transfers between devices: 1520 us -> 457 us
  local copies, waits for them, and re-layouts: 608 us -> 106 us
  Pallas kernels: 0 us -> 339 us
  matrix products: 309 us -> 0 us
  starting transfers between devices: 3.04 us -> 210 us
  blocking collectives: 162 us -> 75.4 us
  other arithmetic: 83.9 us -> 141 us
    reduce_scatter x24 -> x0, waiting for transfers between devices: 891 us -> none  [the longest x4 254 us: collect_rows(): lax.psum_scatter(values.astype(jnp.bfloat16), 'tp', scatter_dimension=1,...]
    all_gather x18 -> x0, waiting for transfers between devices: 509 us -> none  [the longest x4 212 us: spread_grads(): return lax.all_gather(values, 'tp', axis=1, tiled=True)]
    unnamed x211 -> x442, local copies, waits for them, and re-layouts: 486 us -> 23.4 us
    ppermute x0 -> x214, waiting for transfers between devices: none -> 457 us  [the longest x164 289 us: flip(): return lax.ppermute(x, axis, [(i, i ^ m) for i in range(4)])]
    pallas_call x0 -> x40, Pallas kernels: none -> 339 us  [call(): pl.pallas_call(kernel, out_shape=[jax.ShapeDtypeStruct(s, d) for s, d in...]
    dot_general x78 -> x0, matrix products: 309 us -> none  [the longest x14 66.2 us: contract_cols(): lax.dot_general(left_side, right_side, (((1,), (1,)), ((), ())), preferre...]
    ppermute x0 -> x214, starting transfers between devices: none -> 210 us  [the longest x164 141 us: flip(): return lax.ppermute(x, axis, [(i, i ^ m) for i in range(4)])]
    unnamed x47 -> x0, waiting for transfers between devices: 119 us -> none
  transfers between devices with their start and end apart: 45 -> 214, of which waited for: 35 -> 71; matrix products, arithmetic and copies ran while one was open for 24% -> 17% of each run, Pallas kernels for 0% -> 25%
where the time goes in v1:
time: 1340 us; the launch traced here: 1330 us
  waiting for transfers between devices  457 us (34%)
  Pallas kernels  339 us (25%)
  starting transfers between devices  210 us (16%)
  other arithmetic  141 us (11%)
  local copies, waits for them, and re-layouts  106 us (8%)
  blocking collectives  75.4 us (6%)
    pallas_call x40, Pallas kernels, call(): pl.pallas_call(kernel, out_shape=[jax.ShapeDtypeStruct(s, d) for s, d in...  339 us
    ppermute x164, waiting for transfers between devices, flip(): return lax.ppermute(x, axis, [(i, i ^ m) for i in range(4)])  289 us
    ppermute x164, starting transfers between devices, flip(): return lax.ppermute(x, axis, [(i, i ^ m) for i in range(4)])  141 us
    psum x1, blocking collectives, per_device(): sums = lax.psum(sums, ('dp', 'ctx', 'tp'))  65.3 us
    ppermute x8, waiting for transfers between devices, collect_dp(): got = lax.ppermute(other, 'dp', [(0, 1), (1, 0)])  56.7 us
    ppermute x10, waiting for transfers between devices, spread_dp(): other = lax.ppermute(own, 'dp', [(0, 1), (1, 0)])  53.2 us
    ppermute x8, waiting for transfers between devices, tp_gather(): end = lax.ppermute(two, 'tp', [(1, 0), (2, 3)])  52.5 us
    slice x1, local copies, waits for them, and re-layouts, per_device(): pieces = ctx_gather((u * gains[1, l]).astype(BF))  32.8 us
  transfers between devices with their start and end apart: 214, of which 71 were waited for; matrix products, arithmetic and copies ran while one was open for 17% of the time, Pallas kernels for 25%

profile of v1, /device:TPU:0, one launch (start us, length us, event | category | flops | bytes accessed | tf_op | source)
XLA Modules:
  0.0 1332.2 jit_solution(6423240488518518814)
XLA Ops:
  31.3 32.8 %slice_reduce_fusion = (f32[1280]{0:T(1024)}, f32[1280]{0:T(1024)}, f32[1280]{0:T(1024)S(1)}, f32[1280]{0:T(1024)S(1)}) fusion(f32[2,2,1280]{1,0,2:T(2,128)S(1)} %convert_element_type.636), kind=kLoop, calls=%fused_computation.130 | loop fusion | bytes 40960 | tf_op jit(solution)/shard_map/slice | solution.py:491
  200.5 38.6 %collective-permute-done.82 = bf16[4,128,256]{2,1,0:T(8,128)(2,1)S(1)} collective-permute-done((bf16[4,128,256]{2,1,0:T(8,128)(2,1)}, bf16[4,128,256]{2,1,0:T(8,128)(2,1)S(1)}, u32[]{:S(2)}, u32[]{:S(2)}) %collective-permute-start.82) | collective-permute-done | bytes 262176 | tf_op jit(solution)/shard_map/ppermute | solution.py:81
  254.1 13.6 %shard_map.212 = (bf16[4,128,640]{2,1,0:T(8,128)(2,1)}, f32[4,1,640]{2,1,0:T(1,128)}, bf16[128,1280]{1,0:T(8,128)(2,1)}, bf16[128,1280]{1,0:T(8,128)(2,1)}, bf16...) custom-call(s32[3]{0:T(128)} %pad_add_fusion.6.s_ref, bf16[4,5,128,128]{3,2,1,0:T(8,128)(2,1)} %get-tuple-element.191.q_ref, ...), custom_call_target="tpu_custom_call" | custom-call | flops 4596957184 | bytes 7612428 | tf_op jit(solution)/shard_map/pallas_call | solution.py:44
  272.7 14.7 %shard_map.205 = (bf16[4,128,640]{2,1,0:T(8,128)(2,1)}, f32[4,1,640]{2,1,0:T(1,128)}, bf16[128,1280]{1,0:T(8,128)(2,1)}, bf16[128,1280]{1,0:T(8,128)(2,1)}, bf16...) custom-call(s32[3]{0:T(128)} %pad_add_fusion.4.s_ref, bf16[4,5,128,128]{3,2,1,0:T(8,128)(2,1)} %get-tuple-element.171.q_ref, ...), custom_call_target="tpu_custom_call" | custom-call | flops 4596957184 | bytes 7612428 | tf_op jit(solution)/shard_map/pallas_call | solution.py:44
  309.1 11.7 collective-permute-done.31
  321.0 16.5 %collective-permute-done.34 = bf16[3,224,640]{2,1,0:T(8,128)(2,1)S(1)} collective-permute-done((bf16[3,224,640]{2,1,0:T(8,128)(2,1)S(1)}, bf16[3,224,640]{2,1,0:T(8,128)(2,1)S(1)}, u32[]{:S(2)}, u32[]{:S(2)}) %collective-permute-start.34) | collective-permute-done | bytes 860192 | tf_op jit(solution)/shard_map/ppermute | solution.py:418
  400.5 23.1 %collective-permute-done.68 = bf16[3,224,640]{2,1,0:T(8,128)(2,1)} collective-permute-done((bf16[3,224,640]{2,1,0:T(8,128)(2,1)S(1)}, bf16[3,224,640]{2,1,0:T(8,128)(2,1)}, u32[]{:S(2)}, u32[]{:S(2)}) %collective-permute-start.68) | collective-permute-done | bytes 860192 | tf_op jit(solution)/shard_map/ppermute | solution.py:59
  427.1 12.7 collective-permute-done.67
  490.4 14.6 %shard_map.209 = (bf16[4,128,640]{2,1,0:T(8,128)(2,1)}, f32[4,1,640]{2,1,0:T(1,128)}, bf16[128,1280]{1,0:T(8,128)(2,1)}, bf16[128,1280]{1,0:T(8,128)(2,1)}, bf16...) custom-call(s32[3]{0:T(128)} %pad_add_fusion.4.s_ref, bf16[4,5,128,128]{3,2,1,0:T(8,128)(2,1)} %get-tuple-element.181.q_ref, ...), custom_call_target="tpu_custom_call" | custom-call | flops 4596957184 | bytes 7612428 | tf_op jit(solution)/shard_map/pallas_call | solution.py:44
  517.7 14.0 %shard_map.215 = (bf16[4,128,640]{2,1,0:T(8,128)(2,1)}, f32[4,1,640]{2,1,0:T(1,128)}, bf16[128,1280]{1,0:T(8,128)(2,1)}, bf16[128,1280]{1,0:T(8,128)(2,1)}, bf16...) custom-call(s32[3]{0:T(128)} %pad_add_fusion.6.s_ref, bf16[4,5,128,128]{3,2,1,0:T(8,128)(2,1)} %get-tuple-element.201.q_ref, ...), custom_call_target="tpu_custom_call" | custom-call | flops 4596957184 | bytes 7612428 | tf_op jit(solution)/shard_map/pallas_call | solution.py:44
  556.5 11.9 shard_map.217
  617.9 11.9 shard_map.223
  694.6 21.9 %collective-permute-done.206 = bf16[896,640]{1,0:T(8,128)(2,1)S(1)} collective-permute-done((bf16[896,640]{1,0:T(8,128)(2,1)S(1)}, bf16[896,640]{1,0:T(8,128)(2,1)S(1)}, u32[]{:S(2)}, u32[]{:S(2)}) %collective-permute-start.206) | collective-permute-done | bytes 1146912 | tf_op jit(solution)/shard_map/ppermute | solution.py:522
  723.7 17.2 %shard_map.224 = (bf16[4,128,1280]{2,1,0:T(8,128)(2,1)}, bf16[4,128,640]{2,1,0:T(8,128)(2,1)}, bf16[4,128,256]{2,1,0:T(8,128)(2,1)}, bf16[4,128,256]{2,1,0:T(8,1...) custom-call(s32[3]{0:T(128)} %pad_add_fusion.6.s_ref, bf16[128,1280]{1,0:T(8,128)(2,1)} %copy-done.87, ...), custom_call_target="tpu_custom_call" | custom-call | flops 10234101760 | bytes 11151372 | tf_op jit(solution)/shard_map/pallas_call | solution.py:44
  744.2 18.4 %shard_map.218 = (bf16[4,128,1280]{2,1,0:T(8,128)(2,1)}, bf16[4,128,640]{2,1,0:T(8,128)(2,1)}, bf16[4,128,256]{2,1,0:T(8,128)(2,1)}, bf16[4,128,256]{2,1,0:T(8,1...) custom-call(s32[3]{0:T(128)} %pad_add_fusion.4.s_ref, bf16[128,1280]{1,0:T(8,128)(2,1)} %copy-done.84, ...), custom_call_target="tpu_custom_call" | custom-call | flops 10234101760 | bytes 11151372 | tf_op jit(solution)/shard_map/pallas_call | solution.py:44
  785.4 11.2 collective-permute-done.151.g2
  852.1 26.9 %collective-permute-done.209 = bf16[3,224,640]{2,1,0:T(8,128)(2,1)S(1)} collective-permute-done((bf16[3,224,640]{2,1,0:T(8,128)(2,1)S(1)}, bf16[3,224,640]{2,1,0:T(8,128)(2,1)S(1)}, u32[]{:S(2)}, u32[]{:S(2)}) %collective-permute-start.209) | collective-permute-done | bytes 860192 | tf_op jit(solution)/shard_map/ppermute | solution.py:59
  908.3 12.1 shard_map.226
  921.0 11.9 shard_map.220
  1040.0 14.1 %collective-permute-done.195 = bf16[896,640]{1,0:T(8,128)(2,1)S(1)} collective-permute-done((bf16[896,640]{1,0:T(8,128)(2,1)}, bf16[896,640]{1,0:T(8,128)(2,1)S(1)}, u32[]{:S(2)}, u32[]{:S(2)}) %collective-permute-start.195) | collective-permute-done | bytes 1146912 | tf_op jit(solution)/shard_map/ppermute | solution.py:522
  1055.5 18.4 %collective-permute-done.196 = bf16[896,640]{1,0:T(8,128)(2,1)S(1)} collective-permute-done((bf16[896,640]{1,0:T(8,128)(2,1)S(1)}, bf16[896,640]{1,0:T(8,128)(2,1)S(1)}, u32[]{:S(2)}, u32[]{:S(2)}) %collective-permute-start.196) | collective-permute-done | bytes 1146912 | tf_op jit(solution)/shard_map/ppermute | solution.py:522
  1077.0 19.8 %shard_map.227 = (bf16[4,128,1280]{2,1,0:T(8,128)(2,1)}, bf16[4,128,640]{2,1,0:T(8,128)(2,1)}, bf16[4,128,256]{2,1,0:T(8,128)(2,1)}, bf16[4,128,256]{2,1,0:T(8,1...) custom-call(s32[3]{0:T(128)} %pad_add_fusion.6.s_ref, bf16[128,1280]{1,0:T(8,128)(2,1)} %copy-done.100, ...), custom_call_target="tpu_custom_call" | custom-call | flops 10234101760 | bytes 11151372 | tf_op jit(solution)/shard_map/pallas_call | solution.py:44
  1101.6 18.6 %shard_map.221 = (bf16[4,128,1280]{2,1,0:T(8,128)(2,1)}, bf16[4,128,640]{2,1,0:T(8,128)(2,1)}, bf16[4,128,256]{2,1,0:T(8,128)(2,1)}, bf16[4,128,256]{2,1,0:T(8,1...) custom-call(s32[3]{0:T(128)} %pad_add_fusion.4.s_ref, bf16[128,1280]{1,0:T(8,128)(2,1)} %copy-done.85, ...), custom_call_target="tpu_custom_call" | custom-call | flops 10234101760 | bytes 11151372 | tf_op jit(solution)/shard_map/pallas_call | solution.py:44
  1192.1 65.3 %psum.7 = f32[4,1280]{1,0:T(4,128)S(1)} all-reduce(f32[4,1280]{1,0:T(4,128)S(1)} %pad_maximum_fusion.49), channel_id=1, replica_groups=mesh['dp'=2,'ctx'=4,'tp'=4] {'dp','ctx','tp'}, use_global_device_ids=true, to_apply=%region_24.25 | all-reduce | flops 5120 | bytes 40960 | tf_op jit(solution)/shard_map/psum | solution.py:641
  (1158 shorter events, 856.1 us)
Async XLA Ops:
  3.5 72.7 %collective-permute-start.10 = (bf16[160,640]{1,0:T(8,128)(2,1)}, bf16[160,640]{1,0:T(8,128)(2,1)}, u32[]{:S(2)}, u32[]{:S(2)}) collective-permute-start(bf16[160,640]{1,0:T(8,128)(2,1)} %pad_maximum_fusion.46), channel_id=1, source_target_pairs={{0,4},{4,0},{8,12},{12,8},{1,5},{5,1},{9,13},{13,9},{2,6},{6,2},{1... | collective-permute-start | bytes 614408 | tf_op jit(solution)/shard_map/ppermute | solution.py:59
  3.9 74.0 %collective-permute-start.11 = (bf16[160,640]{1,0:T(8,128)(2,1)}, bf16[160,640]{1,0:T(8,128)(2,1)}, u32[]{:S(2)}, u32[]{:S(2)}) collective-permute-start(bf16[160,640]{1,0:T(8,128)(2,1)} %pad_maximum_fusion.46), channel_id=1, source_target_pairs={{0,8},{4,12},{8,0},{12,4},{1,9},{5,13},{9,1},{13,5},{2,10},{6,14},... | collective-permute-start | bytes 614408 | tf_op jit(solution)/shard_map/ppermute | solution.py:59
  6.5 74.1 %collective-permute-start.12 = (bf16[160,640]{1,0:T(8,128)(2,1)}, bf16[160,640]{1,0:T(8,128)(2,1)}, u32[]{:S(2)}, u32[]{:S(2)}) collective-permute-start(bf16[160,640]{1,0:T(8,128)(2,1)} %pad_maximum_fusion.46), channel_id=1, source_target_pairs={{0,12},{4,8},{8,4},{12,0},{1,13},{5,9},{9,5},{13,1},{2,14},{6,10},... | collective-permute-start | bytes 614408 | tf_op jit(solution)/shard_map/ppermute | solution.py:59
  7.4 75.9 %collective-permute-start.48 = (bf16[160,640]{1,0:T(8,128)(2,1)}, bf16[160,640]{1,0:T(8,128)(2,1)}, u32[]{:S(2)}, u32[]{:S(2)}) collective-permute-start(bf16[160,640]{1,0:T(8,128)(2,1)} %pad_maximum_fusion.48), channel_id=1, source_target_pairs={{0,4},{4,0},{8,12},{12,8},{1,5},{5,1},{9,13},{13,9},{2,6},{6,2},{1... | collective-permute-start | bytes 614408 | tf_op jit(solution)/shard_map/ppermute | solution.py:59
  7.5 75.9 %collective-permute-start.49 = (bf16[160,640]{1,0:T(8,128)(2,1)}, bf16[160,640]{1,0:T(8,128)(2,1)}, u32[]{:S(2)}, u32[]{:S(2)}) collective-permute-start(bf16[160,640]{1,0:T(8,128)(2,1)} %pad_maximum_fusion.48), channel_id=1, source_target_pairs={{0,8},{4,12},{8,0},{12,4},{1,9},{5,13},{9,1},{13,5},{2,10},{6,14},... | collective-permute-start | bytes 614408 | tf_op jit(solution)/shard_map/ppermute | solution.py:59
  185.5 82.2 %collective-permute-start.28 = (bf16[3,224,640]{2,1,0:T(8,128)(2,1)S(1)}, bf16[3,224,640]{2,1,0:T(8,128)(2,1)S(1)}, u32[]{:S(2)}, u32[]{:S(2)}) collective-permute-start(bf16[3,224,640]{2,1,0:T(8,128)(2,1)S(1)} %copy-done.24), channel_id=1, source_target_pairs={{0,1},{1,0},{2,3},{3,2},{4,5},{5,4},{6,7},{7,6},{8,9},{9,8},{10,11... | collective-permute-start | bytes 2580488 | tf_op jit(solution)/shard_map/ppermute | solution.py:59
  190.2 79.1 %collective-permute-start.30 = (bf16[3,224,640]{2,1,0:T(8,128)(2,1)S(1)}, bf16[3,224,640]{2,1,0:T(8,128)(2,1)S(1)}, u32[]{:S(2)}, u32[]{:S(2)}) collective-permute-start(bf16[3,224,640]{2,1,0:T(8,128)(2,1)S(1)} %copy-done.24), channel_id=1, source_target_pairs={{0,2},{1,3},{2,0},{3,1},{4,6},{5,7},{6,4},{7,5},{8,10},{9,11},{10,... | collective-permute-start | bytes 2580488 | tf_op jit(solution)/shard_map/ppermute | solution.py:59
  295.8 90.4 %collective-permute-start.66 = (bf16[3,224,640]{2,1,0:T(8,128)(2,1)S(1)}, bf16[3,224,640]{2,1,0:T(8,128)(2,1)}, u32[]{:S(2)}, u32[]{:S(2)}) collective-permute-start(bf16[3,224,640]{2,1,0:T(8,128)(2,1)S(1)} %copy-done.23), channel_id=1, source_target_pairs={{0,1},{1,0},{2,3},{3,2},{4,5},{5,4},{6,7},{7,6},{8,9},{9,8},{10,11... | collective-permute-start | bytes 2580488 | tf_op jit(solution)/shard_map/ppermute | solution.py:59
  475.0 81.5 %collective-permute-start.108 = (bf16[128,1280]{1,0:T(8,128)(2,1)}, bf16[128,1280]{1,0:T(8,128)(2,1)}, u32[]{:S(2)}, u32[]{:S(2)}) collective-permute-start(bf16[128,1280]{1,0:T(8,128)(2,1)} %get-tuple-element.549.y0), channel_id=1, source_target_pairs={{0,4},{4,0},{8,12},{12,8},{1,5},{5,1},{9,13},{13,9},{2,6},{6,2},{1... | collective-permute-start | bytes 983048 | tf_op jit(solution)/shard_map/ppermute | solution.py:59
  483.3 73.2 %collective-permute-start.110 = (bf16[128,1280]{1,0:T(8,128)(2,1)}, bf16[128,1280]{1,0:T(8,128)(2,1)}, u32[]{:S(2)}, u32[]{:S(2)}) collective-permute-start(bf16[128,1280]{1,0:T(8,128)(2,1)} %collective-permute-done.109.y2), channel_id=1, source_target_pairs={{0,4},{4,0},{8,12},{12,8},{1,5},{5,1},{9,13},{13,9},{2,6},{6,2},{1... | collective-permute-start | bytes 983048 | tf_op jit(solution)/shard_map/ppermute | solution.py:59
  658.9 57.6 %collective-permute-start.206 = (bf16[896,640]{1,0:T(8,128)(2,1)S(1)}, bf16[896,640]{1,0:T(8,128)(2,1)S(1)}, u32[]{:S(2)}, u32[]{:S(2)}) collective-permute-start(bf16[896,640]{1,0:T(8,128)(2,1)S(1)} %broadcast_select_fusion), channel_id=1, source_target_pairs={{0,16},{16,0},{1,17},{17,1},{2,18},{18,2},{3,19},{19,3},{4,20},{20... | collective-permute-start | bytes 3440648 | tf_op jit(solution)/shard_map/ppermute | solution.py:522
  689.2 55.0 %collective-permute-start.114 = (bf16[128,1280]{1,0:T(8,128)(2,1)S(1)}, bf16[128,1280]{1,0:T(8,128)(2,1)}, u32[]{:S(2)}, u32[]{:S(2)}) collective-permute-start(bf16[128,1280]{1,0:T(8,128)(2,1)S(1)} %get-tuple-element.361.y0), channel_id=1, source_target_pairs={{0,4},{4,0},{8,12},{12,8},{1,5},{5,1},{9,13},{13,9},{2,6},{6,2},{1... | collective-permute-start | bytes 983048 | tf_op jit(solution)/shard_map/ppermute | solution.py:59
  718.3 106.5 %collective-permute-start.208 = (bf16[3,224,640]{2,1,0:T(8,128)(2,1)}, bf16[3,224,640]{2,1,0:T(8,128)(2,1)}, u32[]{:S(2)}, u32[]{:S(2)}) collective-permute-start(bf16[3,224,640]{2,1,0:T(8,128)(2,1)} %pad_maximum_fusion.23), channel_id=1, source_target_pairs={{0,1},{3,2},{4,5},{7,6},{8,9},{11,10},{12,13},{15,14},{16,17},{19,... | collective-permute-start | bytes 2580488 | tf_op jit(solution)/shard_map/ppermute | solution.py:87
  796.6 55.4 %collective-permute-start.210 = (bf16[3,224,640]{2,1,0:T(8,128)(2,1)}, bf16[3,224,640]{2,1,0:T(8,128)(2,1)}, u32[]{:S(2)}, u32[]{:S(2)}) collective-permute-start(bf16[3,224,640]{2,1,0:T(8,128)(2,1)} %pad_maximum_fusion.23), channel_id=1, source_target_pairs={{1,2},{2,1},{5,6},{6,5},{9,10},{10,9},{13,14},{14,13},{17,18},{18,... | collective-permute-start | bytes 2580488 | tf_op jit(solution)/shard_map/ppermute | solution.py:88
  829.3 56.6 %collective-permute-start.180 = (bf16[896,640]{1,0:T(8,128)(2,1)}, bf16[896,640]{1,0:T(8,128)(2,1)}, u32[]{:S(2)}, u32[]{:S(2)}) collective-permute-start(bf16[896,640]{1,0:T(8,128)(2,1)} %broadcast_select_fusion.6), channel_id=1, source_target_pairs={{0,16},{16,0},{1,17},{17,1},{2,18},{18,2},{3,19},{19,3},{4,20},{20... | collective-permute-start | bytes 3440648 | tf_op jit(solution)/shard_map/ppermute | solution.py:522
  897.8 60.8 %collective-permute-start.181 = (bf16[160,896]{1,0:T(8,128)(2,1)}, bf16[160,896]{1,0:T(8,128)(2,1)}, u32[]{:S(2)}, u32[]{:S(2)}) collective-permute-start(bf16[160,896]{1,0:T(8,128)(2,1)} %get-tuple-element.448), channel_id=1, source_target_pairs={{0,4},{4,0},{8,12},{12,8},{1,5},{5,1},{9,13},{13,9},{2,6},{6,2},{1... | collective-permute-start | bytes 860168 | tf_op jit(solution)/shard_map/ppermute | solution.py:59
  920.4 70.3 %collective-permute-start.160 = (bf16[128,1280]{1,0:T(8,128)(2,1)}, bf16[128,1280]{1,0:T(8,128)(2,1)S(1)}, u32[]{:S(2)}, u32[]{:S(2)}) collective-permute-start(bf16[128,1280]{1,0:T(8,128)(2,1)} %get-tuple-element.267), channel_id=1, source_target_pairs={{0,4},{4,0},{8,12},{12,8},{1,5},{5,1},{9,13},{13,9},{2,6},{6,2},{1... | collective-permute-start | bytes 983048 | tf_op jit(solution)/shard_map/ppermute | solution.py:59
  920.9 97.2 %collective-permute-start.159 = (bf16[128,1280]{1,0:T(8,128)(2,1)}, bf16[128,1280]{1,0:T(8,128)(2,1)S(1)}, u32[]{:S(2)}, u32[]{:S(2)}) collective-permute-start(bf16[128,1280]{1,0:T(8,128)(2,1)} %get-tuple-element.265), channel_id=1, source_target_pairs={{0,4},{4,0},{8,12},{12,8},{1,5},{5,1},{9,13},{13,9},{2,6},{6,2},{1... | collective-permute-start | bytes 983048 | tf_op jit(solution)/shard_map/ppermute | solution.py:59
  1010.0 63.9 %collective-permute-start.196 = (bf16[896,640]{1,0:T(8,128)(2,1)S(1)}, bf16[896,640]{1,0:T(8,128)(2,1)S(1)}, u32[]{:S(2)}, u32[]{:S(2)}) collective-permute-start(bf16[896,640]{1,0:T(8,128)(2,1)S(1)} %broadcast_select_fusion.3), channel_id=1, source_target_pairs={{0,16},{16,0},{1,17},{17,1},{2,18},{18,2},{3,19},{19,3},{4,20},{20... | collective-permute-start | bytes 3440648 | tf_op jit(solution)/shard_map/ppermute | solution.py:522
  1035.5 65.2 %collective-permute-start.130 = (bf16[128,1280]{1,0:T(8,128)(2,1)S(1)}, bf16[128,1280]{1,0:T(8,128)(2,1)S(1)}, u32[]{:S(2)}, u32[]{:S(2)}) collective-permute-start(bf16[128,1280]{1,0:T(8,128)(2,1)S(1)} %get-tuple-element.357.y0), channel_id=1, source_target_pairs={{0,4},{4,0},{8,12},{12,8},{1,5},{5,1},{9,13},{13,9},{2,6},{6,2},{1... | collective-permute-start | bytes 983048 | tf_op jit(solution)/shard_map/ppermute | solution.py:59
  1179.2 82.0 %collective-permute-start.200 = (bf16[3,224,640]{2,1,0:T(8,128)(2,1)}, bf16[3,224,640]{2,1,0:T(8,128)(2,1)}, u32[]{:S(2)}, u32[]{:S(2)}) collective-permute-start(bf16[3,224,640]{2,1,0:T(8,128)(2,1)} %pad_maximum_fusion.21), channel_id=1, source_target_pairs={{1,2},{2,1},{5,6},{6,5},{9,10},{10,9},{13,14},{14,13},{17,18},{18,... | collective-permute-start | bytes 2580488 | tf_op jit(solution)/shard_map/ppermute | solution.py:88
  1181.9 79.3 %collective-permute-start.197 = (bf16[3,224,640]{2,1,0:T(8,128)(2,1)}, bf16[3,224,640]{2,1,0:T(8,128)(2,1)}, u32[]{:S(2)}, u32[]{:S(2)}) collective-permute-start(bf16[3,224,640]{2,1,0:T(8,128)(2,1)} %pad_maximum_fusion.20), channel_id=1, source_target_pairs={{0,1},{1,0},{2,3},{3,2},{4,5},{5,4},{6,7},{7,6},{8,9},{9,8},{10,11... | collective-permute-start | bytes 2580488 | tf_op jit(solution)/shard_map/ppermute | solution.py:59
  1182.8 85.1 %collective-permute-start.172 = (bf16[896,640]{1,0:T(8,128)(2,1)}, bf16[896,640]{1,0:T(8,128)(2,1)}, u32[]{:S(2)}, u32[]{:S(2)}) collective-permute-start(bf16[896,640]{1,0:T(8,128)(2,1)} %broadcast_select_fusion.7), channel_id=1, source_target_pairs={{0,16},{16,0},{1,17},{17,1},{2,18},{18,2},{3,19},{19,3},{4,20},{20... | collective-permute-start | bytes 3440648 | tf_op jit(solution)/shard_map/ppermute | solution.py:522
  1185.2 76.0 %collective-permute-start.199 = (bf16[3,224,640]{2,1,0:T(8,128)(2,1)}, bf16[3,224,640]{2,1,0:T(8,128)(2,1)}, u32[]{:S(2)}, u32[]{:S(2)}) collective-permute-start(bf16[3,224,640]{2,1,0:T(8,128)(2,1)} %add_convert_fusion.11), channel_id=1, source_target_pairs={{0,2},{1,3},{2,0},{3,1},{4,6},{5,7},{6,4},{7,5},{8,10},{9,11},{10,... | collective-permute-start | bytes 2580488 | tf_op jit(solution)/shard_map/ppermute | solution.py:59
  (406 other events, 5982.1 us)

commit v2 on v1

--- a/solution.py
+++ b/solution.py
@@ -1,5 +1,6 @@
 import functools
 import math
+import types
 
 import jax
 import jax.numpy as jnp
@@ -18,6 +19,8 @@
 F32 = jnp.float32
 SLOTS = 4
 LANES = 128
+DP, CTX, TP = "dp", "ctx", "tp"
+PREFIX_MAX = 1024
 
 
 def nt(a, b):
@@ -60,14 +63,14 @@
 
 
 def ctx_gather(x):
-    far = flip(x, "ctx", 2)
-    return [x, flip(x, "ctx", 1), far, flip(far, "ctx", 1)]
+    far = flip(x, CTX, 2)
+    return [x, flip(x, CTX, 1), far, flip(far, CTX, 1)]
 
 
 def ctx_reduce(parts):
-    far = (parts[2].astype(F32) + flip(parts[3], "ctx", 1).astype(F32)).astype(BF)
-    near = flip(parts[1], "ctx", 1)
-    return parts[0].astype(F32) + near.astype(F32) + flip(far, "ctx", 2).astype(F32)
+    far = (parts[2].astype(F32) + flip(parts[3], CTX, 1).astype(F32)).astype(BF)
+    near = flip(parts[1], CTX, 1)
+    return parts[0].astype(F32) + near.astype(F32) + flip(far, CTX, 2).astype(F32)
 
 
 def inner(t):
@@ -75,34 +78,34 @@
 
 
 def tp_gather(x):
-    t = lax.axis_index("tp")
-    two = flip(x, "tp", 2)
-    mid = lax.ppermute(x, "tp", [(1, 2), (2, 1)])
-    end = lax.ppermute(two, "tp", [(1, 0), (2, 3)])
-    return [x, flip(x, "tp", 1), two, jnp.where(inner(t), mid, end)]
+    t = lax.axis_index(TP)
+    two = flip(x, TP, 2)
+    mid = lax.ppermute(x, TP, [(1, 2), (2, 1)])
+    end = lax.ppermute(two, TP, [(1, 0), (2, 3)])
+    return [x, flip(x, TP, 1), two, jnp.where(inner(t), mid, end)]
 
 
 def tp_reduce(parts):
-    one = flip(parts[1], "tp", 1)
-    handed = lax.ppermute(parts[3], "tp", [(0, 1), (3, 2)])
-    mid = lax.ppermute(parts[3], "tp", [(1, 2), (2, 1)])
-    two = flip((parts[2].astype(F32) + handed.astype(F32)).astype(BF), "tp", 2)
+    one = flip(parts[1], TP, 1)
+    handed = lax.ppermute(parts[3], TP, [(0, 1), (3, 2)])
+    mid = lax.ppermute(parts[3], TP, [(1, 2), (2, 1)])
+    two = flip((parts[2].astype(F32) + handed.astype(F32)).astype(BF), TP, 2)
     return (
         parts[0].astype(F32) + one.astype(F32) + two.astype(F32) + mid.astype(F32)
     )
 
 
 def ctx_exchange(stacked, own_first):
-    c = lax.axis_index("ctx")
+    c = lax.axis_index(CTX)
     got = []
     for m in range(4):
         piece = lax.dynamic_index_in_dim(stacked, c ^ m, 0, keepdims=False)
-        got.append(piece if m == 0 else flip(piece, "ctx", m))
+        got.append(piece if m == 0 else flip(piece, CTX, m))
     return by_ctx(jnp.stack(got))
 
 
 def by_ctx(stacked):
-    c = lax.axis_index("ctx")
+    c = lax.axis_index(CTX)
     return jnp.stack(
         [lax.dynamic_index_in_dim(stacked, c ^ i, 0, keepdims=False) for i in range(4)]
     )
@@ -376,6 +379,1141 @@
     o_ref[heads * D : heads * D + 2 * LANES] = a_ref[heads * LANES : (heads + 2) * LANES]
 
 
+def xor(a, b):
+    return lax.rem(a + b, 2) + 2 * lax.rem(lax.div(a, 2) + lax.div(b, 2), 2)
+
+
+class Net:
+    def __init__(self, r):
+        self.r = r
+        self.sems = (r.send, r.recv, r.loc)
+        self.remote, self.local_at = 0, 0
+        self.x, self.c, self.t = (lax.axis_index(a) for a in (DP, CTX, TP))
+        self.inner = (self.t == 1) | (self.t == 2)
+
+    def barrier(self):
+        sem = pltpu.get_barrier_semaphore()
+        peers = [(CTX, 1), (CTX, 2), (CTX, 3), (TP, 1), (TP, 2), (TP, 3), (DP, 1)]
+        for axis, m in peers:
+            pl.semaphore_signal(
+                sem, inc=1, device_id={axis: self.peer(axis, m)}, device_id_type=pl.DeviceIdType.MESH
+            )
+        pl.semaphore_wait(sem, len(peers))
+
+    def peer(self, axis, m):
+        if axis == DP:
+            return 1 - self.x
+        return xor(self.c if axis == CTX else self.t, m)
+
+    def make(self, src, dst, axis, m):
+        i = self.remote
+        self.remote += 1
+        return pltpu.make_async_remote_copy(
+            src_ref=src,
+            dst_ref=dst,
+            send_sem=self.sems[0].at[i],
+            recv_sem=self.sems[1].at[i],
+            device_id={axis: self.peer(axis, m)},
+            device_id_type=pl.DeviceIdType.MESH,
+        )
+
+    def send(self, src, dst, axis, m=1):
+        copy = self.make(src, dst, axis, m)
+        copy.start()
+        return copy
+
+    def local(self, src, dst):
+        i = self.local_at
+        self.local_at += 1
+        copy = pltpu.make_async_copy(src, dst, self.sems[2].at[i])
+        copy.start()
+        return copy
+
+    def close(self, copies):
+        for copy in copies:
+            copy.wait_send()
+
+    def spread_tp(self, src, slots):
+        two = self.send(src, slots[2], TP, 2)
+        one = self.send(src, slots[1], TP, 1)
+        mid = self.make(src, slots[3], TP, 3)
+        end = self.make(slots[2], slots[3], TP, 1)
+        return one, two, mid, end
+
+    def spread_tp_on(self, copies):
+        _, two, mid, end = copies
+        two.wait_recv()
+
+        @pl.when(self.inner)
+        def _():
+            end.start()
+            mid.start()
+
+    def spread_tp_last(self, copies):
+        _, _, mid, end = copies
+        pl.when(self.inner)(mid.wait_recv)
+        pl.when(jnp.logical_not(self.inner))(end.wait_recv)
+
+    def spread_tp_close(self, copies):
+        one, two, mid, end = copies
+        self.close([one, two])
+
+        @pl.when(self.inner)
+        def _():
+            mid.wait_send()
+            end.wait_send()
+
+
+def run(tasks):
+    for task in tasks:
+        next(task, None)
+
+
+def forward_kernel(cfg, r):
+    layers, seqs, block, width, heads, units, share = cfg
+    part, quarter, keys = 4 * share, units // 4, 4 * block
+    net = Net(r)
+    x, c, t = net.x, net.c, net.t
+    low = lax.div(c * heads, GROUP)
+    half = pl.ds(pl.multiple_of(x * part, LANES), part)
+    prefix = [r.prefix[s] for s in range(seqs)]
+    kept = []
+    gu_copy = []
+
+    net.barrier()
+
+    def attn_weights(l):
+        qz, qc, kvl, own, tmp, wa = r.qz.at[l], r.qc.at[l], r.kvl.at[l], r.own, r.tmp, r.wa
+        mine = [net.local(r.qo.at[l], qz.at[0]), net.local(r.kvw.at[l], kvl.at[c])]
+        tp = net.spread_tp(r.qo.at[l], [qz.at[i] for i in range(4)])
+        kvs = [net.send(r.kvw.at[l], kvl.at[c], CTX, m) for m in (1, 2, 3)]
+        wide = heads * LANES
+        wa[l, :wide] = jnp.zeros((wide, width), BF)
+        wa[l, wide + 2 * LANES :] = jnp.zeros((wide, width), BF)
+        yield
+        net.spread_tp_on(tp)
+        yield
+        mine[0].wait()
+        tp[0].wait_recv()
+        net.spread_tp_last(tp)
+        mine.append(net.local(qz.at[xor(t, c)], qc.at[c]))
+        ctx = [net.send(qz.at[xor(t, xor(c, m))], qc.at[c], CTX, m) for m in (1, 2, 3)]
+        yield
+        for copy in kvs + ctx:
+            copy.wait_recv()
+        mine[1].wait()
+        mine[2].wait()
+        stage = [net.local(qc, r.st_q), net.local(kvl, r.st_k)]
+        stage[0].wait()
+        for at in range(0, 2 * heads * D, LANES):
+            got = jnp.transpose(r.st_q[:, :, at : at + LANES].reshape(part, LANES).astype(F32)).astype(BF)
+            for k in range(0, LANES, D):
+                to = at + k if at + k < heads * D else at + k + 2 * LANES
+                own[to : to + D] = got[k : k + D]
+        stage[1].wait()
+        for at in range(0, 2 * KEY_VALUE_HEADS * D, LANES):
+            got = r.st_k[:, :, at : at + LANES].reshape(part, LANES)
+            tmp[at : at + LANES] = jnp.transpose(got.astype(F32)).astype(BF)
+        own[heads * D : heads * D + LANES] = tmp[pl.ds(pl.multiple_of(low * D, D), LANES)]
+        own[heads * D + LANES : heads * D + 2 * LANES] = tmp[
+            pl.ds(pl.multiple_of((KEY_VALUE_HEADS + low) * D, D), LANES)
+        ]
+        dp = net.send(own, r.wc.at[l, :, half], DP)
+        mine.append(net.local(own, r.wc.at[l, :, half]))
+        yield
+        dp.wait_recv()
+        mine[3].wait()
+        pads = []
+        for h in range(heads):
+            side = (lax.div(c * heads + h, GROUP) - low) * D
+            for src, dst in ((h * D, h * LANES), (heads * D + 2 * LANES + h * D, (heads + 2 + h) * LANES)):
+                pads.append(
+                    net.local(
+                        r.wc.at[l, src : src + D],
+                        wa.at[l, pl.ds(pl.multiple_of(dst + side, D), D)],
+                    )
+                )
+        pads.append(
+            net.local(r.wc.at[l, heads * D : heads * D + 2 * LANES], wa.at[l, wide : wide + 2 * LANES])
+        )
+        yield
+        for copy in pads:
+            copy.wait()
+        net.close(kvs + ctx + [dp])
+        net.spread_tp_close(tp)
+        kept.append(net.local(wa.at[l], r.wa_o.at[l]))
+        yield
+
+    def ffn_weights(l):
+        fc, wf = r.fc.at[l], r.wf
+        ctx = [net.send(r.fp.at[l, xor(c, m)], fc.at[c], CTX, m) for m in (1, 2, 3)]
+        mine = net.local(r.fp.at[l, c], fc.at[c])
+        yield
+        for copy in ctx:
+            copy.wait_recv()
+        mine.wait()
+        stage = net.local(fc, r.st_f)
+        stage.wait()
+        for i in range(3):
+            piece = [r.st_f[k][:, i * share : (i + 1) * share] for k in range(4)]
+            wf[l, i, :quarter, half] = jnp.concatenate(piece, axis=1)
+        yield
+        slots = [wf.at[l, :, i * quarter : (i + 1) * quarter, half] for i in range(4)]
+        tp = net.spread_tp(slots[0], slots)
+        dp = [net.send(slots[0], slots[0], DP)]
+        yield
+        net.spread_tp_on(tp)
+        dp.append(net.send(slots[2], slots[2], DP))
+        tp[0].wait_recv()
+        dp.append(net.send(slots[1], slots[1], DP))
+        yield
+        net.spread_tp_last(tp)
+        dp.append(net.send(slots[3], slots[3], DP))
+        yield
+        for copy in dp:
+            copy.wait_recv()
+        net.close(ctx + dp)
+        net.spread_tp_close(tp)
+        kept.append(net.local(wf.at[l], r.wf_o.at[l]))
+        yield
+
+    def gather_start(v, gain, s, rows):
+        u = v * lax.rsqrt(jnp.mean(v * v, axis=-1, keepdims=True) + EPS)
+        rows[s, 0] = (u * gain).astype(BF)
+        return [
+            net.send(rows.at[s, 0], rows.at[s, 2], CTX, 2),
+            net.send(rows.at[s, 0], rows.at[s, 1], CTX, 1),
+        ]
+
+    def gather_on(copies, s, rows):
+        copies[0].wait_recv()
+        copies.append(net.send(rows.at[s, 2], rows.at[s, 3], CTX, 1))
+
+    def gather_end(copies):
+        copies[1].wait_recv()
+        copies[2].wait_recv()
+
+    def reduce_start(s):
+        pt, rn = r.pt, r.rn
+        return [
+            net.send(pt.at[s, 3], rn.at[s, 1], CTX, 1),
+            net.send(pt.at[s, 1], rn.at[s, 0], CTX, 1),
+        ]
+
+    def reduce_on(copies, s):
+        copies[0].wait_recv()
+        r.far[s] = (r.pt[s, 2].astype(F32) + r.rn[s, 1].astype(F32)).astype(BF)
+        copies.append(net.send(r.far.at[s], r.rf.at[s], CTX, 2))
+
+    def reduce_end(copies, s):
+        copies[1].wait_recv()
+        copies[2].wait_recv()
+        total = r.pt[s, 0].astype(F32) + r.rn[s, 0].astype(F32) + r.rf[s].astype(F32)
+        net.close(copies)
+        return total
+
+    def sequence(s):
+        rows, frows, q, att, pt, gu = r.rows, r.frows, r.q, r.att, r.pt, r.gu
+        carry = []
+        for l in range(layers):
+            kv = r.kv
+            gather = gather_start(r.stream[s], r.gain[l : l + 1], s, rows)
+            yield
+            gather_on(gather, s, rows)
+            yield
+            gather_end(gather)
+            qkv_body(heads, rows.at[s], r.wa.at[l], r.cos, r.sin, q.at[s], kv.at[l, s, 0])
+            tp = net.spread_tp(kv.at[l, s, 0], [kv.at[l, s, i] for i in range(4)])
+            outs = [net.local(rows.at[s], r.rows_o.at[l, s]), net.local(q.at[s], r.q_o.at[l, s])] + carry
+            yield
+            net.spread_tp_on(tp)
+            yield
+            tp[0].wait_recv()
+            net.spread_tp_last(tp)
+            outs.append(net.local(kv.at[l, s], r.kv_o.at[l, s]))
+            attn_body(
+                heads, c, t, prefix[s], q.at[s], kv.at[l, s], r.wa.at[l], att.at[s], r.lse.at[s],
+                pt.at[s], r.k_s, r.vt_s, r.m_s, r.l_s, r.a_s,
+            )
+            reduce = reduce_start(s)
+            outs.append(net.local(att.at[s], r.att_o.at[l, s]))
+            outs.append(net.local(r.lse.at[s], r.lse_o.at[l, s]))
+            net.close(gather)
+            yield
+            reduce_on(reduce, s)
+            yield
+            r.middle[s] = r.stream[s] + reduce_end(reduce, s)
+            outs.append(net.local(r.middle.at[s], r.middle_o.at[l, s]))
+            gather = gather_start(r.middle[s], r.gain[layers + l : layers + l + 1], s, frows)
+            yield
+            gather_on(gather, s, frows)
+            yield
+            gather_end(gather)
+            outs.pop(0).wait()
+            if gu_copy:
+                gu_copy.pop().wait()
+            ffn_body(frows.at[s], r.wf.at[l], gu, pt.at[s], r.hid)
+            reduce = reduce_start(s)
+            outs.append(net.local(frows.at[s], r.frows_o.at[l, s]))
+            gu_copy.append(net.local(gu, r.gu_o.at[l, s]))
+            net.close(gather)
+            net.spread_tp_close(tp)
+            yield
+            reduce_on(reduce, s)
+            yield
+            for copy in outs:
+                copy.wait()
+            r.stream[s] = r.middle[s] + reduce_end(reduce, s)
+            if l + 1 < layers:
+                carry = [net.local(r.stream.at[s], r.stream_o.at[l, s])]
+            else:
+                r.far[s] = r.stream[s].astype(BF)
+                kept.append(net.local(r.far.at[s], r.out_o.at[s]))
+            yield
+
+    gl = r.gl
+    start = net.local(r.tokens, r.far)
+    gl[x, c] = r.gains[...]
+    near = [net.send(gl.at[x, c], gl.at[x, c], CTX, m) for m in (1, 2, 3)]
+    (w0, w1), (f0, f1) = [attn_weights(l) for l in range(layers)], [ffn_weights(l) for l in range(layers)]
+    run([f0, w0])
+    start.wait()
+    r.stream[...] = r.far[...].astype(F32)
+    for copy in near:
+        copy.wait_recv()
+    over = net.send(gl.at[x], gl.at[x], DP)
+    over.wait_recv()
+    pieces = [gl[k, i][: 2 * layers, :share] for k in range(2) for i in range(4)]
+    r.gain[...] = jnp.concatenate(pieces, axis=1)
+    kept.append(net.local(r.gain, r.gain_o))
+
+    def cotangent():
+        cot, dy = r.cot, r.dy_o
+        mine = [net.local(cot.at[s], dy.at[s, 0]) for s in range(seqs)]
+        far = [net.send(cot.at[s], dy.at[s, 2], CTX, 2) for s in range(seqs)]
+        side = [net.send(cot.at[s], dy.at[s, 1], CTX, 1) for s in range(seqs)]
+        yield
+        for s in range(seqs):
+            far[s].wait_recv()
+            side.append(net.send(dy.at[s, 2], dy.at[s, 3], CTX, 1))
+        yield
+        for copy in side:
+            copy.wait_recv()
+        for copy in mine:
+            copy.wait()
+        net.close(far + side)
+        yield
+
+    a, b, extra = sequence(0), sequence(1), cotangent()
+    order = (
+        w0, f0, a, f0, w0, w0, b, f0, b, f1, w0, w0, b, b,
+        f1, a, w1, a, f0, b, b, w1, a, f1, w1, b, a, f0,
+        a, b, w1, b, a, b, a, f1, a, b, b, a, w1, w1,
+        b, b, a, a, b, extra, f1, a, a, b, extra, a, b, a,
+        b, a, b, extra, a, f1, b, a, b, a, a, b, a,
+    )
+    run(order)
+    net.close(near + [over])
+    for copy in kept + gu_copy:
+        copy.wait()
+
+
+def qkv_body(heads, rows_ref, w_ref, cos_ref, sin_ref, q_o, kv_o):
+    block, width = rows_ref.shape[1], rows_ref.shape[2]
+    rows = rows_ref[...].reshape(4 * block, width)
+    cos, sin = cos_ref[...], sin_ref[...]
+    at = 0
+    total = (heads + 2) * LANES
+    while at < total:
+        wide = min(3 * LANES, total - at)
+        lin = nt(rows, w_ref[at : at + wide])
+        for j in range(wide // LANES):
+            slot = at // LANES + j
+            v = lin[:, j * LANES : (j + 1) * LANES]
+            if slot <= heads:
+                v = v * cos + half_turn(v) * sin
+            if slot < heads:
+                v = (v * 0.125).astype(BF)
+                for m in range(4):
+                    q_o[m, slot] = v[m * block : (m + 1) * block]
+            else:
+                v = v.astype(BF)
+                lo = (slot - heads) * LANES
+                for m in range(4):
+                    kv_o[m, :, lo : lo + LANES] = v[m * block : (m + 1) * block]
+        at += wide
+
+
+def attn_body(heads, c, t, prefix, q_ref, kv_ref, w_ref, att_o, lse_o, pt_o, k_s, vt_s, m_s, l_s, a_s):
+    block = q_ref.shape[2]
+    keys = 4 * block
+    wide = heads * block
+    for ck in range(4):
+        m = xor(c, ck)
+        v = jnp.concatenate([kv_ref[i, m, :, LANES:] for i in range(4)], axis=0)
+        vt_s[ck] = jnp.transpose(v.astype(F32)).astype(BF)
+        for i in range(4):
+            k_s[ck, i * block : (i + 1) * block] = kv_ref[i, m, :, :LANES]
+    mask = side_mask(c, heads, block)
+    q_at = lax.broadcasted_iota(jnp.int32, (1, wide), 1) % block + t * block
+    for cq in range(4):
+        m = xor(c, cq)
+        q_all = q_ref[m].reshape(wide, LANES)
+        for first, span in chunks(wide, 3 * LANES):
+            own = slice(first, first + span)
+            q = q_all[own]
+            for ck in range(4):
+                if ck > cq and ck * keys >= PREFIX_MAX:
+                    continue
+                s = nt(k_s[ck], q)
+                if ck >= cq:
+                    at = key_positions(t, block, ck * keys, keys)
+                    seen = (at <= q_at[:, own] + cq * keys) | (at < prefix)
+                    s = jnp.where(seen, s, MASKED)
+                top = jnp.max(s, axis=0, keepdims=True)
+                if ck:
+                    old = m_s[:, own]
+                    top = jnp.maximum(old, top)
+                    decay = jnp.exp(old - top)
+                p = jnp.exp(s - top)
+                add, term = jnp.sum(p, axis=0, keepdims=True), nn(vt_s[ck], p.astype(BF))
+                l_s[:, own] = l_s[:, own] * decay + add if ck else add
+                a_s[:, own] = a_s[:, own] * decay + term if ck else term
+                m_s[:, own] = top
+        o = jnp.transpose(a_s[...] / l_s[...])
+        o = jnp.where(mask, o, 0.0).astype(BF)
+        for h in range(heads):
+            att_o[m, :, h * LANES : (h + 1) * LANES] = o[h * block : (h + 1) * block]
+        lse_o[cq] = m_s[...] + jnp.log(l_s[...])
+    full = att_o[...].reshape(4 * block, heads * LANES)
+    w_at = (heads + 2) * LANES
+    for at, span in chunks(w_ref.shape[1]):
+        own = slice(at, at + span)
+        part = nn(full, w_ref[w_at : w_at + heads * LANES, own]).astype(BF)
+        for m in range(4):
+            pt_o[m, :, own] = part[m * block : (m + 1) * block]
+
+
+def ffn_body(rows_ref, w_ref, gu_o, pt_o, hid):
+    block, width = rows_ref.shape[1], rows_ref.shape[2]
+    rows = rows_ref[...].reshape(4 * block, width)
+    for at, wide in chunks(w_ref.shape[1]):
+        own = slice(at, at + wide)
+        g = nt(rows, w_ref[0, own])
+        u = nt(rows, w_ref[1, own])
+        gu_o[0, :, own] = g.astype(BF)
+        gu_o[1, :, own] = u.astype(BF)
+        hid[:, own] = (g / (1.0 + jnp.exp(-g)) * u).astype(BF)
+    for at, wide in chunks(width):
+        own = slice(at, at + wide)
+        part = nn(hid[...], w_ref[2, :, own]).astype(BF)
+        for m in range(4):
+            pt_o[m, :, own] = part[m * block : (m + 1) * block]
+
+
+def launch(kernel, number, ins, outs, scratch, sems=(80, 90), vmem=62):
+    sem = pltpu.SemaphoreType.DMA
+    scratch = {k: pltpu.VMEM(*v) for k, v in scratch.items()}
+    scratch.update(send=sem((sems[0],)), recv=sem((sems[0],)), loc=sem((sems[1],)))
+    names = [*ins, *outs, *scratch]
+
+    def body(*refs):
+        kernel(types.SimpleNamespace(**dict(zip(names, refs))))
+
+    got = pl.pallas_call(
+        body,
+        out_shape=[jax.ShapeDtypeStruct(v[0], v[1]) for v in outs.values()],
+        in_specs=[pl.BlockSpec(memory_space=v[1]) for v in ins.values()],
+        out_specs=[pl.BlockSpec(memory_space=v[2]) for v in outs.values()],
+        scratch_shapes=list(scratch.values()),
+        compiler_params=pltpu.CompilerParams(
+            collective_id=number, has_side_effects=True, vmem_limit_bytes=vmem * 2**20
+        ),
+        cost_estimate=pl.CostEstimate(flops=10**11, bytes_accessed=10**8, transcendentals=10**7),
+    )(*[v[0] for v in ins.values()])
+    return types.SimpleNamespace(**dict(zip(outs, got)))
+
+
+def forward_pass(cfg, tokens, cot, prefix, gains, qo, kvw, fp, cos, sin):
+    layers, seqs, block, width, heads, units, share = cfg
+    hbm, vm = pl.ANY, pltpu.VMEM
+    keys, part = 4 * block, 4 * share
+    rows = (seqs, 4, block, width)
+    own = (seqs, block, width)
+    size = 2 * (heads + 1) * LANES
+    compact = 2 * heads * D + 2 * LANES
+    q_s = (4, heads, block, LANES)
+    kv_s = (4, 4, block, 2 * LANES)
+    raw = (4, share, 2 * heads * D)
+    raw_k = (4, share, 2 * KEY_VALUE_HEADS * D)
+    raw_f = (4, units // 4, 3 * share)
+    return launch(
+        functools.partial(forward_kernel, cfg),
+        0,
+        dict(
+            prefix=(prefix, pltpu.SMEM), tokens=(tokens, hbm), cot=(cot, hbm), gains=(gains, vm), qo=(qo, hbm),
+            kvw=(kvw, hbm), fp=(fp, hbm), cos=(cos, vm), sin=(sin, vm),
+        ),
+        dict(
+            out_o=(own, BF, hbm),
+            wc=((layers, compact, width), BF, hbm),
+            wa_o=((layers, size, width), BF, hbm),
+            wf_o=((layers, 3, units, width), BF, hbm),
+            rows_o=((layers, *rows), BF, hbm),
+            q_o=((layers, seqs, *q_s), BF, hbm),
+            kv_o=((layers, seqs, *kv_s), BF, hbm),
+            att_o=((layers, seqs, 4, block, heads * LANES), BF, hbm),
+            lse_o=((layers, seqs, 4, 1, heads * block), F32, hbm),
+            middle_o=((layers, *own), F32, hbm),
+            frows_o=((layers, *rows), BF, hbm),
+            gu_o=((layers, seqs, 2, keys, units), BF, hbm),
+            stream_o=((layers - 1, *own), F32, hbm),
+            gain_o=((2 * layers, width), F32, hbm),
+            dy_o=(rows, BF, hbm),
+            qz=((layers, *raw), BF, hbm),
+            qc=((layers, *raw), BF, hbm),
+            kvl=((layers, *raw_k), BF, hbm),
+            fc=((layers, *raw_f), BF, hbm),
+        ),
+        dict(
+            stream=(own, F32),
+            middle=(own, F32),
+            rows=(rows, BF),
+            frows=(rows, BF),
+            q=((seqs, *q_s), BF),
+            kv=((layers, seqs, *kv_s), BF),
+            att=((seqs, 4, block, heads * LANES), BF),
+            lse=((seqs, 4, 1, heads * block), F32),
+            pt=(rows, BF),
+            rn=((seqs, 2, block, width), BF),
+            far=(own, BF),
+            rf=(own, BF),
+            gu=((2, keys, units), BF),
+            hid=((keys, units), BF),
+            k_s=((4, keys, LANES), BF),
+            vt_s=((4, LANES, keys), BF),
+            m_s=((1, heads * block), F32),
+            l_s=((1, heads * block), F32),
+            a_s=((LANES, heads * block), F32),
+            wa=((layers, size, width), BF),
+            wf=((layers, 3, units, width), BF),
+            st_q=(raw, BF),
+            st_k=(raw_k, BF),
+            st_f=(raw_f, BF),
+            own=((compact, part), BF),
+            tmp=((2 * KEY_VALUE_HEADS * D, part), BF),
+            gl=((2, 4, 8, 256), F32),
+            gain=((2 * layers, width), F32),
+        ),
+        sems=(130, 110),
+        vmem=63,
+    )
+
+
+class Rows(Net):
+    def gather_start(self, v, s, rows):
+        rows[s, 0] = v.astype(BF)
+        return [
+            self.send(rows.at[s, 0], rows.at[s, 2], CTX, 2),
+            self.send(rows.at[s, 0], rows.at[s, 1], CTX, 1),
+        ]
+
+    def gather_on(self, copies, s, rows):
+        copies[0].wait_recv()
+        copies.append(self.send(rows.at[s, 2], rows.at[s, 3], CTX, 1))
+
+    def gather_end(self, copies):
+        copies[1].wait_recv()
+        copies[2].wait_recv()
+        self.close(copies)
+
+    def reduce_start(self, s):
+        pt, rn = self.r.pt, self.r.rn
+        return [
+            self.send(pt.at[s, 3], rn.at[s, 1], CTX, 1),
+            self.send(pt.at[s, 1], rn.at[s, 0], CTX, 1),
+        ]
+
+    def reduce_on(self, copies, s):
+        r = self.r
+        copies[0].wait_recv()
+        r.far[s] = (r.pt[s, 2].astype(F32) + r.rn[s, 1].astype(F32)).astype(BF)
+        copies.append(self.send(r.far.at[s], r.rf.at[s], CTX, 2))
+
+    def reduce_end(self, copies, s):
+        r = self.r
+        copies[1].wait_recv()
+        copies[2].wait_recv()
+        total = r.pt[s, 0].astype(F32) + r.rn[s, 0].astype(F32) + r.rf[s].astype(F32)
+        self.close(copies)
+        return total
+
+    def norm_back(self, s, copies, gain, row):
+        r = self.r
+        local, v = self.reduce_end(copies, s), r.base[s]
+        scale = lax.rsqrt(jnp.mean(v * v, axis=-1, keepdims=True) + EPS)
+        u = v * scale
+        e = local * gain
+        r.grad[s] = r.grad[s] + scale * (e - u * jnp.mean(e * u, axis=-1, keepdims=True))
+        r.gs_o[row : row + 1] += jnp.sum(local * u, axis=0, keepdims=True)
+
+    def sum_tp(self, parts, lands):
+        outer = jnp.logical_not(self.inner)
+        one = self.make(parts[1], lands[0], TP, 1)
+        two = self.make(parts[2], lands[1], TP, 2)
+        hand = self.make(parts[3], lands[2], TP, 1)
+        mid = self.make(parts[3], lands[3], TP, 3)
+
+        @pl.when(outer)
+        def _():
+            hand.start()
+            two.start()
+
+        @pl.when(self.inner)
+        def _():
+            mid.start()
+            one.start()
+
+        return one, two, hand, mid
+
+    def sum_tp_on(self, copies, part, land):
+        one, two, hand, _ = copies
+        pl.when(jnp.logical_not(self.inner))(one.start)
+
+        @pl.when(self.inner)
+        def _():
+            hand.wait_recv()
+            part[...] = (part[...].astype(F32) + land[...].astype(F32)).astype(BF)
+            two.start()
+
+    def sum_tp_end(self, copies, own, lands):
+        one, two, hand, mid = copies
+        outer = jnp.logical_not(self.inner)
+        one.wait_recv()
+        two.wait_recv()
+
+        @pl.when(self.inner)
+        def _():
+            mid.wait_recv()
+            mid.wait_send()
+
+        @pl.when(outer)
+        def _():
+            lands[3][...] = jnp.zeros(lands[3].shape, lands[3].dtype)
+            hand.wait_send()
+
+        one.wait_send()
+        two.wait_send()
+        return (
+            own[...].astype(F32)
+            + lands[0][...].astype(F32)
+            + lands[1][...].astype(F32)
+            + lands[3][...].astype(F32)
+        )
+
+
+def ffn_back_body(rows_ref, w_ref, gu_ref, hgu, pt_o, waits, between=None):
+    block, width = rows_ref.shape[1], rows_ref.shape[2]
+    rows = rows_ref[...].reshape(4 * block, width)
+    for at, wide in chunks(w_ref.shape[1]):
+        own = slice(at, at + wide)
+        dh = nt(rows, w_ref[2, own])
+        g = gu_ref[0, :, own].astype(F32)
+        u = gu_ref[1, :, own].astype(F32)
+        s = 1.0 / (1.0 + jnp.exp(-g))
+        hgu[0, :, own] = (g * s * u).astype(BF)
+        hgu[1, :, own] = (dh * u * s * (1.0 + g * (1.0 - s))).astype(BF)
+        hgu[2, :, own] = (dh * g * s).astype(BF)
+    for copy in waits:
+        copy.wait()
+    if between:
+        between()
+    for at, wide in chunks(width):
+        own = slice(at, at + wide)
+        part = (nn(hgu[1], w_ref[0, :, own]) + nn(hgu[2], w_ref[1, :, own])).astype(BF)
+        for m in range(4):
+            pt_o[m, :, own] = part[m * block : (m + 1) * block]
+
+
+def weight_grad_body(lefts, rights, cols, out):
+    rows = lefts[0].shape[0]
+    for at, wide in chunks(lefts[0].shape[1]):
+        total = None
+        for left, right in zip(lefts, rights):
+            term = tn(left[:, at : at + wide], right[:, :, cols].reshape(rows, out.shape[1]))
+            total = term if total is None else total + term
+        out[at : at + wide] = total.astype(BF)
+
+
+def attn_back_body(
+    heads, c, t, prefix, rows_ref, w_ref, q_ref, kv_ref, att_ref, lse_ref, cos_ref, sin_ref, d_o, dkv_o,
+    do_s, de_s, dqt_s, dk_s, dv_s
+):
+    block = q_ref.shape[2]
+    keys = 4 * block
+    wide = heads * block
+    w_at = (heads + 2) * LANES
+    rows = rows_ref[...].reshape(keys, rows_ref.shape[2])
+    for at, span in chunks(wide):
+        do = nt(rows, w_ref[w_at + at : w_at + at + span]).astype(BF)
+        for m in range(4):
+            for j in range(span // LANES):
+                h = at // LANES + j
+                do_s[m, h * block : (h + 1) * block] = do[
+                    m * block : (m + 1) * block, j * LANES : (j + 1) * LANES
+                ]
+    mask = side_mask(c, heads, block)
+    for cq in range(4):
+        m = xor(c, cq)
+        for h in range(heads):
+            own = slice(h * block, (h + 1) * block)
+            prod = att_ref[m, :, h * LANES : (h + 1) * LANES].astype(F32) * do_s[m, own].astype(F32)
+            de_s[cq, :, own] = jnp.sum(jnp.transpose(prod), axis=0, keepdims=True)
+    dqt_s[...] = jnp.zeros_like(dqt_s)
+    q_at = lax.broadcasted_iota(jnp.int32, (1, wide), 1) % block + t * block
+    for ck in range(4):
+        mk = xor(c, ck)
+        k = jnp.concatenate([kv_ref[i, mk, :, :LANES] for i in range(4)], axis=0)
+        v = jnp.concatenate([kv_ref[i, mk, :, LANES:] for i in range(4)], axis=0)
+        kt = jnp.transpose(k.astype(F32)).astype(BF)
+        dk_s[...] = jnp.zeros_like(dk_s)
+        dv_s[...] = jnp.zeros_like(dv_s)
+        for cq in range(4):
+            if ck > cq and ck * keys >= PREFIX_MAX:
+                continue
+            m = xor(c, cq)
+            q_all = q_ref[m].reshape(wide, LANES)
+            for first, span in chunks(wide, 3 * LANES):
+                own = slice(first, first + span)
+                q, d_out = q_all[own], do_s[m, own]
+                p = jnp.exp(nt(k, q) - lse_ref[cq, :, own])
+                if ck >= cq:
+                    at = key_positions(t, block, ck * keys, keys)
+                    seen = (at <= q_at[:, own] + cq * keys) | (at < prefix)
+                    p = jnp.where(seen, p, 0.0)
+                ds = (p * (nt(v, d_out) - de_s[cq, :, own])).astype(BF)
+                dk_s[...] += nn(ds, q)
+                dv_s[...] += nn(p.astype(BF), d_out)
+                dqt_s[cq, :, own] += nn(kt, ds)
+        for i in range(4):
+            dkv_o[i, mk, :, :LANES] = dk_s[i * block : (i + 1) * block].astype(BF)
+            dkv_o[i, mk, :, LANES:] = dv_s[i * block : (i + 1) * block].astype(BF)
+    for cq in range(4):
+        m = xor(c, cq)
+        dq = jnp.transpose(dqt_s[cq]) * 0.125
+        turned = half_turn(dq)
+        cos, sin = cos_ref[m], sin_ref[m]
+        for h in range(heads):
+            own = slice(h * block, (h + 1) * block)
+            back = dq[own] * cos - turned[own] * sin
+            d_o[m, :, h * LANES : (h + 1) * LANES] = jnp.where(mask[own], back, 0.0).astype(BF)
+
+
+def proj_back_body(heads, total, w_ref, cos_ref, sin_ref, d_o, pt_o):
+    block = d_o.shape[1]
+    low = heads * LANES
+    for m in range(4):
+        dk = total[m, :, :LANES]
+        dk = dk * cos_ref[m] - half_turn(dk) * sin_ref[m]
+        d_o[m, :, low : low + LANES] = dk.astype(BF)
+        d_o[m, :, low + LANES :] = total[m, :, LANES:].astype(BF)
+    full = d_o[...].reshape(4 * block, low + 2 * LANES)
+    for at, span in chunks(w_ref.shape[1]):
+        own = slice(at, at + span)
+        part = nn(full, w_ref[: low + 2 * LANES, own]).astype(BF)
+        for m in range(4):
+            pt_o[m, :, own] = part[m * block : (m + 1) * block]
+
+
+def ffn_sums(net, cfg):
+    layers, seqs, block, width, heads, units, share = cfg
+    quarter = units // 4
+    r, c = net.r, net.c
+    parts = [[r.fs.at[i, m * quarter : (m + 1) * quarter] for m in range(4)] for i in range(3)]
+    lands = [[r.fz.at[k, i] for k in range(4)] for i in range(3)]
+    loads, sends = {}, {}
+
+    def start():
+        for i in (2, 0, 1):
+            loads[i] = [net.local(r.dwk.at[i], r.fs.at[i])]
+        loads[2].append(net.local(r.dwx, r.fx.at[2]))
+        for i in (0, 1):
+            sends[i] = net.send(r.dws.at[i], r.fx.at[i], DP)
+        yield
+
+    def one(i):
+        for copy in loads[i]:
+            copy.wait()
+        if i in sends:
+            sends[i].wait_recv()
+        for m in (3, 2, 1, 0):
+            own = slice(m * quarter, (m + 1) * quarter)
+            r.fs[i, own] = (r.fs[i, own].astype(F32) + r.fx[i, own].astype(F32)).astype(BF)
+        sums = net.sum_tp(parts[i], lands[i])
+        yield
+        net.sum_tp_on(sums, parts[i][2], lands[i][2])
+        yield
+        total = net.sum_tp_end(sums, parts[i][0], lands[i])
+        r.fo[i * quarter : (i + 1) * quarter] = total.astype(BF)
+        yield
+
+    def piece(i):
+        return r.ft.at[pl.ds(pl.multiple_of(i * share, 32), share)]
+
+    def end():
+        for at in range(0, 4 * share, LANES):
+            r.ft[at : at + LANES] = jnp.transpose(r.fo[:, at : at + LANES].astype(F32)).astype(BF)
+        out = [net.send(piece(xor(c, m)), r.fg.at[c], CTX, m) for m in (1, 2, 3)]
+        r.fg[c] = r.ft[pl.ds(pl.multiple_of(c * share, 32), share)]
+        yield
+        for copy in out:
+            copy.wait_recv()
+        for i, o in enumerate((r.g_o, r.u_o, r.d_o)):
+            own = slice(i * quarter, (i + 1) * quarter)
+            o[...] = jnp.concatenate([r.fg[k, :, own].astype(F32) for k in range(4)], axis=1)
+        net.close(out + list(sends.values()))
+        yield
+
+    return start(), one(2), one(0), one(1), end()
+
+
+def finish_attn(net, cfg, mine, other, waits):
+    layers, seqs, block, width, heads, units, share = cfg
+    r = net.r
+    c, t = net.c, net.t
+    wide = 2 * heads * D
+    for copy in waits:
+        copy.wait()
+    for at in range(0, 4 * share, LANES):
+        own = slice(at, at + LANES)
+        total = mine[:, own].astype(F32) + other[:, own].astype(F32)
+        r.at[own] = jnp.transpose(total).astype(BF)
+
+    def piece(i):
+        return r.at.at[pl.ds(pl.multiple_of(i * share, 32), share)]
+
+    out = [net.send(piece(xor(c, m)), r.ac.at[c], CTX, m) for m in (1, 2, 3)]
+    own = net.local(piece(c), r.ac.at[c])
+    yield
+    for copy in out:
+        copy.wait_recv()
+    own.wait()
+    net.close(out)
+    for m in range(4):
+        r.aq[m] = r.ac[xor(t, m), :, :wide]
+    parts = [r.aq.at[m] for m in range(4)]
+    lands = [r.az.at[k] for k in range(4)]
+    sums = net.sum_tp(parts, lands)
+    for first, at in ((0, wide), (KEY_VALUE_HEADS * D, wide + LANES)):
+        terms = []
+        for h in range(KEY_VALUE_HEADS):
+            total = None
+            for i in range(4):
+                j = h - i * heads // GROUP
+                if j in (0, 1):
+                    term = r.ac[i, :, at + j * D : at + (j + 1) * D].astype(F32)
+                    total = term if total is None else total + term
+            terms.append(total)
+        r.av[:, first : first + KEY_VALUE_HEADS * D] = jnp.concatenate(terms, axis=1)
+    r.asum[...] = r.av[...].astype(BF)
+    kv = [net.send(r.asum, r.al.at[m - 1], TP, m) for m in (1, 2, 3)]
+    yield
+    net.sum_tp_on(sums, parts[2], lands[2])
+    yield
+    r.qo_o[...] = net.sum_tp_end(sums, parts[0], lands)
+    for copy in kv:
+        copy.wait_recv()
+    r.kv_o[...] = r.av[...] + r.al[0].astype(F32) + r.al[1].astype(F32) + r.al[2].astype(F32)
+    net.close(kv)
+    yield
+
+
+def finish_gains(net):
+    r = net.r
+    r.gt[...] = r.gs_o[...]
+    for k, axis in enumerate((CTX, TP, DP)):
+        ms = (1, 2, 3) if axis != DP else (1,)
+        copies = [net.send(r.gt, r.gr.at[k, m - 1], axis, m) for m in ms]
+        yield
+        for copy in copies:
+            copy.wait_recv()
+        net.close(copies)
+        total = r.gt[...]
+        for m in ms:
+            total = total + r.gr[k, m - 1]
+        r.gt[...] = total
+    r.gs_o[...] = r.gt[...]
+    yield
+
+
+def ffn_back_kernel2(cfg, l, tail, r):
+    layers, seqs, block, width, heads, units, share = cfg
+    net = Rows(r)
+    part = 4 * share
+    keep = pl.ds(pl.multiple_of(net.x * part, LANES), part)
+    away = pl.ds(pl.multiple_of((1 - net.x) * part, LANES), part)
+    net.barrier()
+    first = [net.local(r.dy_i.at[0], r.dy.at[0]), net.local(r.wf_i.at[l, 2], r.wf.at[2])]
+    first.append(net.local(r.gu_i.at[l, 0], r.gu.at[0]))
+    second = [net.local(r.wf_i.at[l, i], r.wf.at[i]) for i in (0, 1)]
+    later = [net.local(r.dy_i.at[s], r.dy.at[s]) for s in range(1, seqs)]
+    later += [net.local(r.gu_i.at[l, s], r.gu.at[s]) for s in range(1, seqs)]
+    state = [net.local(r.grad_i, r.grad), net.local(r.base_i.at[l], r.base)]
+    state += [net.local(r.frows_i.at[l, s], r.frows.at[s]) for s in range(seqs)]
+    r.gs_o[...] = r.gs_i[...]
+    row = layers + l
+    gain = r.gain[row : row + 1]
+    saved, busy = [], {}
+
+    def sequence(s, waits, more):
+        rows, hgu, pt = r.dy.at[s], r.hgu.at[s], r.pt.at[s]
+        for copy in waits:
+            copy.wait()
+        ffn_back_body(rows, r.wf, r.gu.at[s], hgu, pt, more)
+        red = net.reduce_start(s)
+        yield
+        net.reduce_on(red, s)
+        yield
+        while state:
+            state.pop().wait()
+        net.norm_back(s, red, gain, row)
+        gather = net.gather_start(r.grad[s], s, r.dn)
+        saved.append(net.local(r.grad.at[s], r.grad_o.at[s]))
+        yield
+        net.gather_on(gather, s, r.dn)
+        yield
+        net.gather_end(gather)
+        saved.append(net.local(r.dn.at[s], r.dn_o.at[s]))
+        yield
+
+    def weights(i, to):
+        lefts = [r.hgu.at[s, i] for s in range(seqs)]
+        rights = [(r.frows if i else r.dy).at[s] for s in range(seqs)]
+        while state:
+            state.pop().wait()
+        if i:
+            if 0 in busy:
+                busy.pop(0).wait()
+            weight_grad_body(lefts, rights, away, r.ws.at[0])
+            busy[0] = net.local(r.ws.at[0], r.dws_o.at[to])
+        else:
+            weight_grad_body(lefts, rights, away, r.wx)
+            cross = net.send(r.wx, r.dwx_o, DP)
+        yield
+        if 1 in busy:
+            busy.pop(1).wait()
+        weight_grad_body(lefts, rights, keep, r.ws.at[1])
+        busy[1] = net.local(r.ws.at[1], r.dwk_o.at[to])
+        yield
+        if not i:
+            cross.wait()
+        yield
+
+    a, b = sequence(0, first, second), sequence(1, later, [])
+    w0, w1, w2 = weights(0, 2), weights(1, 0), weights(2, 1)
+    if tail:
+        loads = [net.local(r.dak, r.ak), net.local(r.dax, r.ax)]
+        fa = finish_attn(net, cfg, r.ak, r.ax, loads)
+        run((fa, a, b, a, w0, b, fa, w1, w1, w0, a, b, fa, w2, w2, a, fa, w0, b, a, b))
+    else:
+        run((a, b, a, w0, b, w1, w1, a, w2, w2, w0, b, a, a, b, w0, b))
+    for copy in saved + list(busy.values()):
+        copy.wait()
+
+
+def attn_back_kernel2(cfg, l, r):
+    layers, seqs, block, width, heads, units, share = cfg
+    net = Rows(r)
+    c, t = net.c, net.t
+    part = 4 * share
+    keep = pl.ds(pl.multiple_of(net.x * part, LANES), part)
+    away = pl.ds(pl.multiple_of((1 - net.x) * part, LANES), part)
+    net.barrier()
+    loads = []
+    for s in range(seqs):
+        loads.append([net.local(r.dy_i.at[s], r.dy.at[s])])
+        if s == 0:
+            loads[0].append(net.local(r.wa_i.at[l], r.wa))
+        for src, dst in ((r.q_i, r.q), (r.kv_i, r.kv), (r.att_i, r.att), (r.lse_i, r.lse)):
+            loads[s].append(net.local(src.at[l, s], dst.at[s]))
+    x, f0, f1, f2, g = ffn_sums(net, cfg)
+    run((x,))
+    state = [net.local(r.grad_i, r.grad), net.local(r.base_i.at[l - 1] if l else r.base_i, r.base)]
+    state += [net.local(r.rows_i.at[l, s], r.rows.at[s]) for s in range(seqs)]
+    r.gs_o[...] = r.gs_i[...]
+    gain = r.gain[l : l + 1]
+    saved = []
+
+    def sequence(s):
+        for copy in loads[s]:
+            copy.wait()
+        attn_back_body(
+            heads, c, t, r.prefix[s], r.dy.at[s], r.wa, r.q.at[s], r.kv.at[s], r.att.at[s],
+            r.lse.at[s], r.cos, r.sin, r.dqkv.at[s], r.dkv.at[s], r.do_s, r.de_s, r.dqt_s, r.dk_s, r.dv_s,
+        )
+        lands = [r.dz.at[k, s] for k in range(4)]
+        sums = net.sum_tp([r.dkv.at[s, m] for m in range(4)], lands)
+        yield
+        net.sum_tp_on(sums, r.dkv.at[s, 2], lands[2])
+        yield
+        r.dt[...] = net.sum_tp_end(sums, r.dkv.at[s, 0], lands)
+        proj_back_body(heads, r.dt, r.wa, r.cos, r.sin, r.dqkv.at[s], r.pt.at[s])
+        red = net.reduce_start(s)
+        yield
+        net.reduce_on(red, s)
+        yield
+        while state:
+            state.pop().wait()
+        net.norm_back(s, red, gain, l)
+        saved.append(net.local(r.grad.at[s], r.grad_o.at[s]))
+        if l:
+            gather = net.gather_start(r.grad[s], s, r.dn)
+        yield
+        if l:
+            net.gather_on(gather, s, r.dn)
+            yield
+            net.gather_end(gather)
+            saved.append(net.local(r.dn.at[s], r.dn_o.at[s]))
+            yield
+
+    def weights(lefts, rights, cols, out, at):
+        while state:
+            state.pop().wait()
+        low = lax.div(c * heads, GROUP)
+        lf = [lefts.at[s] for s in range(seqs)]
+        rg = [rights.at[s] for s in range(seqs)]
+        for a, wide in chunks(lf[0].shape[-1]):
+            total = None
+            for left, right in zip(lf, rg):
+                term = tn(
+                    left[:, :, a : a + wide].reshape(4 * block, wide),
+                    right[:, :, cols].reshape(4 * block, part),
+                )
+                total = term if total is None else total + term
+            r.ws[a : a + wide] = total.astype(BF)
+        for h in range(heads):
+            side = (lax.div(c * heads + h, GROUP) - low) * D
+            out[at + h * D : at + (h + 1) * D] = r.ws[pl.ds(pl.multiple_of(h * LANES + side, D), D)]
+        if at == 0:
+            out[2 * heads * D :] = r.ws[heads * LANES : (heads + 2) * LANES]
+
+    def out_weights():
+        weights(r.att, r.dy, away, r.wo.at[0], heads * D)
+        yield
+        weights(r.att, r.dy, keep, r.wo.at[1], heads * D)
+        yield
+
+    cross = []
+
+    def qkv_weights():
+        weights(r.dqkv, r.rows, away, r.wo.at[0], 0)
+        yield
+        cross.append(net.send(r.wo.at[0], r.dax_o if l else r.ax, DP))
+        yield
+        weights(r.dqkv, r.rows, keep, r.wo.at[1], 0)
+        if l:
+            saved.append(net.local(r.wo.at[1], r.dak_o))
+        yield
+
+    a, b, wo, wq = sequence(0), sequence(1), out_weights(), qkv_weights()
+    if l:
+        run((f0, a, f0, b, wo, a, b, a, f1, b, wo, f2, a, f0, wq, b, wq, f1, a, f2, b, b, f1, f2, g, b, wq, a, a, g))
+        cross[0].wait()
+    else:
+        gn = finish_gains(net)
+        run((f0, a, b, a, b, f1, wo, wo, a, b, wq, wq, b, f2, b, f0, a, f1, f2, a, gn, wq))
+        fa = finish_attn(net, cfg, r.wo.at[1], r.ax, cross)
+        run((fa, f0, gn, gn, gn, f2, f1, fa, g, fa, g, fa))
+    for copy in saved:
+        copy.wait()
+
+
+def backward_pass(cfg, tokens, prefix, cotangent, cos4, sin4, f):
+    layers, seqs, block, width, heads, units, share = cfg
+    keys, part = 4 * block, 4 * share
+    rows = (seqs, 4, block, width)
+    size = 2 * (heads + 1) * LANES
+    compact = 2 * heads * D + 2 * LANES
+    own = (seqs, block, width)
+    hbm, vm = pl.ANY, pltpu.VMEM
+    grads = ((8, width), F32, vm)
+    common = dict(
+        pt=(rows, BF), rn=((seqs, 2, block, width), BF), far=(own, BF), rf=(own, BF),
+        grad=(own, F32), base=(own, F32), dy=(rows, BF),
+    )
+    kvs = (share, 2 * KEY_VALUE_HEADS * D)
+    qos = (share, 2 * heads * D)
+    finish_out = dict(qo_o=(qos, F32, vm), kv_o=(kvs, F32, vm))
+    finish_scratch = dict(
+        ax=((compact, part), BF), at=((part, compact), BF),
+        ac=((4, share, compact), BF), aq=((4, *qos), BF), az=((4, *qos), BF),
+        av=(kvs, F32), asum=(kvs, BF), al=((3, *kvs), BF),
+    )
+    grad, dy = cotangent.astype(F32), f.dy_o
+    sums = jnp.zeros((8, width), F32)
+    units_of, heads_of = [None] * layers, [None] * layers
+    number = 1
+    d, finish_in = None, {}
+    for l in reversed(range(layers)):
+        tail = d is not None
+        more = (finish_in, finish_out, finish_scratch) if tail else ({}, {}, {})
+        c = launch(
+            functools.partial(ffn_back_kernel2, cfg, l, tail),
+            number,
+            dict(
+                dy_i=(dy, hbm), grad_i=(grad, hbm), base_i=(f.middle_o, hbm), gain=(f.gain_o, vm), wf_i=(f.wf_o, hbm),
+                frows_i=(f.frows_o, hbm), gu_i=(f.gu_o, hbm), gs_i=(sums, vm), **more[0],
+            ),
+            dict(
+                gs_o=grads, grad_o=(own, F32, hbm), dn_o=(rows, BF, hbm), dwk_o=((3, units, part), BF, hbm),
+                dws_o=((2, units, part), BF, hbm), dwx_o=((units, part), BF, hbm), **more[1],
+            ),
+            dict(
+                wf=((3, units, width), BF), frows=(rows, BF), gu=((seqs, 2, keys, units), BF), dn=(rows, BF),
+                hgu=((seqs, 3, keys, units), BF), ws=((2, units, part), BF), wx=((units, part), BF),
+                **(dict(ak=((compact, part), BF)) if tail else {}), **common, **more[2],
+            ),
+        )
+        if tail:
+            heads_of[l + 1] = c
+        base = f.stream_o if l else tokens.astype(F32)
+        d = launch(
+            functools.partial(attn_back_kernel2, cfg, l),
+            number + 1,
+            dict(
+                prefix=(prefix, pltpu.SMEM), dy_i=(c.dn_o, hbm), grad_i=(c.grad_o, hbm), base_i=(base, hbm),
+                gain=(f.gain_o, vm), wa_i=(f.wa_o, hbm), rows_i=(f.rows_o, hbm), q_i=(f.q_o, hbm), kv_i=(f.kv_o, hbm),
+                att_i=(f.att_o, hbm), lse_i=(f.lse_o, hbm), cos=(cos4, vm), sin=(sin4, vm), gs_i=(c.gs_o, vm),
+                dwk=(c.dwk_o, hbm), dws=(c.dws_o, hbm), dwx=(c.dwx_o, hbm),
+            ),
+            dict(
+                gs_o=grads, grad_o=(own, F32, hbm),
+                g_o=((share, units), F32, vm), u_o=((share, units), F32, vm), d_o=((share, units), F32, vm),
+                **(dict(dn_o=(rows, BF, hbm), dak_o=((compact, part), BF, hbm), dax_o=((compact, part), BF, hbm)) if l else finish_out),
+            ),
+            dict(
+                wa=((size, width), BF), q=((seqs, 4, heads, block, LANES), BF), kv=((seqs, 4, 4, block, 2 * LANES), BF),
+                att=((seqs, 4, block, heads * LANES), BF), lse=((seqs, 4, 1, heads * block), F32), rows=(rows, BF),
+                dqkv=((seqs, 4, block, (heads + 2) * LANES), BF), dkv=((seqs, 4, 4, block, 2 * LANES), BF),
+                do_s=((4, heads * block, LANES), BF), de_s=((4, 1, heads * block), F32),
+                dqt_s=((4, LANES, heads * block), F32), dk_s=((keys, LANES), F32), dv_s=((keys, LANES), F32),
+                dz=((4, seqs, 4, block, 2 * LANES), BF), dt=((4, block, 2 * LANES), F32),
+                ws=(((heads + 2) * LANES, part), BF), wo=((2, compact, part), BF),
+                fs=((3, units, part), BF), fx=((3, units, part), BF), fz=((4, 3, units // 4, part), BF),
+                fo=((3 * units // 4, part), BF), ft=((part, 3 * units // 4), BF), fg=((4, share, 3 * units // 4), BF),
+                **(dict(dn=(rows, BF)) if l else dict(gt=((8, width), F32), gr=((3, 3, 8, width), F32), **finish_scratch)), **common,
+            ),
+            vmem=63,
+        )
+        number += 2
+        units_of[l] = d
+        grad, dy, sums = d.grad_o, d.dn_o if l else None, d.gs_o
+        if l:
+            finish_in = dict(dak=(d.dak_o, hbm), dax=(d.dax_o, hbm))
+    heads_of[0] = d
+    return grad, units_of, heads_of
+
+
 def rms(v):
     r = lax.rsqrt(jnp.mean(v * v, axis=-1, keepdims=True) + EPS)
     return v * r, r
@@ -387,8 +1525,8 @@
 ):
     layers = w_query.shape[0]
     seqs, block, width = tokens.shape
-    dps = lax.axis_size("dp")
-    x, c, t = (lax.axis_index(a) for a in ("dp", "ctx", "tp"))
+    dps = lax.axis_size(DP)
+    x, c, t = (lax.axis_index(a) for a in (DP, CTX, TP))
     heads = w_query.shape[2] // D
     share = w_query.shape[1]
     part = 4 * share
@@ -410,16 +1548,16 @@
         jnp.stack([c, t, prefix[s]]).astype(jnp.int32) for s in range(seqs)
     ]
 
-    gains = jnp.stack([gain_attn, gain_ffn])
-    gains = lax.all_gather(gains, ("dp", "ctx"), axis=2, tiled=True).astype(F32)
+    shards = jnp.stack([gain_attn, gain_ffn])
+    gains = None if dps == 2 else lax.all_gather(shards, (DP, CTX), axis=2, tiled=True).astype(F32)
 
     def spread_dp(own):
         if dps == 2:
-            other = lax.ppermute(own, "dp", [(0, 1), (1, 0)])
+            other = lax.ppermute(own, DP, [(0, 1), (1, 0)])
             return jnp.concatenate(
                 [jnp.where(x == 0, own, other), jnp.where(x == 0, other, own)], axis=-1
             )
-        return lax.all_gather(own, "dp", axis=own.ndim - 1, tiled=True)
+        return lax.all_gather(own, DP, axis=own.ndim - 1, tiled=True)
 
     def attn_weights(l):
         qo = jnp.concatenate([w_query[l], w_out[l]], axis=1)
@@ -429,7 +1567,7 @@
         )
         got = ctx_exchange(to_ctx, True).reshape(part, 2 * heads * D).T
         kv = jnp.concatenate([key_weight[l], value_weight[l]], axis=1)
-        kv = by_ctx(jnp.stack([kv] + [flip(kv, "ctx", m) for m in (1, 2, 3)]))
+        kv = by_ctx(jnp.stack([kv] + [flip(kv, CTX, m) for m in (1, 2, 3)]))
         kv = kv.reshape(part, 2 * KEY_VALUE_HEADS * D).T
         k = lax.dynamic_slice_in_dim(kv, low * D, 2 * D, 0)
         v = lax.dynamic_slice_in_dim(kv, (KEY_VALUE_HEADS + low) * D, 2 * D, 0)
@@ -451,6 +1589,27 @@
         slots = [spread_dp(s) for s in tp_gather(own)]
         return jnp.concatenate(slots, axis=1)
 
+    if dps == 2:
+        cfg = (layers, seqs, block, width, heads, units, share)
+        small = jnp.pad(
+            shards.astype(F32).reshape(2 * layers, share), ((0, 8 - 2 * layers), (0, 256 - share))
+        )
+        qo = jnp.concatenate([w_query, w_out], axis=2)
+        kvw = jnp.concatenate([key_weight, value_weight], axis=2)
+        fp = jnp.concatenate([w_gate, w_up, w_down], axis=1)
+        fp = jnp.transpose(fp, (0, 2, 1)).reshape(layers, 4, quarter, 3 * share)
+        f = forward_pass(cfg, tokens, cotangent, prefix, small, qo, kvw, fp, cos, sin)
+        grad, fd, hd = backward_pass(cfg, tokens, prefix, cotangent, cos4, sin4, f)
+        wide = heads * D
+        kd = KEY_VALUE_HEADS * D
+        qo = jnp.stack([d.qo_o for d in hd])
+        kv = jnp.stack([d.kv_o for d in hd])
+        sums = lax.dynamic_slice_in_dim(hd[0].gs_o, (x * 4 + c) * share, share, 1)
+        return (
+            f.out_o, grad, qo[:, :, :wide], kv[:, :, :kd], kv[:, :, kd:], qo[:, :, wide:],
+            jnp.stack([d.g_o for d in fd]), jnp.stack([d.u_o for d in fd]), jnp.stack([d.d_o for d in fd]),
+            sums[:layers], sums[layers : 2 * layers],
+        )
     watt = [None] * layers
     wffn = [None] * layers
     for l in range(layers):
@@ -499,6 +1658,8 @@
             kept[l, s] = (stream[s], rows, q, kvs, att, lse, middle, frows, gate, up)
             stream[s] = middle + ctx_reduce(parts)
 
+    output = jnp.stack(stream).astype(BF)
+
     def norm_back(grad, local, v, gain):
         u, r = rms(v)
         e = local * gain
@@ -519,10 +1680,10 @@
         if dps == 2:
             mine = jnp.where(x == 0, halves[0], halves[1])
             other = jnp.where(x == 0, halves[1], halves[0])
-            got = lax.ppermute(other, "dp", [(0, 1), (1, 0)])
+            got = lax.ppermute(other, DP, [(0, 1), (1, 0)])
             return mine.astype(F32) + got.astype(F32)
         return lax.psum_scatter(
-            halves[0], "dp", scatter_dimension=halves[0].ndim - 1, tiled=True
+            halves[0], DP, scatter_dimension=halves[0].ndim - 1, tiled=True
         ).astype(F32)
 
     grads = {}
@@ -566,7 +1727,7 @@
         both = jnp.concatenate(both, axis=1)
         sent = both.astype(BF)
         for m in (1, 2, 3):
-            both = both + flip(sent, "tp", m).astype(F32)
+            both = both + flip(sent, TP, m).astype(F32)
         grads[l, "k"], grads[l, "v"] = (
             both[:, : KEY_VALUE_HEADS * D],
             both[:, KEY_VALUE_HEADS * D :],
@@ -616,10 +1777,10 @@
                 flops=2 * 5 * keys * long * heads * 256 * 0.7 + 2 * keys * heads * LANES * width,
                 exps=keys * long * heads,
             )
-            one = flip(dkv[1], "tp", 1)
-            handed = lax.ppermute(dkv[3], "tp", [(0, 1), (3, 2)])
-            mid = lax.ppermute(dkv[3], "tp", [(1, 2), (2, 1)])
-            two = flip((dkv[2].astype(F32) + handed.astype(F32)).astype(BF), "tp", 2)
+            one = flip(dkv[1], TP, 1)
+            handed = lax.ppermute(dkv[3], TP, [(0, 1), (3, 2)])
+            mid = lax.ppermute(dkv[3], TP, [(1, 2), (2, 1)])
+            two = flip((dkv[2].astype(F32) + handed.astype(F32)).astype(BF), TP, 2)
             dqkv, *parts = call(
                 functools.partial(proj_back_kernel, heads),
                 [dkv[0], one, two, mid, dq, watt[l], cos4, sin4],
@@ -638,14 +1799,14 @@
         )
 
     sums = jnp.stack([gain_sums[k, l] for k in range(2) for l in range(layers)])
-    sums = lax.psum(sums, ("dp", "ctx", "tp"))
+    sums = lax.psum(sums, (DP, CTX, TP))
     sums = lax.dynamic_slice_in_dim(sums, (x * 4 + c) * share, share, 1).reshape(2, layers, share)
 
     def stacked(name):
         return jnp.stack([grads[l, name] for l in range(layers)])
 
     return (
-        jnp.stack(stream).astype(BF),
+        output,
         jnp.stack(grad),
         stacked("q"),
         stacked("k"),
@@ -660,11 +1821,11 @@
 
 
 def solution(mesh):
-    rows = P("dp", ("ctx", "tp"), None)
-    sharded = P(None, ("dp", "ctx"), "tp")
-    heads = P(None, ("dp", "ctx"), None)
-    gains = P(None, ("dp", "ctx"))
-    in_specs = (rows, P("dp"), sharded, heads, heads, sharded, sharded, sharded, sharded, gains, gains, rows)
+    rows = P(DP, (CTX, TP), None)
+    sharded = P(None, (DP, CTX), TP)
+    heads = P(None, (DP, CTX), None)
+    gains = P(None, (DP, CTX))
+    in_specs = (rows, P(DP), sharded, heads, heads, sharded, sharded, sharded, sharded, gains, gains, rows)
     out_specs = (rows, rows, sharded, heads, heads, sharded, sharded, sharded, sharded, gains, gains)
     return jax.shard_map(
         per_device, mesh=mesh, in_specs=in_specs, out_specs=out_specs, check_vma=False

time: 1340 us -> 701 us (0.52)
  waiting for transfers between devices: 457 us -> 0 us
  Pallas kernels: 339 us -> 663 us
  starting transfers between devices: 210 us -> 0 us
  other arithmetic: 141 us -> 17.4 us
  local copies, waits for them, and re-layouts: 106 us -> 9.59 us
  blocking collectives: 75.4 us -> 0 us
    ppermute x214 -> x0, waiting for transfers between devices: 457 us -> none  [the longest x164 289 us: flip(): return lax.ppermute(x, axis, [(i, i ^ m) for i in range(4)])]
    pallas_call x40 -> x5, Pallas kernels: 339 us -> 663 us  [launch(): pl.pallas_call(body, out_shape=[jax.ShapeDtypeStruct(v[0], v[1]) for v in...]
    ppermute x214 -> x0, starting transfers between devices: 210 us -> none  [the longest x164 141 us: flip(): return lax.ppermute(x, axis, [(i, i ^ m) for i in range(4)])]
    psum x1 -> x0, blocking collectives: 65.3 us -> none  [per_device(): sums = lax.psum(sums, ('dp', 'ctx', 'tp'))]
    slice x30 -> x1, local copies, waits for them, and re-layouts: 51.3 us -> 1.44 us  [per_device(): sums[layers:2 * layers]]
    select_n x24 -> x0, other arithmetic: 34.4 us -> none  [the longest x8 17.3 us: collect_dp(): other = jnp.where(x == 0, halves[1], halves[0])]
    another operation x52 -> x6, other arithmetic: 40 us -> 7.42 us  [the longest x1 2.28 us: per_device(): qo = jnp.stack([d.qo_o for d in hd])]
    concatenate x12 -> x1, other arithmetic: 28.5 us -> 2.45 us  [per_device(): qo = jnp.concatenate([w_query, w_out], axis=2)]
  transfers between devices with their start and end apart: 214 -> 0, of which waited for: 71 -> 0; matrix products, arithmetic and copies ran while one was open for 17% -> 0% of each run, Pallas kernels for 25% -> 0%
where the time goes in v2:
time: 701 us; the launch traced here: 691 us
  Pallas kernels  663 us (95%)
  other arithmetic  17.4 us (2%)
  local copies, waits for them, and re-layouts  9.59 us (1%)
    pallas_call x5, Pallas kernels, launch(): pl.pallas_call(body, out_shape=[jax.ShapeDtypeStruct(v[0], v[1]) for v in...  663 us

profile of v2, /device:TPU:0, one launch (start us, length us, event | category | flops | bytes accessed | tf_op | source)
XLA Modules:
  0.0 690.9 jit_solution(4730607955256654962)
XLA Ops:
  0.7 0.8 pad_maximum_fusion.9
  2.1 2.4 pad_maximum_fusion.5
  4.7 2.4 copy.29
  7.8 1.0 fusion.3
  9.7 0.8 copy.32.refs_7_
  10.5 1.0 pad_maximum_fusion.7.refs_8_
  11.5 286.3 %shard_map.203 = (bf16[2,128,1280]{2,1,0:T(8,128)(2,1)}, bf16[2,896,1280]{2,1,0:T(8,128)(2,1)}, bf16[2,1536,1280]{2,1,0:T(8,128)(2,1)}, bf16[2,3,896,1280]{3,2,1...) custom-call(s32[2]{0:T(128)} %refs_0_.5, ...), custom_call_target="tpu_custom_call" | custom-call | flops 99999997952 | bytes 100000000 | tf_op jit(solution)/shard_map/pallas_call | solution.py:823
  297.8 1.1 convert_element_type.37.refs_1_
  299.6 53.3 %shard_map.204 = (f32[8,1280]{1,0:T(8,128)}, f32[2,128,1280]{2,1,0:T(8,128)}, bf16[2,4,128,1280]{3,2,1,0:T(8,128)(2,1)}, bf16[3,896,640]{2,1,0:T(8,128)(2,1)}, b...) custom-call(bf16[2,4,128,1280]{3,2,1,0:T(8,128)(2,1)} %get-tuple-element.55.refs_0_, ...), custom_call_target="tpu_custom_call" | custom-call | flops 99999997952 | bytes 100000000 | tf_op jit(solution)/shard_map/pallas_call | solution.py:823
  353.0 0.8 copy.33.refs_11_
  353.8 0.9 fusion.2
  354.8 1.0 pad_maximum_fusion.8.refs_12_
  355.7 118.5 %shard_map.205 = (f32[8,1280]{1,0:T(8,128)}, f32[2,128,1280]{2,1,0:T(8,128)}, f32[160,896]{1,0:T(8,128)}, f32[160,896]{1,0:T(8,128)}, f32[160,896]{1,0:T(8,128)}...) custom-call(s32[2]{0:T(128)} %refs_0_.5, ...), custom_call_target="tpu_custom_call" | custom-call | flops 99999997952 | bytes 100000000 | tf_op jit(solution)/shard_map/pallas_call | solution.py:823
  474.2 63.4 %shard_map.206 = (f32[8,1280]{1,0:T(8,128)}, f32[2,128,1280]{2,1,0:T(8,128)}, bf16[2,4,128,1280]{3,2,1,0:T(8,128)(2,1)}, bf16[3,896,640]{2,1,0:T(8,128)(2,1)}, b...) custom-call(bf16[2,4,128,1280]{3,2,1,0:T(8,128)(2,1)} %get-tuple-element.74.ref, ...), custom_call_target="tpu_custom_call" | custom-call | flops 99999997952 | bytes 100000000 | tf_op jit(solution)/shard_map/pallas_call | solution.py:823
  537.6 1.1 convert_element_type.38.refs_3_
  538.8 141.4 %shard_map.207 = (f32[8,1280]{1,0:T(8,128)}, f32[2,128,1280]{2,1,0:T(8,128)}, f32[160,896]{1,0:T(8,128)}, f32[160,896]{1,0:T(8,128)}, f32[160,896]{1,0:T(8,128)}...) custom-call(s32[2]{0:T(128)} %refs_0_.5, bf16[2,4,128,1280]{3,2,1,0:T(8,128)(2,1)} %get-tuple-element.79.refs_1_, ...), custom_call_target="tpu_custom_call" | custom-call | flops 99999997952 | bytes 100000000 | tf_op jit(solution)/shard_map/pallas_call | solution.py:823
  680.2 2.3 pad_maximum_fusion.3
  682.5 1.1 pad_maximum_fusion.4
  683.6 1.1 pad_maximum_fusion
  684.7 1.1 pad_maximum_fusion.1
  686.3 1.1 pad_maximum_fusion.2
  687.4 1.4 fusion.5
  688.9 0.8 copy.37
  689.7 1.1 copy.38
  (52 shorter events, 3.6 us)
Async XLA Ops:
  0.6 3.9 copy-start.6
  0.7 3.9 copy-start.7
  0.7 3.9 copy-start.8
  7.1 1.7 copy-start.19
  8.9 0.7 copy-start
  11.5 286.3 %copy-start.4 = (bf16[2,128,1280]{2,1,0:T(8,128)(2,1)S(1)}, bf16[2,128,1280]{2,1,0:T(8,128)(2,1)}, u32[]{:S(2)}) copy-start(bf16[2,128,1280]{2,1,0:T(8,128)(2,1)} %refs_2_.1) | copy-start | bytes 1966084
  299.6 53.3 %copy-start.1 = (f32[512,4,32]{0,2,1:T(8,128)S(1)}, f32[512,4,32]{0,2,1:T(8,128)}, u32[]{:S(2)}) copy-start(f32[512,4,32]{0,2,1:T(8,128)} %copy-done) | copy-start | bytes 786436
  299.6 54.3 %copy-start.18 = (f32[4,128]{1,0:T(4,128)S(1)}, f32[4,128]{1,0:T(4,128)}, u32[]{:S(2)}) copy-start(f32[4,128]{1,0:T(4,128)} %get-tuple-element.108) | copy-start | bytes 6148
  299.6 54.3 %copy-start.20 = (f32[32]{0:T(128)S(1)}, f32[32]{0:T(128)}, u32[]{:S(2)}) copy-start(f32[32]{0:T(128)} %copy-done.19) | copy-start | bytes 388
  474.2 63.4 %copy-start.5 = (bf16[2,128,1280]{2,1,0:T(8,128)(2,1)S(1)}, bf16[2,128,1280]{2,1,0:T(8,128)(2,1)}, u32[]{:S(2)}) copy-start(bf16[2,128,1280]{2,1,0:T(8,128)(2,1)} %refs_1_.1) | copy-start | bytes 1966084
  538.8 141.4 %copy-start.16 = (f32[160,640]{1,0:T(8,128)S(1)}, f32[160,640]{1,0:T(8,128)}, u32[]{:S(2)}) copy-start(f32[160,640]{1,0:T(8,128)} %get-tuple-element.87) | copy-start | bytes 1228804
  680.2 2.3 copy-start.15
  680.2 2.3 copy-start.17
  680.2 3.4 copy-start.11
  680.2 3.4 copy-start.14
  682.5 2.2 copy-start.10
  682.5 2.2 copy-start.13
  684.7 1.2 copy-start.9
  684.7 1.6 copy-start.12
  685.8 3.1 copy-start.3
  686.3 3.4 copy-start.2

commit v3 on v2

--- a/solution.py
+++ b/solution.py
@@ -622,8 +622,12 @@
             gather_on(gather, s, rows)
             yield
             gather_end(gather)
-            qkv_body(heads, rows.at[s], r.wa.at[l], r.cos, r.sin, q.at[s], kv.at[l, s, 0])
-            tp = net.spread_tp(kv.at[l, s, 0], [kv.at[l, s, i] for i in range(4)])
+            tp = []
+            qkv_body(
+                heads, rows.at[s], r.wa.at[l], r.cos, r.sin, q.at[s], kv.at[l, s, 0],
+                lambda: tp.append(net.spread_tp(kv.at[l, s, 0], [kv.at[l, s, i] for i in range(4)])),
+            )
+            tp = tp[0]
             outs = [net.local(rows.at[s], r.rows_o.at[l, s]), net.local(q.at[s], r.q_o.at[l, s])] + carry
             yield
             net.spread_tp_on(tp)
@@ -718,14 +722,11 @@
         copy.wait()
 
 
-def qkv_body(heads, rows_ref, w_ref, cos_ref, sin_ref, q_o, kv_o):
+def qkv_body(heads, rows_ref, w_ref, cos_ref, sin_ref, q_o, kv_o, between=None):
     block, width = rows_ref.shape[1], rows_ref.shape[2]
     rows = rows_ref[...].reshape(4 * block, width)
     cos, sin = cos_ref[...], sin_ref[...]
-    at = 0
-    total = (heads + 2) * LANES
-    while at < total:
-        wide = min(3 * LANES, total - at)
+    for at, wide in [(heads * LANES, 2 * LANES)] + chunks(heads * LANES):
         lin = nt(rows, w_ref[at : at + wide])
         for j in range(wide // LANES):
             slot = at // LANES + j
@@ -741,7 +742,8 @@
                 lo = (slot - heads) * LANES
                 for m in range(4):
                     kv_o[m, :, lo : lo + LANES] = v[m * block : (m + 1) * block]
-        at += wide
+        if at == heads * LANES and between:
+            between()
 
 
 def attn_body(heads, c, t, prefix, q_ref, kv_ref, w_ref, att_o, lse_o, pt_o, k_s, vt_s, m_s, l_s, a_s):
@@ -1125,56 +1127,65 @@
             pt_o[m, :, own] = part[m * block : (m + 1) * block]
 
 
-def ffn_sums(net, cfg):
+def ffn_sums(net, cfg, where):
     layers, seqs, block, width, heads, units, share = cfg
     quarter = units // 4
     r, c = net.r, net.c
-    parts = [[r.fs.at[i, m * quarter : (m + 1) * quarter] for m in range(4)] for i in range(3)]
-    lands = [[r.fz.at[k, i] for k in range(4)] for i in range(3)]
     loads, sends = {}, {}
 
     def start():
-        for i in (2, 0, 1):
-            loads[i] = [net.local(r.dwk.at[i], r.fs.at[i])]
-        loads[2].append(net.local(r.dwx, r.fx.at[2]))
-        for i in (0, 1):
-            sends[i] = net.send(r.dws.at[i], r.fx.at[i], DP)
+        if where == 2:
+            loads[1] = [net.local(r.fs_i, r.fs.at[0])]
+        else:
+            for i in (2, 0, 1):
+                loads[i] = [net.local(r.dwk.at[i], r.fs.at[i])]
+            loads[2].append(net.local(r.dwx, r.fx.at[2]))
+            for i in (0, 1):
+                sends[i] = net.send(r.dws.at[i], r.fx.at[i], DP)
         yield
 
     def one(i):
+        at = 0 if where == 2 else i
+        parts = [r.fs.at[at, m * quarter : (m + 1) * quarter] for m in range(4)]
         for copy in loads[i]:
             copy.wait()
         if i in sends:
             sends[i].wait_recv()
-        for m in (3, 2, 1, 0):
-            own = slice(m * quarter, (m + 1) * quarter)
-            r.fs[i, own] = (r.fs[i, own].astype(F32) + r.fx[i, own].astype(F32)).astype(BF)
-        sums = net.sum_tp(parts[i], lands[i])
-        yield
-        net.sum_tp_on(sums, parts[i][2], lands[i][2])
-        yield
-        total = net.sum_tp_end(sums, parts[i][0], lands[i])
-        r.fo[i * quarter : (i + 1) * quarter] = total.astype(BF)
-        yield
-
-    def piece(i):
-        return r.ft.at[pl.ds(pl.multiple_of(i * share, 32), share)]
-
-    def end():
-        for at in range(0, 4 * share, LANES):
-            r.ft[at : at + LANES] = jnp.transpose(r.fo[:, at : at + LANES].astype(F32)).astype(BF)
-        out = [net.send(piece(xor(c, m)), r.fg.at[c], CTX, m) for m in (1, 2, 3)]
-        r.fg[c] = r.ft[pl.ds(pl.multiple_of(c * share, 32), share)]
+        if where != 2:
+            for m in (3, 2, 1, 0):
+                own = slice(m * quarter, (m + 1) * quarter)
+                r.fs[i, own] = (r.fs[i, own].astype(F32) + r.fx[i, own].astype(F32)).astype(BF)
+        if where == 1 and i == 1:
+            out = net.local(r.fs.at[i], r.fs_o)
+            yield
+            out.wait()
+            net.close(list(sends.values()))
+            yield
+        lands = [r.fz.at[k, at] for k in range(4)]
+        sums = net.sum_tp(parts, lands)
+        yield
+        net.sum_tp_on(sums, parts[2], lands[2])
+        yield
+        r.fo[...] = net.sum_tp_end(sums, parts[0], lands).astype(BF)
+        ft, fg = r.ft.at[at], r.fg.at[at]
+        for first in range(0, 4 * share, LANES):
+            ft[first : first + LANES] = jnp.transpose(r.fo[:, first : first + LANES].astype(F32)).astype(BF)
+        out = [net.send(ft.at[piece(xor(c, m))], fg.at[c], CTX, m) for m in (1, 2, 3)]
+        fg[c] = ft[piece(c)]
         yield
         for copy in out:
             copy.wait_recv()
-        for i, o in enumerate((r.g_o, r.u_o, r.d_o)):
-            own = slice(i * quarter, (i + 1) * quarter)
-            o[...] = jnp.concatenate([r.fg[k, :, own].astype(F32) for k in range(4)], axis=1)
-        net.close(out + list(sends.values()))
-        yield
-
-    return start(), one(2), one(0), one(1), end()
+        to = r.u_o if i == 1 else r.d_o if i else r.g_o
+        to[...] = jnp.concatenate([fg[k].astype(F32) for k in range(4)], axis=1)
+        net.close(out)
+        if where == 0 and i in sends:
+            net.close([sends[i]])
+        yield
+
+    def piece(i):
+        return pl.ds(pl.multiple_of(i * share, 32), share)
+
+    return start(), one(2), one(0), one(1)
 
 
 def finish_attn(net, cfg, mine, other, waits):
@@ -1215,16 +1226,45 @@
                     total = term if total is None else total + term
             terms.append(total)
         r.av[:, first : first + KEY_VALUE_HEADS * D] = jnp.concatenate(terms, axis=1)
-    r.asum[...] = r.av[...].astype(BF)
-    kv = [net.send(r.asum, r.al.at[m - 1], TP, m) for m in (1, 2, 3)]
+    outer = jnp.logical_not(net.inner)
+    r.asum[0] = r.av[...].astype(BF)
+    ends = net.make(r.asum.at[0], r.al.at[0], TP, 1)
+    swap = net.make(r.asum.at[1], r.al.at[1], TP, 3)
+    back = net.make(r.asum.at[2], r.al.at[2], TP, 1)
+    pl.when(outer)(ends.start)
+    yield
+
+    @pl.when(net.inner)
+    def _():
+        ends.wait_recv()
+        r.asum[1] = (r.av[...] + r.al[0].astype(F32)).astype(BF)
+        swap.start()
+
     yield
     net.sum_tp_on(sums, parts[2], lands[2])
     yield
+
+    @pl.when(net.inner)
+    def _():
+        swap.wait_recv()
+        r.asum[2] = (r.asum[1].astype(F32) + r.al[1].astype(F32)).astype(BF)
+        back.start()
+
+    yield
     r.qo_o[...] = net.sum_tp_end(sums, parts[0], lands)
-    for copy in kv:
-        copy.wait_recv()
-    r.kv_o[...] = r.av[...] + r.al[0].astype(F32) + r.al[1].astype(F32) + r.al[2].astype(F32)
-    net.close(kv)
+
+    @pl.when(net.inner)
+    def _():
+        swap.wait_send()
+        back.wait_send()
+        r.kv_o[...] = r.asum[2].astype(F32)
+
+    @pl.when(outer)
+    def _():
+        ends.wait_send()
+        back.wait_recv()
+        r.kv_o[...] = r.al[2].astype(F32)
+
     yield
 
 
@@ -1253,6 +1293,7 @@
     keep = pl.ds(pl.multiple_of(net.x * part, LANES), part)
     away = pl.ds(pl.multiple_of((1 - net.x) * part, LANES), part)
     net.barrier()
+    loads = [net.local(r.dak, r.ak), net.local(r.dax, r.ax)] if tail else []
     first = [net.local(r.dy_i.at[0], r.dy.at[0]), net.local(r.wf_i.at[l, 2], r.wf.at[2])]
     first.append(net.local(r.gu_i.at[l, 0], r.gu.at[0]))
     second = [net.local(r.wf_i.at[l, i], r.wf.at[i]) for i in (0, 1)]
@@ -1312,11 +1353,19 @@
     a, b = sequence(0, first, second), sequence(1, later, [])
     w0, w1, w2 = weights(0, 2), weights(1, 0), weights(2, 1)
     if tail:
-        loads = [net.local(r.dak, r.ak), net.local(r.dax, r.ax)]
         fa = finish_attn(net, cfg, r.ak, r.ax, loads)
-        run((fa, a, b, a, w0, b, fa, w1, w1, w0, a, b, fa, w2, w2, a, fa, w0, b, a, b))
+        x, _, _, f2 = ffn_sums(net, cfg, 2)
+        order = (
+            x,
+            fa, a, f2, a, b, w0, fa, b, w0, w1, a, w1, f2, fa, w2, fa, w2, b,
+            fa, a, f2, a, w1, b, w0, fa, w2, f2, b,
+        )
     else:
-        run((a, b, a, w0, b, w1, w1, a, w2, w2, w0, b, a, a, b, w0, b))
+        order = (
+            a, b, a, w0, b, a, w1, b, w0, w2, w2, a, a, w2, w1, w1, b, w0,
+            b,
+        )
+    run(order)
     for copy in saved + list(busy.values()):
         copy.wait()
 
@@ -1336,7 +1385,7 @@
             loads[0].append(net.local(r.wa_i.at[l], r.wa))
         for src, dst in ((r.q_i, r.q), (r.kv_i, r.kv), (r.att_i, r.att), (r.lse_i, r.lse)):
             loads[s].append(net.local(src.at[l, s], dst.at[s]))
-    x, f0, f1, f2, g = ffn_sums(net, cfg)
+    x, f0, f1, f2 = ffn_sums(net, cfg, 1 if l else 0)
     run((x,))
     state = [net.local(r.grad_i, r.grad), net.local(r.base_i.at[l - 1] if l else r.base_i, r.base)]
     state += [net.local(r.rows_i.at[l, s], r.rows.at[s]) for s in range(seqs)]
@@ -1411,19 +1460,25 @@
         cross.append(net.send(r.wo.at[0], r.dax_o if l else r.ax, DP))
         yield
         weights(r.dqkv, r.rows, keep, r.wo.at[1], 0)
-        if l:
-            saved.append(net.local(r.wo.at[1], r.dak_o))
         yield
 
     a, b, wo, wq = sequence(0), sequence(1), out_weights(), qkv_weights()
     if l:
-        run((f0, a, f0, b, wo, a, b, a, f1, b, wo, f2, a, f0, wq, b, wq, f1, a, f2, b, b, f1, f2, g, b, wq, a, a, g))
+        order = (
+            f0, a, b, a, b, a, a, f1, b, wo, wq, b, a, f0, wq, wq, f1, b,
+            f1, b, f0, wo, a, b, f1, f2, f2, wq, a, f0,
+        )
+    else:
+        gn, fa = finish_gains(net), finish_attn(net, cfg, r.wo.at[1], r.ax, cross)
+        order = (
+            f0, a, b, a, wo, b, a, f1, b, wq, wq, wo, wq, f0, f2, b, b, f1,
+            a, a, fa, f2, f2, gn, f0, fa, f1, fa, f0, gn, fa, fa, f2, gn, f1, gn,
+            fa,
+        )
+    run(order)
+    if l:
+        saved.append(net.local(r.wo.at[1], r.dak_o))
         cross[0].wait()
-    else:
-        gn = finish_gains(net)
-        run((f0, a, b, a, b, f1, wo, wo, a, b, wq, wq, b, f2, b, f0, a, f1, f2, a, gn, wq))
-        fa = finish_attn(net, cfg, r.wo.at[1], r.ax, cross)
-        run((fa, f0, gn, gn, gn, f2, f1, fa, g, fa, g, fa))
     for copy in saved:
         copy.wait()
 
@@ -1443,15 +1498,22 @@
     )
     kvs = (share, 2 * KEY_VALUE_HEADS * D)
     qos = (share, 2 * heads * D)
-    finish_out = dict(qo_o=(qos, F32, vm), kv_o=(kvs, F32, vm))
+    one = (share, units)
+    finish_out = dict(
+        qo_o=(qos, F32, vm), kv_o=(kvs, F32, vm), u_o=(one, F32, vm)
+    )
     finish_scratch = dict(
         ax=((compact, part), BF), at=((part, compact), BF),
         ac=((4, share, compact), BF), aq=((4, *qos), BF), az=((4, *qos), BF),
-        av=(kvs, F32), asum=(kvs, BF), al=((3, *kvs), BF),
+        av=(kvs, F32), asum=((3, *kvs), BF), al=((3, *kvs), BF),
+    )
+    mid_out = dict(
+        dn_o=(rows, BF, hbm), dak_o=((compact, part), BF, hbm), dax_o=((compact, part), BF, hbm),
+        fs_o=((units, part), BF, hbm), g_o=(one, F32, vm), d_o=(one, F32, vm),
     )
     grad, dy = cotangent.astype(F32), f.dy_o
     sums = jnp.zeros((8, width), F32)
-    units_of, heads_of = [None] * layers, [None] * layers
+    done, units_of = [None] * layers, [None] * layers
     number = 1
     d, finish_in = None, {}
     for l in reversed(range(layers)):
@@ -1471,11 +1533,13 @@
             dict(
                 wf=((3, units, width), BF), frows=(rows, BF), gu=((seqs, 2, keys, units), BF), dn=(rows, BF),
                 hgu=((seqs, 3, keys, units), BF), ws=((2, units, part), BF), wx=((units, part), BF),
-                **(dict(ak=((compact, part), BF)) if tail else {}), **common, **more[2],
+                **(dict(ak=((compact, part), BF), fs=((1, units, part), BF), fz=((4, 1, units // 4, part), BF),
+                fo=((units // 4, part), BF), ft=((1, part, units // 4), BF), fg=((1, 4, share, units // 4), BF)) if tail else {}), **common, **more[2],
             ),
         )
         if tail:
-            heads_of[l + 1] = c
+            done[l + 1] = c
+            units_of[l + 1] = d
         base = f.stream_o if l else tokens.astype(F32)
         d = launch(
             functools.partial(attn_back_kernel2, cfg, l),
@@ -1488,8 +1552,7 @@
             ),
             dict(
                 gs_o=grads, grad_o=(own, F32, hbm),
-                g_o=((share, units), F32, vm), u_o=((share, units), F32, vm), d_o=((share, units), F32, vm),
-                **(dict(dn_o=(rows, BF, hbm), dak_o=((compact, part), BF, hbm), dax_o=((compact, part), BF, hbm)) if l else finish_out),
+                **(mid_out if l else dict(g_o=(one, F32, vm), d_o=(one, F32, vm), **finish_out)),
             ),
             dict(
                 wa=((size, width), BF), q=((seqs, 4, heads, block, LANES), BF), kv=((seqs, 4, 4, block, 2 * LANES), BF),
@@ -1500,18 +1563,17 @@
                 dz=((4, seqs, 4, block, 2 * LANES), BF), dt=((4, block, 2 * LANES), F32),
                 ws=(((heads + 2) * LANES, part), BF), wo=((2, compact, part), BF),
                 fs=((3, units, part), BF), fx=((3, units, part), BF), fz=((4, 3, units // 4, part), BF),
-                fo=((3 * units // 4, part), BF), ft=((part, 3 * units // 4), BF), fg=((4, share, 3 * units // 4), BF),
+                fo=((units // 4, part), BF), ft=((3, part, units // 4), BF), fg=((3, 4, share, units // 4), BF),
                 **(dict(dn=(rows, BF)) if l else dict(gt=((8, width), F32), gr=((3, 3, 8, width), F32), **finish_scratch)), **common,
             ),
             vmem=63,
         )
         number += 2
-        units_of[l] = d
         grad, dy, sums = d.grad_o, d.dn_o if l else None, d.gs_o
         if l:
-            finish_in = dict(dak=(d.dak_o, hbm), dax=(d.dax_o, hbm))
-    heads_of[0] = d
-    return grad, units_of, heads_of
+            finish_in = dict(dak=(d.dak_o, hbm), dax=(d.dax_o, hbm), fs_i=(d.fs_o, hbm))
+    done[0] = units_of[0] = d
+    return grad, done, units_of
 
 
 def rms(v):
@@ -1599,15 +1661,15 @@
         fp = jnp.concatenate([w_gate, w_up, w_down], axis=1)
         fp = jnp.transpose(fp, (0, 2, 1)).reshape(layers, 4, quarter, 3 * share)
         f = forward_pass(cfg, tokens, cotangent, prefix, small, qo, kvw, fp, cos, sin)
-        grad, fd, hd = backward_pass(cfg, tokens, prefix, cotangent, cos4, sin4, f)
+        grad, done, fd = backward_pass(cfg, tokens, prefix, cotangent, cos4, sin4, f)
         wide = heads * D
         kd = KEY_VALUE_HEADS * D
-        qo = jnp.stack([d.qo_o for d in hd])
-        kv = jnp.stack([d.kv_o for d in hd])
-        sums = lax.dynamic_slice_in_dim(hd[0].gs_o, (x * 4 + c) * share, share, 1)
+        qo = jnp.stack([d.qo_o for d in done])
+        kv = jnp.stack([d.kv_o for d in done])
+        sums = lax.dynamic_slice_in_dim(done[0].gs_o, (x * 4 + c) * share, share, 1)
         return (
             f.out_o, grad, qo[:, :, :wide], kv[:, :, :kd], kv[:, :, kd:], qo[:, :, wide:],
-            jnp.stack([d.g_o for d in fd]), jnp.stack([d.u_o for d in fd]), jnp.stack([d.d_o for d in fd]),
+            jnp.stack([d.g_o for d in fd]), jnp.stack([d.u_o for d in done]), jnp.stack([d.d_o for d in fd]),
             sums[:layers], sums[layers : 2 * layers],
         )
     watt = [None] * layers

time: 701 us -> 676 us (0.964)
  Pallas kernels: 663 us -> 638 us
    pallas_call x5, Pallas kernels: 663 us -> 638 us  [launch(): pl.pallas_call(body, out_shape=[jax.ShapeDtypeStruct(v[0], v[1]) for v in...]
where the time goes in v3:
time: 676 us; the launch traced here: 666 us
  Pallas kernels  638 us (94%)
  other arithmetic  17.4 us (3%)
  local copies, waits for them, and re-layouts  9.61 us (1%)
    pallas_call x5, Pallas kernels, launch(): pl.pallas_call(body, out_shape=[jax.ShapeDtypeStruct(v[0], v[1]) for v in...  638 us

profile of v3, /device:TPU:0, one launch (start us, length us, event | category | flops | bytes accessed | tf_op | source)
XLA Modules:
  0.0 666.1 jit_solution(11047175458245154827)
XLA Ops:
  0.7 0.8 pad_maximum_fusion.9
  2.1 2.4 pad_maximum_fusion.5
  4.7 2.4 copy.29
  7.8 1.0 fusion.3
  9.7 0.8 copy.32.refs_7_
  10.5 1.0 pad_maximum_fusion.7.refs_8_
  11.5 286.6 %shard_map.203 = (bf16[2,128,1280]{2,1,0:T(8,128)(2,1)}, bf16[2,896,1280]{2,1,0:T(8,128)(2,1)}, bf16[2,1536,1280]{2,1,0:T(8,128)(2,1)}, bf16[2,3,896,1280]{3,2,1...) custom-call(s32[2]{0:T(128)} %refs_0_.5, ...), custom_call_target="tpu_custom_call" | custom-call | flops 99999997952 | bytes 100000000 | tf_op jit(solution)/shard_map/pallas_call | solution.py:825
  298.1 1.1 convert_element_type.37.refs_1_
  299.9 53.8 %shard_map.204 = (f32[8,1280]{1,0:T(8,128)}, f32[2,128,1280]{2,1,0:T(8,128)}, bf16[2,4,128,1280]{3,2,1,0:T(8,128)(2,1)}, bf16[3,896,640]{2,1,0:T(8,128)(2,1)}, b...) custom-call(bf16[2,4,128,1280]{3,2,1,0:T(8,128)(2,1)} %get-tuple-element.56.refs_0_, ...), custom_call_target="tpu_custom_call" | custom-call | flops 99999997952 | bytes 100000000 | tf_op jit(solution)/shard_map/pallas_call | solution.py:825
  353.7 0.8 copy.33.refs_11_
  354.6 0.9 fusion.2
  355.5 1.0 pad_maximum_fusion.8.refs_12_
  356.5 99.8 %shard_map.205 = (f32[8,1280]{1,0:T(8,128)}, f32[2,128,1280]{2,1,0:T(8,128)}, bf16[2,4,128,1280]{3,2,1,0:T(8,128)(2,1)}, bf16[896,640]{1,0:T(8,128)(2,1)}, bf16[...) custom-call(s32[2]{0:T(128)} %refs_0_.5, ...), custom_call_target="tpu_custom_call" | custom-call | flops 99999997952 | bytes 100000000 | tf_op jit(solution)/shard_map/pallas_call | solution.py:825
  456.3 58.8 %shard_map.206 = (f32[8,1280]{1,0:T(8,128)}, f32[2,128,1280]{2,1,0:T(8,128)}, bf16[2,4,128,1280]{3,2,1,0:T(8,128)(2,1)}, bf16[3,896,640]{2,1,0:T(8,128)(2,1)}, b...) custom-call(bf16[2,4,128,1280]{3,2,1,0:T(8,128)(2,1)} %get-tuple-ele, ...), custom_call_target="tpu_custom_call" | custom-call | flops 99999997952 | bytes 100000000 | tf_op jit(solution)/shard_map/pallas_call | solution.py:825
  515.2 1.1 convert_element_type.38.refs_3_
  516.3 139.0 %shard_map.207 = (f32[8,1280]{1,0:T(8,128)}, f32[2,128,1280]{2,1,0:T(8,128)}, f32[160,896]{1,0:T(8,128)}, f32[160,896]{1,0:T(8,128)}, f32[160,640]{1,0:T(8,128)}...) custom-call(s32[2]{0:T(128)} %refs_0_.5, bf16[2,4,128,1280]{3,2,1,0:T(8,128)(2,1)} %get-tuple-element.81.refs_1_, ...), custom_call_target="tpu_custom_call" | custom-call | flops 99999997952 | bytes 100000000 | tf_op jit(solution)/shard_map/pallas_call | solution.py:825
  655.4 2.3 pad_maximum_fusion.3
  657.7 1.1 pad_maximum_fusion.4
  658.7 1.1 pad_maximum_fusion
  659.8 1.1 pad_maximum_fusion.1
  661.5 1.1 pad_maximum_fusion.2
  662.5 1.4 fusion.5
  664.0 0.8 copy.37
  664.8 1.1 copy.38
  (52 shorter events, 3.6 us)
Async XLA Ops:
  0.6 3.9 copy-start.6
  0.7 3.9 copy-start.7
  0.7 3.9 copy-start.8
  7.2 1.7 copy-start.19
  9.0 0.7 copy-start
  11.5 286.6 %copy-start.4 = (bf16[2,128,1280]{2,1,0:T(8,128)(2,1)S(1)}, bf16[2,128,1280]{2,1,0:T(8,128)(2,1)}, u32[]{:S(2)}) copy-start(bf16[2,128,1280]{2,1,0:T(8,128)(2,1)} %refs_2_.1) | copy-start | bytes 1966084
  299.8 53.8 %copy-start.1 = (f32[512,4,32]{0,2,1:T(8,128)S(1)}, f32[512,4,32]{0,2,1:T(8,128)}, u32[]{:S(2)}) copy-start(f32[512,4,32]{0,2,1:T(8,128)} %copy-done) | copy-start | bytes 786436
  299.9 54.7 %copy-start.18 = (f32[4,128]{1,0:T(4,128)S(1)}, f32[4,128]{1,0:T(4,128)}, u32[]{:S(2)}) copy-start(f32[4,128]{1,0:T(4,128)} %get-tuple-element.110) | copy-start | bytes 6148
  299.9 54.7 %copy-start.20 = (f32[32]{0:T(128)S(1)}, f32[32]{0:T(128)}, u32[]{:S(2)}) copy-start(f32[32]{0:T(128)} %copy-done.19) | copy-start | bytes 388
  456.3 58.8 %copy-start.5 = (bf16[2,128,1280]{2,1,0:T(8,128)(2,1)S(1)}, bf16[2,128,1280]{2,1,0:T(8,128)(2,1)}, u32[]{:S(2)}) copy-start(bf16[2,128,1280]{2,1,0:T(8,128)(2,1)} %refs_1_.1) | copy-start | bytes 1966084
  516.3 139.0 %copy-start.16 = (f32[160,640]{1,0:T(8,128)S(1)}, f32[160,640]{1,0:T(8,128)}, u32[]{:S(2)}) copy-start(f32[160,640]{1,0:T(8,128)} %get-tuple-element.89) | copy-start | bytes 1228804
  655.3 2.3 copy-start.15
  655.3 2.3 copy-start.17
  655.3 3.4 copy-start.10
  655.3 3.4 copy-start.14
  657.6 2.2 copy-start.11
  657.6 2.2 copy-start.13
  659.8 1.2 copy-start.9
  659.8 1.6 copy-start.12
  660.9 3.1 copy-start.3
  661.5 3.4 copy-start.2

commit v4 on v3

--- a/solution.py
+++ b/solution.py
@@ -710,11 +710,10 @@
 
     a, b, extra = sequence(0), sequence(1), cotangent()
     order = (
-        w0, f0, a, f0, w0, w0, b, f0, b, f1, w0, w0, b, b,
-        f1, a, w1, a, f0, b, b, w1, a, f1, w1, b, a, f0,
-        a, b, w1, b, a, b, a, f1, a, b, b, a, w1, w1,
-        b, b, a, a, b, extra, f1, a, a, b, extra, a, b, a,
-        b, a, b, extra, a, f1, b, a, b, a, a, b, a,
+        w0, f0, f0, w0, w0, a, a, b, b, w1, w0, w0, a, w1, a, f0, f1, w1,
+        a, a, b, a, f0, b, f1, w1, f1, a, b, f0, a, b, a, b, w1, a,
+        f1, w1, b, a, b, b, a, f1, a, b, b, extra, a, b, b, a, extra, b,
+        a, b, a, b, a, extra, f1, b, a, b, a, b, a, b, b,
     )
     run(order)
     net.close(near + [over])
@@ -1188,17 +1187,51 @@
     return start(), one(2), one(0), one(1)
 
 
+def finish_out(net, cfg, mine, other, waits):
+    layers, seqs, block, width, heads, units, share = cfg
+    r = net.r
+    c, t = net.c, net.t
+    one = slice(heads * D, 2 * heads * D)
+    for copy in waits:
+        copy.wait()
+    for at in range(0, 4 * share, LANES):
+        own = slice(at, at + LANES)
+        r.ot[own] = jnp.transpose(mine[one, own].astype(F32) + other[one, own].astype(F32)).astype(BF)
+
+    def piece(i):
+        return r.ot.at[pl.ds(pl.multiple_of(i * share, 32), share)]
+
+    out = [net.send(piece(xor(c, m)), r.oc.at[c], CTX, m) for m in (1, 2, 3)]
+    own = net.local(piece(c), r.oc.at[c])
+    yield
+    for copy in out:
+        copy.wait_recv()
+    own.wait()
+    net.close(out)
+    for m in range(4):
+        r.oq[m] = r.oc[xor(t, m)]
+    parts = [r.oq.at[m] for m in range(4)]
+    lands = [r.oz.at[k] for k in range(4)]
+    sums = net.sum_tp(parts, lands)
+    yield
+    net.sum_tp_on(sums, parts[2], lands[2])
+    yield
+    r.wo_o[...] = net.sum_tp_end(sums, parts[0], lands)
+    yield
+
+
 def finish_attn(net, cfg, mine, other, waits):
     layers, seqs, block, width, heads, units, share = cfg
     r = net.r
     c, t = net.c, net.t
-    wide = 2 * heads * D
+    one, two = slice(0, heads * D), slice(2 * heads * D, 2 * heads * D + 2 * LANES)
     for copy in waits:
         copy.wait()
     for at in range(0, 4 * share, LANES):
         own = slice(at, at + LANES)
-        total = mine[:, own].astype(F32) + other[:, own].astype(F32)
-        r.at[own] = jnp.transpose(total).astype(BF)
+        for units_, to in ((two, slice(0, 2 * LANES)), (one, slice(2 * LANES, 2 * LANES + heads * D))):
+            total = mine[units_, own].astype(F32) + other[units_, own].astype(F32)
+            r.at[own, to] = jnp.transpose(total).astype(BF)
 
     def piece(i):
         return r.at.at[pl.ds(pl.multiple_of(i * share, 32), share)]
@@ -1211,11 +1244,10 @@
     own.wait()
     net.close(out)
     for m in range(4):
-        r.aq[m] = r.ac[xor(t, m), :, :wide]
+        r.aq[m] = r.ac[xor(t, m), :, 2 * LANES :]
     parts = [r.aq.at[m] for m in range(4)]
     lands = [r.az.at[k] for k in range(4)]
-    sums = net.sum_tp(parts, lands)
-    for first, at in ((0, wide), (KEY_VALUE_HEADS * D, wide + LANES)):
+    for first, at in ((0, 0), (KEY_VALUE_HEADS * D, LANES)):
         terms = []
         for h in range(KEY_VALUE_HEADS):
             total = None
@@ -1232,6 +1264,7 @@
     swap = net.make(r.asum.at[1], r.al.at[1], TP, 3)
     back = net.make(r.asum.at[2], r.al.at[2], TP, 1)
     pl.when(outer)(ends.start)
+    sums = net.sum_tp(parts, lands)
     yield
 
     @pl.when(net.inner)
@@ -1251,7 +1284,7 @@
         back.start()
 
     yield
-    r.qo_o[...] = net.sum_tp_end(sums, parts[0], lands)
+    r.wq_o[...] = net.sum_tp_end(sums, parts[0], lands)
 
     @pl.when(net.inner)
     def _():
@@ -1353,12 +1386,12 @@
     a, b = sequence(0, first, second), sequence(1, later, [])
     w0, w1, w2 = weights(0, 2), weights(1, 0), weights(2, 1)
     if tail:
-        fa = finish_attn(net, cfg, r.ak, r.ax, loads)
+        fa, fo = finish_attn(net, cfg, r.ak, r.ax, loads), finish_out(net, cfg, r.ak, r.ax, [])
         x, _, _, f2 = ffn_sums(net, cfg, 2)
         order = (
             x,
-            fa, a, f2, a, b, w0, fa, b, w0, w1, a, w1, f2, fa, w2, fa, w2, b,
-            fa, a, f2, a, w1, b, w0, fa, w2, f2, b,
+            fa, a, fo, f2, fa, a, b, w0, b, a, f2, w1, w1, w2, b, fo, fa, w2,
+            w1, a, w2, fa, f2, fa, fo, b, w0, fo, fa, w0, a, f2, b,
         )
     else:
         order = (
@@ -1446,18 +1479,26 @@
         if at == 0:
             out[2 * heads * D :] = r.ws[heads * LANES : (heads + 2) * LANES]
 
+    side, cross = [], []
+    o_rows, q_rows, kv_rows = (
+        slice(a * D, b * D) for a, b in ((heads, 2 * heads), (0, heads), (2 * heads, 2 * heads + 4))
+    )
+
     def out_weights():
         weights(r.att, r.dy, away, r.wo.at[0], heads * D)
+        if not l:
+            side.append(net.send(r.wo.at[0, o_rows], r.ax.at[o_rows], DP))
         yield
         weights(r.att, r.dy, keep, r.wo.at[1], heads * D)
         yield
-
-    cross = []
 
     def qkv_weights():
         weights(r.dqkv, r.rows, away, r.wo.at[0], 0)
-        yield
-        cross.append(net.send(r.wo.at[0], r.dax_o if l else r.ax, DP))
+        if l:
+            yield
+            cross.append(net.send(r.wo.at[0], r.dax_o, DP))
+        else:
+            cross.extend(net.send(r.wo.at[0, k], r.ax.at[k], DP) for k in (kv_rows, q_rows))
         yield
         weights(r.dqkv, r.rows, keep, r.wo.at[1], 0)
         yield
@@ -1470,10 +1511,11 @@
         )
     else:
         gn, fa = finish_gains(net), finish_attn(net, cfg, r.wo.at[1], r.ax, cross)
+        fo = finish_out(net, cfg, r.wo.at[1], r.ax, side)
         order = (
-            f0, a, b, a, wo, b, a, f1, b, wq, wq, wo, wq, f0, f2, b, b, f1,
-            a, a, fa, f2, f2, gn, f0, fa, f1, fa, f0, gn, fa, fa, f2, gn, f1, gn,
-            fa,
+            f0, a, b, a, b, wo, f0, a, f2, b, wq, a, wq, f1, f0, b, f2, fa,
+            wo, fo, f1, fa, a, b, gn, gn, f2, fo, fa, fa, f1, fa, fo, f2, gn, fa,
+            f0, f1, gn, fo,
         )
     run(order)
     if l:
@@ -1497,15 +1539,14 @@
         grad=(own, F32), base=(own, F32), dy=(rows, BF),
     )
     kvs = (share, 2 * KEY_VALUE_HEADS * D)
-    qos = (share, 2 * heads * D)
+    hs = (share, heads * D)
+    mixed = 2 * LANES + heads * D
     one = (share, units)
-    finish_out = dict(
-        qo_o=(qos, F32, vm), kv_o=(kvs, F32, vm), u_o=(one, F32, vm)
-    )
+    finish_out_ = dict(wq_o=(hs, F32, vm), wo_o=(hs, F32, vm), kv_o=(kvs, F32, vm), u_o=(one, F32, vm))
     finish_scratch = dict(
-        ax=((compact, part), BF), at=((part, compact), BF),
-        ac=((4, share, compact), BF), aq=((4, *qos), BF), az=((4, *qos), BF),
-        av=(kvs, F32), asum=((3, *kvs), BF), al=((3, *kvs), BF),
+        ax=((compact, part), BF), at=((part, mixed), BF), ac=((4, share, mixed), BF), aq=((4, *hs), BF),
+        az=((4, *hs), BF), av=(kvs, F32), asum=((3, *kvs), BF), al=((3, *kvs), BF),
+        ot=((part, heads * D), BF), oc=((4, *hs), BF), oq=((4, *hs), BF), oz=((4, *hs), BF),
     )
     mid_out = dict(
         dn_o=(rows, BF, hbm), dak_o=((compact, part), BF, hbm), dax_o=((compact, part), BF, hbm),
@@ -1518,7 +1559,7 @@
     d, finish_in = None, {}
     for l in reversed(range(layers)):
         tail = d is not None
-        more = (finish_in, finish_out, finish_scratch) if tail else ({}, {}, {})
+        more = (finish_in, finish_out_, finish_scratch) if tail else ({}, {}, {})
         c = launch(
             functools.partial(ffn_back_kernel2, cfg, l, tail),
             number,
@@ -1552,7 +1593,7 @@
             ),
             dict(
                 gs_o=grads, grad_o=(own, F32, hbm),
-                **(mid_out if l else dict(g_o=(one, F32, vm), d_o=(one, F32, vm), **finish_out)),
+                **(mid_out if l else dict(g_o=(one, F32, vm), d_o=(one, F32, vm), **finish_out_)),
             ),
             dict(
                 wa=((size, width), BF), q=((seqs, 4, heads, block, LANES), BF), kv=((seqs, 4, 4, block, 2 * LANES), BF),
@@ -1664,11 +1705,11 @@
         grad, done, fd = backward_pass(cfg, tokens, prefix, cotangent, cos4, sin4, f)
         wide = heads * D
         kd = KEY_VALUE_HEADS * D
-        qo = jnp.stack([d.qo_o for d in done])
         kv = jnp.stack([d.kv_o for d in done])
         sums = lax.dynamic_slice_in_dim(done[0].gs_o, (x * 4 + c) * share, share, 1)
         return (
-            f.out_o, grad, qo[:, :, :wide], kv[:, :, :kd], kv[:, :, kd:], qo[:, :, wide:],
+            f.out_o, grad, jnp.stack([d.wq_o for d in done]), kv[:, :, :kd], kv[:, :, kd:],
+            jnp.stack([d.wo_o for d in done]),
             jnp.stack([d.g_o for d in fd]), jnp.stack([d.u_o for d in done]), jnp.stack([d.d_o for d in fd]),
             sums[:layers], sums[layers : 2 * layers],
         )

time: 676 us -> 668 us (0.988)
  Pallas kernels: 638 us -> 628 us
    pallas_call x5, Pallas kernels: 638 us -> 628 us  [launch(): pl.pallas_call(body, out_shape=[jax.ShapeDtypeStruct(v[0], v[1]) for v in...]
where the time goes in v4:
time: 668 us; the launch traced here: 657 us
  Pallas kernels  628 us (94%)
  other arithmetic  18.9 us (3%)
  local copies, waits for them, and re-layouts  9.58 us (1%)
    pallas_call x5, Pallas kernels, launch(): pl.pallas_call(body, out_shape=[jax.ShapeDtypeStruct(v[0], v[1]) for v in...  628 us

profile of v4, /device:TPU:0, one launch (start us, length us, event | category | flops | bytes accessed | tf_op | source)
XLA Modules:
  0.0 657.5 jit_solution(18398885590798015428)
XLA Ops:
  0.7 0.8 pad_maximum_fusion.10
  2.1 2.4 pad_maximum_fusion.6
  4.7 2.4 copy.29
  7.8 1.0 fusion.2
  9.6 0.8 copy.32.refs_7_
  10.5 1.0 pad_maximum_fusion.8.refs_8_
  11.5 288.8 %shard_map.203 = (bf16[2,128,1280]{2,1,0:T(8,128)(2,1)}, bf16[2,896,1280]{2,1,0:T(8,128)(2,1)}, bf16[2,1536,1280]{2,1,0:T(8,128)(2,1)}, bf16[2,3,896,1280]{3,2,1...) custom-call(s32[2]{0:T(128)} %refs_0_.5, ...), custom_call_target="tpu_custom_call" | custom-call | flops 99999997952 | bytes 100000000 | tf_op jit(solution)/shard_map/pallas_call | solution.py:824
  300.3 1.1 convert_element_type.37.refs_1_
  302.1 50.7 %shard_map.204 = (f32[8,1280]{1,0:T(8,128)}, f32[2,128,1280]{2,1,0:T(8,128)}, bf16[2,4,128,1280]{3,2,1,0:T(8,128)(2,1)}, bf16[3,896,640]{2,1,0:T(8,128)(2,1)}, b...) custom-call(bf16[2,4,128,1280]{3,2,1,0:T(8,128)(2,1)} %get-tuple-element.58.refs_0_, ...), custom_call_target="tpu_custom_call" | custom-call | flops 99999997952 | bytes 100000000 | tf_op jit(solution)/shard_map/pallas_call | solution.py:824
  352.9 0.8 copy.33.refs_11_
  353.7 0.9 fusion.1
  354.6 1.0 pad_maximum_fusion.9.refs_12_
  355.6 97.0 %shard_map.205 = (f32[8,1280]{1,0:T(8,128)}, f32[2,128,1280]{2,1,0:T(8,128)}, bf16[2,4,128,1280]{3,2,1,0:T(8,128)(2,1)}, bf16[896,640]{1,0:T(8,128)(2,1)}, bf16[...) custom-call(s32[2]{0:T(128)} %refs_0_.5, ...), custom_call_target="tpu_custom_call" | custom-call | flops 99999997952 | bytes 100000000 | tf_op jit(solution)/shard_map/pallas_call | solution.py:824
  452.6 60.6 %shard_map.206 = (f32[8,1280]{1,0:T(8,128)}, f32[2,128,1280]{2,1,0:T(8,128)}, bf16[2,4,128,1280]{3,2,1,0:T(8,128)(2,1)}, bf16[3,896,640]{2,1,0:T(8,128)(2,1)}, b...) custom-call(bf16[2,4,128,1280]{3,2,1,0:T(8,128)(2,1)} %get-tuple-ele, ...), custom_call_target="tpu_custom_call" | custom-call | flops 99999997952 | bytes 100000000 | tf_op jit(solution)/shard_map/pallas_call | solution.py:824
  513.2 1.1 convert_element_type.38.refs_3_
  514.4 130.9 %shard_map.207 = (f32[8,1280]{1,0:T(8,128)}, f32[2,128,1280]{2,1,0:T(8,128)}, f32[160,896]{1,0:T(8,128)}, f32[160,896]{1,0:T(8,128)}, f32[160,320]{1,0:T(8,128)}...) custom-call(s32[2]{0:T(128)} %refs_0_.5, bf16[2,4,128,1280]{3,2,1,0:T(8,128)(2,1)} %get-tuple-element.83.refs_1_, ...), custom_call_target="tpu_custom_call" | custom-call | flops 99999997952 | bytes 100000000 | tf_op jit(solution)/shard_map/pallas_call | solution.py:824
  645.3 1.9 pad_maximum_fusion.4
  647.2 2.1 pad_maximum_fusion.3
  650.1 1.1 pad_maximum_fusion
  651.2 1.1 pad_maximum_fusion.1
  652.9 1.1 pad_maximum_fusion.2
  653.9 1.4 fusion.4
  655.4 0.8 copy.37
  656.2 1.1 copy.38
  (55 shorter events, 4.4 us)
Async XLA Ops:
  0.6 3.9 copy-start.6
  0.7 3.9 copy-start.7
  0.7 3.9 copy-start.8
  7.1 1.7 copy-start.20
  8.9 0.7 copy-start
  11.5 288.8 %copy-start.4 = (bf16[2,128,1280]{2,1,0:T(8,128)(2,1)S(1)}, bf16[2,128,1280]{2,1,0:T(8,128)(2,1)}, u32[]{:S(2)}) copy-start(bf16[2,128,1280]{2,1,0:T(8,128)(2,1)} %refs_2_.1) | copy-start | bytes 1966084
  302.1 50.7 %copy-start.1 = (f32[512,4,32]{0,2,1:T(8,128)S(1)}, f32[512,4,32]{0,2,1:T(8,128)}, u32[]{:S(2)}) copy-start(f32[512,4,32]{0,2,1:T(8,128)} %copy-done) | copy-start | bytes 786436
  302.1 51.6 %copy-start.19 = (f32[4,128]{1,0:T(4,128)S(1)}, f32[4,128]{1,0:T(4,128)}, u32[]{:S(2)}) copy-start(f32[4,128]{1,0:T(4,128)} %get-tuple-element.112) | copy-start | bytes 6148
  302.1 51.6 %copy-start.21 = (f32[32]{0:T(128)S(1)}, f32[32]{0:T(128)}, u32[]{:S(2)}) copy-start(f32[32]{0:T(128)} %copy-done.20) | copy-start | bytes 388
  452.6 60.6 %copy-start.5 = (bf16[2,128,1280]{2,1,0:T(8,128)(2,1)S(1)}, bf16[2,128,1280]{2,1,0:T(8,128)(2,1)}, u32[]{:S(2)}) copy-start(bf16[2,128,1280]{2,1,0:T(8,128)(2,1)} %refs_1_.1) | copy-start | bytes 1966084
  514.4 130.9 %copy-start.17 = (f32[160,320]{1,0:T(8,128)S(1)}, f32[160,320]{1,0:T(8,128)}, u32[]{:S(2)}) copy-start(f32[160,320]{1,0:T(8,128)} %get-tuple-element.91) | copy-start | bytes 614404
  514.4 132.8 %copy-start.15 = (f32[160,640]{1,0:T(8,128)S(1)}, f32[160,640]{1,0:T(8,128)}, u32[]{:S(2)}) copy-start(f32[160,640]{1,0:T(8,128)} %get-tuple-element.93) | copy-start | bytes 1228804
  645.2 4.1 copy-start.16
  645.2 4.1 copy-start.18
  645.3 4.9 copy-start.10
  645.3 4.9 copy-start.14
  649.3 1.9 copy-start.11
  649.3 1.9 copy-start.13
  651.2 1.2 copy-start.9
  651.2 1.6 copy-start.12
  652.3 3.1 copy-start.3
  652.9 3.4 copy-start.2

commit v5 on v4

--- a/solution.py
+++ b/solution.py
@@ -614,7 +614,7 @@
 
     def sequence(s):
         rows, frows, q, att, pt, gu = r.rows, r.frows, r.q, r.att, r.pt, r.gu
-        carry = []
+        carry = [net.local(r.stream.at[s], r.stream_o.at[0, s])]
         for l in range(layers):
             kv = r.kv
             gather = gather_start(r.stream[s], r.gain[l : l + 1], s, rows)
@@ -669,7 +669,7 @@
                 copy.wait()
             r.stream[s] = r.middle[s] + reduce_end(reduce, s)
             if l + 1 < layers:
-                carry = [net.local(r.stream.at[s], r.stream_o.at[l, s])]
+                carry = [net.local(r.stream.at[s], r.stream_o.at[l + 1, s])]
             else:
                 r.far[s] = r.stream[s].astype(BF)
                 kept.append(net.local(r.far.at[s], r.out_o.at[s]))
@@ -868,7 +868,7 @@
             middle_o=((layers, *own), F32, hbm),
             frows_o=((layers, *rows), BF, hbm),
             gu_o=((layers, seqs, 2, keys, units), BF, hbm),
-            stream_o=((layers - 1, *own), F32, hbm),
+            stream_o=((layers, *own), F32, hbm),
             gain_o=((2 * layers, width), F32, hbm),
             dy_o=(rows, BF, hbm),
             qz=((layers, *raw), BF, hbm),
@@ -1332,9 +1332,10 @@
     second = [net.local(r.wf_i.at[l, i], r.wf.at[i]) for i in (0, 1)]
     later = [net.local(r.dy_i.at[s], r.dy.at[s]) for s in range(1, seqs)]
     later += [net.local(r.gu_i.at[l, s], r.gu.at[s]) for s in range(1, seqs)]
-    state = [net.local(r.grad_i, r.grad), net.local(r.base_i.at[l], r.base)]
+    top = l + 1 == layers
+    state = [net.local(r.base_i.at[l], r.base)] + ([] if top else [net.local(r.grad_i, r.grad)])
     state += [net.local(r.frows_i.at[l, s], r.frows.at[s]) for s in range(seqs)]
-    r.gs_o[...] = r.gs_i[...]
+    r.gs_o[...] = jnp.zeros_like(r.gs_o) if top else r.gs_i[...]
     row = layers + l
     gain = r.gain[row : row + 1]
     saved, busy = [], {}
@@ -1343,6 +1344,8 @@
         rows, hgu, pt = r.dy.at[s], r.hgu.at[s], r.pt.at[s]
         for copy in waits:
             copy.wait()
+        if top:
+            r.grad[s] = rows[0].astype(F32)
         ffn_back_body(rows, r.wf, r.gu.at[s], hgu, pt, more)
         red = net.reduce_start(s)
         yield
@@ -1420,7 +1423,7 @@
             loads[s].append(net.local(src.at[l, s], dst.at[s]))
     x, f0, f1, f2 = ffn_sums(net, cfg, 1 if l else 0)
     run((x,))
-    state = [net.local(r.grad_i, r.grad), net.local(r.base_i.at[l - 1] if l else r.base_i, r.base)]
+    state = [net.local(r.grad_i, r.grad), net.local(r.base_i.at[l], r.base)]
     state += [net.local(r.rows_i.at[l, s], r.rows.at[s]) for s in range(seqs)]
     r.gs_o[...] = r.gs_i[...]
     gain = r.gain[l : l + 1]
@@ -1552,8 +1555,7 @@
         dn_o=(rows, BF, hbm), dak_o=((compact, part), BF, hbm), dax_o=((compact, part), BF, hbm),
         fs_o=((units, part), BF, hbm), g_o=(one, F32, vm), d_o=(one, F32, vm),
     )
-    grad, dy = cotangent.astype(F32), f.dy_o
-    sums = jnp.zeros((8, width), F32)
+    grad, sums, dy = None, None, f.dy_o
     done, units_of = [None] * layers, [None] * layers
     number = 1
     d, finish_in = None, {}
@@ -1564,8 +1566,8 @@
             functools.partial(ffn_back_kernel2, cfg, l, tail),
             number,
             dict(
-                dy_i=(dy, hbm), grad_i=(grad, hbm), base_i=(f.middle_o, hbm), gain=(f.gain_o, vm), wf_i=(f.wf_o, hbm),
-                frows_i=(f.frows_o, hbm), gu_i=(f.gu_o, hbm), gs_i=(sums, vm), **more[0],
+                dy_i=(dy, hbm), base_i=(f.middle_o, hbm), gain=(f.gain_o, vm), wf_i=(f.wf_o, hbm),
+                frows_i=(f.frows_o, hbm), gu_i=(f.gu_o, hbm), **more[0], **({} if d is None else dict(grad_i=(grad, hbm), gs_i=(sums, vm))),
             ),
             dict(
                 gs_o=grads, grad_o=(own, F32, hbm), dn_o=(rows, BF, hbm), dwk_o=((3, units, part), BF, hbm),
@@ -1581,12 +1583,11 @@
         if tail:
             done[l + 1] = c
             units_of[l + 1] = d
-        base = f.stream_o if l else tokens.astype(F32)
         d = launch(
             functools.partial(attn_back_kernel2, cfg, l),
             number + 1,
             dict(
-                prefix=(prefix, pltpu.SMEM), dy_i=(c.dn_o, hbm), grad_i=(c.grad_o, hbm), base_i=(base, hbm),
+                prefix=(prefix, pltpu.SMEM), dy_i=(c.dn_o, hbm), grad_i=(c.grad_o, hbm), base_i=(f.stream_o, hbm),
                 gain=(f.gain_o, vm), wa_i=(f.wa_o, hbm), rows_i=(f.rows_o, hbm), q_i=(f.q_o, hbm), kv_i=(f.kv_o, hbm),
                 att_i=(f.att_o, hbm), lse_i=(f.lse_o, hbm), cos=(cos4, vm), sin=(sin4, vm), gs_i=(c.gs_o, vm),
                 dwk=(c.dwk_o, hbm), dws=(c.dws_o, hbm), dwx=(c.dwx_o, hbm),
@@ -1640,12 +1641,13 @@
     long = 4 * keys
 
     half = D // 2
-    freq = jnp.exp(-math.log(10000.0) * jnp.arange(half).astype(F32) / half)
+    lane = jnp.arange(LANES)
+    freq = jnp.exp(-math.log(10000.0) * (lane % half).astype(F32) / half)
     at = ((c ^ jnp.arange(4)) * keys + t * block)[:, None] + jnp.arange(block)[None, :]
     angle = at.astype(F32).reshape(keys, 1) * freq[None, :]
-    cos = jnp.tile(jnp.cos(angle), (1, 4))
-    sin = jnp.sin(angle)
-    sin = jnp.concatenate([-sin, sin, -sin, sin], axis=1)
+    cos = jnp.cos(angle)
+    sin = jnp.where(lane % D < half, -1.0, 1.0)[None, :] * jnp.sin(angle)
+    cos, sin = lax.optimization_barrier((cos, sin))
     cos4, sin4 = cos.reshape(4, block, LANES), sin.reshape(4, block, LANES)
     scalars = [
         jnp.stack([c, t, prefix[s]]).astype(jnp.int32) for s in range(seqs)

time: 668 us -> 660 us (0.988)
  no operation moved by 1% of the time
where the time goes in v5:
time: 660 us; the launch traced here: 649 us
  Pallas kernels  628 us (95%)
  other arithmetic  13.8 us (2%)
  local copies, waits for them, and re-layouts  6.83 us (1%)
    pallas_call x5, Pallas kernels, launch(): pl.pallas_call(body, out_shape=[jax.ShapeDtypeStruct(v[0], v[1]) for v in...  628 us

profile of v5, /device:TPU:0, one launch (start us, length us, event | category | flops | bytes accessed | tf_op | source)
XLA Modules:
  0.0 649.4 jit_solution(4819775443327256866)
XLA Ops:
  0.7 0.1 convert_bitcast_fusion
  0.8 0.8 pad_maximum_fusion.8
  1.6 0.6 pad_convert_fusion.refs_3_
  2.2 1.8 fusion.1
  4.0 2.4 pad_maximum_fusion.6
  6.5 0.1 maximum_bitcast_fusion
  6.6 2.4 copy.23
  9.0 288.8 %shard_map.203 = (bf16[2,128,1280]{2,1,0:T(8,128)(2,1)}, bf16[2,896,1280]{2,1,0:T(8,128)(2,1)}, bf16[2,1536,1280]{2,1,0:T(8,128)(2,1)}, bf16[2,3,896,1280]{3,2,1...) custom-call(s32[2]{0:T(128)} %refs_0_.5, ...), custom_call_target="tpu_custom_call" | custom-call | flops 99999997952 | bytes 100000000 | tf_op jit(solution)/shard_map/pallas_call | solution.py:824
  297.8 50.6 %shard_map.204 = (f32[8,1280]{1,0:T(8,128)}, f32[2,128,1280]{2,1,0:T(8,128)}, bf16[2,4,128,1280]{3,2,1,0:T(8,128)(2,1)}, bf16[3,896,640]{2,1,0:T(8,128)(2,1)}, b...) custom-call(bf16[2,4,128,1280]{3,2,1,0:T(8,128)(2,1)} %get-tuple-element.62.refs_0_, ...), custom_call_target="tpu_custom_call" | custom-call | flops 99999997952 | bytes 100000000 | tf_op jit(solution)/shard_map/pallas_call | solution.py:824
  348.5 96.8 %shard_map.205 = (f32[8,1280]{1,0:T(8,128)}, f32[2,128,1280]{2,1,0:T(8,128)}, bf16[2,4,128,1280]{3,2,1,0:T(8,128)(2,1)}, bf16[896,640]{1,0:T(8,128)(2,1)}, bf16[...) custom-call(s32[2]{0:T(128)} %refs_0_.5, ...), custom_call_target="tpu_custom_call" | custom-call | flops 99999997952 | bytes 100000000 | tf_op jit(solution)/shard_map/pallas_call | solution.py:824
  445.3 60.7 %shard_map.206 = (f32[8,1280]{1,0:T(8,128)}, f32[2,128,1280]{2,1,0:T(8,128)}, bf16[2,4,128,1280]{3,2,1,0:T(8,128)(2,1)}, bf16[3,896,640]{2,1,0:T(8,128)(2,1)}, b...) custom-call(bf16[2,4,128,1280]{3,2,1,0:T(8,128)(2,1)} %get-tuple-ele, ...), custom_call_target="tpu_custom_call" | custom-call | flops 99999997952 | bytes 100000000 | tf_op jit(solution)/shard_map/pallas_call | solution.py:824
  506.0 130.9 %shard_map.207 = (f32[8,1280]{1,0:T(8,128)}, f32[2,128,1280]{2,1,0:T(8,128)}, f32[160,896]{1,0:T(8,128)}, f32[160,896]{1,0:T(8,128)}, f32[160,320]{1,0:T(8,128)}...) custom-call(s32[2]{0:T(128)} %refs_0_.5, bf16[2,4,128,1280]{3,2,1,0:T(8,128)(2,1)} %get-tuple-element.87.refs_1_, ...), custom_call_target="tpu_custom_call" | custom-call | flops 99999997952 | bytes 100000000 | tf_op jit(solution)/shard_map/pallas_call | solution.py:824
  636.9 1.8 pad_maximum_fusion.4
  638.8 1.5 fusion.5
  640.2 1.8 pad_maximum_fusion.5
  642.0 1.1 pad_maximum_fusion
  643.1 1.1 pad_maximum_fusion.1
  644.2 0.2 copy-done.5
  644.3 0.4 copy-done.8
  644.7 1.1 pad_maximum_fusion.2
  645.8 0.4 copy-done.12
  646.2 1.1 pad_maximum_fusion.3
  647.3 0.8 copy.26
  648.1 1.1 copy.27
  (30 shorter events, 0.1 us)
Async XLA Ops:
  0.6 5.8 copy-start.2
  0.7 5.8 copy-start.3
  0.7 5.8 copy-start.4
  506.0 130.9 %copy-start.14 = (f32[160,320]{1,0:T(8,128)S(1)}, f32[160,320]{1,0:T(8,128)}, u32[]{:S(2)}) copy-start(f32[160,320]{1,0:T(8,128)} %get-tuple-element.95) | copy-start | bytes 614404
  506.0 134.3 %copy-start.13 = (f32[160,320]{1,0:T(8,128)S(1)}, f32[160,320]{1,0:T(8,128)}, u32[]{:S(2)}) copy-start(f32[160,320]{1,0:T(8,128)} %get-tuple-element.99) | copy-start | bytes 614404
  636.9 5.1 copy-start.6
  636.9 5.1 copy-start.10
  638.8 4.3 copy-start.7
  638.8 4.3 copy-start.9
  643.1 1.2 copy-start.5
  643.1 1.6 copy-start.8
  644.7 1.1 copy-start.11
  644.7 1.5 copy-start.12
  644.7 2.6 copy-start.1
  646.2 1.9 copy-start
